TPU v7x, 32 devices: a whole 2x2x4 slice. The times are simulated.
32 devices in a mesh: groups: 2 (over y), gx: 4 (over z), gy: 2 (over x), gz: 2 (over core).
Axes of the slice: x: 2, y: 2, z: 4, core: 2. Of those that a mesh axis runs over, the one named last changes fastest.
Arguments:
- members: bfloat16 [64, 16, 32, 256], P('groups', 'gz', 'gx', 'gy'), parts along dimension 0, may hold values from -6 to 6
- obs_value: float32 [4, 4, 2, 256], P(('groups', 'gz'), 'gx', 'gy'), parts along dimension 0, may hold values from -6 to 6
- obs_rinv: float32 [4, 4, 2, 256], P(('groups', 'gz'), 'gx', 'gy'), parts along dimension 0, may hold values from 0.25 to 4
- obs_count: int32 [4, 4, 2], P(('groups', 'gz'), 'gx', 'gy'), parts along dimension 0, may hold values from 32 to 256, as said below
- stencil_cell: int32 [4, 4, 2, 8, 256], P(('groups', 'gz'), 'gx', 'gy'), parts along dimension 0, may hold values from 0 to 8191, as said below
- stencil_weight: float32 [4, 4, 2, 8, 256], P(('groups', 'gz'), 'gx', 'gy'), parts along dimension 0, may hold values from 0 to 1, as said below
- patch_list: int32 [16, 256, 64], P(('groups', 'gx'), 'gy'), parts along dimension 0, may hold values from 0 to 4607
- patch_taper: float32 [16, 256, 64], P(('groups', 'gx'), 'gy'), parts along dimension 0, may hold values from 0.05 to 1
Outputs:
- analysis: bfloat16 [64, 16, 32, 256], P('groups', 'gz', 'gx', 'gy'), parts along dimension 0
There are 2 independent parts, one for each index of `groups`. A program takes and returns all parts, laid end to end along the dimension named above; each array names one. Nothing has to cross between parts.
Inputs may be any that keep to these rules, and one draw needn't show every extreme that they name: Each buffer's first obs_count slots are live; in every draw some buffer is full. `stencil_cell`: the eight corners (l + a, x + b, y + c), a, b, c in 0, 1, of one grid box of the owner's block, as local numbers (l*8 + x)*128 + y. `stencil_weight`: trilinear weights: nonnegative, summing to one over a sample's eight cells. `patch_list`: ids ((h*3 + a)*3 + b)*256 + o into the buffers of both level halves of the 3 x 3 tiles around the patch's own.
All inputs are finite; a program needn't handle non-finite values.
Results may differ from a plain program's by a relative error of at most 0.001.
Values sent between devices are 32-bit elements; how exact they have to be, the bound alone decides.
No kernel may reach another device: no remote copies, remote signals or barrier semaphores. Data moves between devices by JAX's collectives and lax.ppermute only.
A program may use at most 64 MiB of HBM per device.

v0:
```python
import math

import jax
import jax.numpy as jnp
from jax import lax
from jax.sharding import PartitionSpec as P

PX = 4
NSIT = 4


def extended(x, sides, width):
    for axis, dim in sides:
        size, length = (lax.axis_size(axis), x.shape[dim])
        up = [(i, (i + 1) % size) for i in range(size)]
        down = [(j, i) for i, j in up]
        last = lax.slice_in_dim(x, length - width, length, axis=dim)
        initial = lax.slice_in_dim(x, 0, width, axis=dim)
        before = lax.ppermute(last, axis, up)
        after = lax.ppermute(initial, axis, down)
        x = jnp.concatenate([before, x, after], axis=dim)
    return x


def batched_product(first_mat, second_mat):
    return jnp.einsum("ijp,jkp->ikp", first_mat, second_mat, precision=lax.Precision.HIGHEST)


def transforms(nearby, list_ids, tapers):
    ensemble = nearby.shape[0] - 2
    picked = jnp.take(nearby, list_ids.reshape(-1), axis=1).reshape(
        ensemble + 2, list_ids.shape[0], list_ids.shape[1]
    )
    observed_perturbation = picked[:ensemble]
    innovation = picked[ensemble]
    weight = picked[ensemble + 1] * tapers
    scaled_product = observed_perturbation * weight[None]
    gram_matrix = jnp.einsum(
        "sfe,bfe->sbf", scaled_product, observed_perturbation, precision=lax.Precision.HIGHEST
    )
    rhs_vec = jnp.einsum("ipm,pm->ip", scaled_product, innovation, precision=lax.Precision.HIGHEST)
    identity = jnp.eye(ensemble, dtype=jnp.float32)[:, :, None]
    system = gram_matrix + (ensemble - 1.0) * identity
    half_trace = 0.5 * jnp.einsum("iip->p", system)
    iterate = system / half_trace[None, None]
    root = jnp.broadcast_to(identity, system.shape)
    for sweep in range(NSIT):
        middle = 1.5 * identity - 0.5 * batched_product(root, iterate)
        iterate = batched_product(iterate, middle)
        root = batched_product(middle, root)
    inner = jnp.einsum("ijp,jp->ip", root, rhs_vec, precision=lax.Precision.HIGHEST)
    mean_weight = (
        jnp.einsum("ijp,jp->ip", root, inner, precision=lax.Precision.HIGHEST) / half_trace[None]
    )
    return (
        mean_weight[:, None, :]
        + math.sqrt(ensemble - 1.0) * root / jnp.sqrt(half_trace)[None, None]
    )


def row_transforms(nearby, list_ids, tapers):

    def one_row(pair):
        return transforms(nearby, pair[0], pair[1])

    stacked = lax.map(one_row, (list_ids, tapers))
    return jnp.transpose(stacked, (1, 2, 0, 3))


def per_device(
    members, obs_value, obs_rinv, obs_count, stencil_cell, stencil_weight, patch_list, patch_taper
):
    ensemble, levels, width_x, width_y = members.shape
    slots = obs_value.shape[-1]
    field = members.astype(jnp.float32)
    mean = jnp.sum(field, axis=0) / ensemble
    pert = field - mean[None]
    flat_pert = pert.reshape(ensemble, -1)
    flat_mean = mean.reshape(-1)
    cells = stencil_cell.reshape(-1, slots)
    weights = stencil_weight.reshape(-1, slots)
    observed_perturbation = jnp.sum(jnp.take(flat_pert, cells, axis=1) * weights[None], axis=1)
    innovation = obs_value.reshape(slots) - jnp.sum(
        jnp.take(flat_mean, cells, axis=0) * weights, axis=0
    )
    live = (jnp.arange(slots, dtype=jnp.int32) < obs_count.reshape(())).astype(jnp.float32)
    packet = jnp.concatenate(
        [observed_perturbation, innovation[None], (obs_rinv.reshape(slots) * live)[None]], axis=0
    )
    packet = packet.reshape(ensemble + 2, 1, 1, 1, slots)
    joined = lax.all_gather(packet, "gz", axis=1, tiled=True)
    nearby = extended(joined, (("gx", 2), ("gy", 3)), 1)
    nearby = nearby.reshape(ensemble + 2, -1)
    patch_rows = patch_list.shape[0]
    transform = row_transforms(nearby, patch_list, patch_taper)
    pert_cols = pert.reshape(ensemble, levels, patch_rows, PX, width_y)
    mean_cols = mean.reshape(levels, patch_rows, PX, width_y)
    outputs = []
    padded = extended(transform, (("gx", 2),), 1)
    centre = padded[:, :, 1:-1]
    lower = padded[:, :, :-2]
    upper = padded[:, :, 2:]
    for column in range(PX):
        index_shift = (column + 0.5) / PX - 0.5
        beside = lower if index_shift < 0 else upper
        blend = (1.0 - abs(index_shift)) * centre + abs(index_shift) * beside
        update = jnp.einsum(
            "jlay,jkay->klay", pert_cols[:, :, :, column], blend, precision=lax.Precision.HIGHEST
        )
        outputs.append((mean_cols[None, :, :, column] + update).astype(jnp.bfloat16))
    return jnp.stack(outputs, axis=3).reshape(ensemble, levels, width_x, width_y)


def solution(mesh):
    return jax.shard_map(
        per_device,
        mesh=mesh,
        in_specs=(
            P("groups", "gz", "gx", "gy"),
            P(("groups", "gz"), "gx", "gy", None),
            P(("groups", "gz"), "gx", "gy", None),
            P(("groups", "gz"), "gx", "gy"),
            P(("groups", "gz"), "gx", "gy", None, None),
            P(("groups", "gz"), "gx", "gy", None, None),
            P(("groups", "gx"), "gy", None),
            P(("groups", "gx"), "gy", None),
        ),
        out_specs=P("groups", "gz", "gx", "gy"),
        check_vma=False,
    )
```

profile of v0, /device:TPU:0, one launch (start us, length us, event | category | flops | bytes accessed | tf_op | source)
XLA Modules:
  0.0 333.1 jit_solution(13836307138665868735)
XLA Ops:
  2.4 2.7 copy.189
  5.1 7.6 %gather_fusion.1 = f32[2048,32]{1,0:T(8,128)S(1)} fusion(f32[32,8192]{0,1:T(8,128)} %bitcast.281, s32[2048]{0:T(1024)S(1)} %broadcast_clamp_fusion.1), kind=kCustom, calls=%fused_computation.1 | custom fusion | bytes 532480 | tf_op jit(solution)/shard_map/jit(_take)/gather | solution.py:82
  12.8 11.8 %gather_fusion.2 = f32[2048]{0:T(1024)S(1)} fusion(f32[8192]{0:T(1024)S(1)} %bitcast.279, s32[2048]{0:T(1024)S(1)} %broadcast_clamp_fusion.1), kind=kCustom, calls=%fused_computation.2 | custom fusion | bytes 24576 | tf_op jit(solution)/shard_map/jit(_take)/gather | solution.py:84
  28.1 3.0 collective-permute-start
  33.2 2.6 collective-permute-done
  38.7 6.1 %collective-permute-done.2 = f32[34,2,3,1,256]{4,1,3,2,0:T(2,128)S(1)} collective-permute-done((f32[34,2,3,1,256]{4,1,3,2,0:T(2,128)S(1)}, f32[34,2,3,1,256]{4,1,3,2,0:T(2,128)S(1)}, u32[]{:S(2)}, u32[]{:S(2)}) %collective-permute-start.2) | collective-permute-done | bytes 208928 | tf_op jit(solution)/shard_map/ppermute | solution.py:19
  44.8 2.9 collective-permute-done.3
  49.1 205.7 %while.10 = (s32[]{:T(128)}, f32[2,32,32,128]{3,2,0,1:T(8,128)}, s32[2,128,64]{1,2,0:T(8,128)S(1)}, f32[34,4608]{0,1:T(8,128)S(1)}, f32[2,128,64]{1,2,0:T(8,128)S(1)}, /*index=5*/s32[]{:T(128)}) while((s32[]{:T(128)}, f32[2,32,32,128]{3,2,0,1:T(8,128)}, s32[2,128,64]{1,2,0:T(8,128)S(1)}, f32[34,4608]{0,1:T(8,128)S(1)}, ...), condition=%wide.region_5.6_spmd, body=%wide.region_3.5_spmd.sunk | while | flops 664389632 | bytes 49203900 | solution.py:66
  49.6 27.8 %gather_fusion = f32[8192,34]{1,0:T(8,128)} fusion(f32[34,4608]{0,1:T(8,128)S(1)} %get-tuple-element.163, s32[8192]{0:T(1024)S(1)} %broadcast_clamp_fusion.3), kind=kCustom, calls=%fused_computation.clone.1 | custom fusion | bytes 2260992 | tf_op jit(solution)/shard_map/while/body/eval_jaxpr/jit(_take)/gather | solution.py:31
  77.4 6.2 %select_bitcast_fusion.2 = f32[34,8192]{0,1:T(8,128)S(1)} fusion(f32[8192,34]{1,0:T(8,128)} %gather_fusion, pred[8192]{0:T(1024)(128)(4,1)S(1)} %compare_and_fusion.4), kind=kLoop, calls=%fused_computation.5.clone.1 | loop fusion | flops 278528 | bytes 2236416 | tf_op jit(solution)/shard_map/while/body/eval_jaxpr/jit(_take)/select_n | solution.py:31
  83.7 4.4 %slice_reduce_fusion.3 = (f32[8192]{0:T(1024)S(1)}, f32[8192]{0:T(1024)S(1)}) fusion(f32[34,8192]{0,1:T(8,128)S(1)} %select_bitcast_fusion.2), kind=kLoop, calls=%fused_computation.4.clone.1 | loop fusion | bytes 131072 | tf_op jit(solution)/shard_map/while/body/eval_jaxpr/slice | solution.py:35
  88.3 4.4 %copy.270 = f32[32,128,64]{2,1,0:T(8,128)} copy(f32[32,128,64]{0,2,1:T(8,128)} %bitcast.277) | data formatting | bytes 2097152 | tf_op jit(solution)/shard_map/while/body/eval_jaxpr/slice | solution.py:34
  95.5 8.2 %select_reduce_fusion.2 = (f32[128]{0:T(128)S(1)}, f32[128,32,32]{2,1,0:T(8,128)S(1)}) fusion(f32[32,32]{0,1:T(8,128)S(1)} %get-tuple-element.140, pred[32,32]{0,1:T(8,128)(4,1)S(1)} %iota_compare_fusion.3, f32[32,128,64]{0,2,1:T(8,128)S(1)} %bitcast.278, f32[32,128,64]{2,1,0:T(8,128)S(1)} %broadcast_multiply_fusion.4), kind=kOutput, calls=%fused_computation.39.clone.1 | convolution fusion | flops 101056384 | bytes 2627072 | tf_op jit(solution)/shard_map/while/body/eval_jaxpr/sfe,bfe->sbf/dot_general | solution.py:38
  105.8 3.0 fusion.164
  110.8 2.4 fusion.165
  113.2 2.5 fusion.167
  115.7 2.4 fusion.166
  118.1 2.6 fusion.168
  120.6 2.5 fusion.170
  125.5 2.4 fusion.171
  127.9 3.6 %fusion.172 = f32[128,32,32]{2,1,0:T(8,128)} fusion(f32[128,32,32]{2,1,0:T(8,128)S(1)} %fusion.169, f32[128,32,32]{2,1,0:T(8,128)S(1)} %fusion.171, f32[32,32]{0,1:T(8,128)S(1)} %get-tuple-element.145), kind=kOutput, calls=%fused_computation.15.clone.1 | convolution fusion | flops 50593792 | bytes 1576960 | tf_op jit(solution)/shard_map/while/body/eval_jaxpr/ijp,jkp->ikp/dot_general | solution.py:26
  131.6 6.2 %fusion.173 = f32[32,128,1]{0,2,1:T(1,128)S(1)} fusion(f32[128,64,1]{1,2,0:T(1,128)S(1)} %bitcast.283, f32[32,128,64]{2,1,0:T(8,128)} %copy-done.3), kind=kOutput, calls=%fused_computation.47.clone.1 | convolution fusion | flops 3145728 | bytes 1097728 | tf_op jit(solution)/shard_map/while/body/eval_jaxpr/ipm,pm->ip/dot_general | solution.py:41
  143.2 2.8 copy.272
  147.6 27.8 %gather_fusion = f32[8192,34]{1,0:T(8,128)} fusion(f32[34,4608]{0,1:T(8,128)S(1)} %get-tuple-element.163, s32[8192]{0:T(1024)S(1)} %broadcast_clamp_fusion.3), kind=kCustom, calls=%fused_computation.clone.1 | custom fusion | bytes 2260992 | tf_op jit(solution)/shard_map/while/body/eval_jaxpr/jit(_take)/gather | solution.py:31
  175.5 6.2 %select_bitcast_fusion.2 = f32[34,8192]{0,1:T(8,128)S(1)} fusion(f32[8192,34]{1,0:T(8,128)} %gather_fusion, pred[8192]{0:T(1024)(128)(4,1)S(1)} %compare_and_fusion.4), kind=kLoop, calls=%fused_computation.5.clone.1 | loop fusion | flops 278528 | bytes 2236416 | tf_op jit(solution)/shard_map/while/body/eval_jaxpr/jit(_take)/select_n | solution.py:31
  181.7 4.4 %slice_reduce_fusion.3 = (f32[8192]{0:T(1024)S(1)}, f32[8192]{0:T(1024)S(1)}) fusion(f32[34,8192]{0,1:T(8,128)S(1)} %select_bitcast_fusion.2), kind=kLoop, calls=%fused_computation.4.clone.1 | loop fusion | bytes 131072 | tf_op jit(solution)/shard_map/while/body/eval_jaxpr/slice | solution.py:35
  186.3 4.3 %copy.270 = f32[32,128,64]{2,1,0:T(8,128)} copy(f32[32,128,64]{0,2,1:T(8,128)} %bitcast.277) | data formatting | bytes 2097152 | tf_op jit(solution)/shard_map/while/body/eval_jaxpr/slice | solution.py:34
  193.4 8.2 %select_reduce_fusion.2 = (f32[128]{0:T(128)S(1)}, f32[128,32,32]{2,1,0:T(8,128)S(1)}) fusion(f32[32,32]{0,1:T(8,128)S(1)} %get-tuple-element.140, pred[32,32]{0,1:T(8,128)(4,1)S(1)} %iota_compare_fusion.3, f32[32,128,64]{0,2,1:T(8,128)S(1)} %bitcast.278, f32[32,128,64]{2,1,0:T(8,128)S(1)} %broadcast_multiply_fusion.4), kind=kOutput, calls=%fused_computation.39.clone.1 | convolution fusion | flops 101056384 | bytes 2627072 | tf_op jit(solution)/shard_map/while/body/eval_jaxpr/sfe,bfe->sbf/dot_general | solution.py:38
  203.8 2.8 fusion.164
  208.5 2.4 fusion.165
  211.0 2.5 fusion.167
  215.8 2.8 fusion.168
  218.6 2.5 fusion.170
  223.4 2.4 fusion.171
  225.8 3.6 %fusion.172 = f32[128,32,32]{2,1,0:T(8,128)} fusion(f32[128,32,32]{2,1,0:T(8,128)S(1)} %fusion.169, f32[128,32,32]{2,1,0:T(8,128)S(1)} %fusion.171, f32[32,32]{0,1:T(8,128)S(1)} %get-tuple-element.145), kind=kOutput, calls=%fused_computation.15.clone.1 | convolution fusion | flops 50593792 | bytes 1576960 | tf_op jit(solution)/shard_map/while/body/eval_jaxpr/ijp,jkp->ikp/dot_general | solution.py:26
  229.5 6.2 %fusion.173 = f32[32,128,1]{0,2,1:T(1,128)S(1)} fusion(f32[128,64,1]{1,2,0:T(1,128)S(1)} %bitcast.283, f32[32,128,64]{2,1,0:T(8,128)} %copy-done.3), kind=kOutput, calls=%fused_computation.47.clone.1 | convolution fusion | flops 3145728 | bytes 1097728 | tf_op jit(solution)/shard_map/while/body/eval_jaxpr/ipm,pm->ip/dot_general | solution.py:41
  241.1 2.8 copy.272
  266.8 6.1 %collective-permute-done.4 = f32[32,32,1,128]{3,1,2,0:T(8,128)S(1)} collective-permute-done((f32[32,32,1,128]{3,1,2,0:T(8,128)S(1)}, f32[32,32,1,128]{3,1,2,0:T(8,128)S(1)}, u32[]{:S(2)}, u32[]{:S(2)}) %collective-permute-start.4) | collective-permute-done | bytes 524320 | tf_op jit(solution)/shard_map/ppermute | solution.py:19
  273.7 8.0 %collective-permute-done.5 = f32[32,32,1,128]{3,1,2,0:T(8,128)} collective-permute-done((f32[32,32,1,128]{3,1,2,0:T(8,128)S(1)}, f32[32,32,1,128]{3,1,2,0:T(8,128)}, u32[]{:S(2)}, u32[]{:S(2)}) %collective-permute-start.5) | collective-permute-done | bytes 524320 | tf_op jit(solution)/shard_map/ppermute | solution.py:20
  281.7 3.6 %multiply_add_fusion.3 = (f32[32,32,2,128]{3,1,2,0:T(8,128)}, f32[32,32,2,128]{3,1,2,0:T(8,128)S(1)}, f32[32,32,2,128]{3,1,2,0:T(8,128)S(1)}, f32[32,32,2,128]{3,1,2,0:T(8,128)S(1)}) fusion(f32[32,32,2,128]{3,1,2,0:T(8,128)} %bitcast.286, f32[32,32,1,128]{3,1,2,0:T(8,128)} %copy-done.8, f32[32,32,1,128]{3,1,2,0:T(8,128)} %collective-permute-done.5), kind=kLoop, calls=%fused_computation.118 | loop fusion | flops 3145728 | bytes 6291456 | tf_op jit(solution)/shard_map/add | solution.py:106
  285.3 5.4 %copy.201 = f32[32,32,2,128]{1,0,3,2:T(8,128)} copy(f32[32,32,2,128]{3,1,2,0:T(8,128)} %get-tuple-element.83) | data formatting | bytes 2097152 | tf_op jit(solution)/shard_map/add | solution.py:106
  290.7 7.0 %fusion.81 = bf16[32,8,2,1,128]{0,1,4,2,3:T(8,128)(2,1)} fusion(f32[32,32,2,128]{1,0,3,2:T(8,128)} %copy.201, f32[32,8,2,1,128]{0,1,4,2,3:T(8,128)} %copy.241, f32[8,2,128]{0,2,1:T(8,128)} %copy.188), kind=kOutput, calls=%fused_computation.107 | convolution fusion | flops 25296896 | bytes 1449984 | tf_op jit(solution)/shard_map/jlay,jkay->klay/dot_general | solution.py:107
  299.8 4.4 %copy.204 = f32[32,32,2,128]{1,0,3,2:T(8,128)} copy(f32[32,32,2,128]{3,1,2,0:T(8,128)S(1)} %get-tuple-element.84) | data formatting | bytes 2097152 | tf_op jit(solution)/shard_map/add | solution.py:106
  304.2 6.2 %fusion.80 = bf16[32,8,2,1,128]{0,1,4,2,3:T(8,128)(2,1)S(1)} fusion(f32[32,32,2,128]{1,0,3,2:T(8,128)} %copy.204, f32[32,8,2,1,128]{0,1,4,2,3:T(8,128)} %copy.242, f32[8,2,128]{0,2,1:T(8,128)S(1)} %copy.202), kind=kOutput, calls=%fused_computation.106 | convolution fusion | flops 25296896 | bytes 1449984 | tf_op jit(solution)/shard_map/jlay,jkay->klay/dot_general | solution.py:107
  310.8 4.4 %copy.207 = f32[32,32,2,128]{1,0,3,2:T(8,128)} copy(f32[32,32,2,128]{3,1,2,0:T(8,128)S(1)} %get-tuple-element.92) | data formatting | bytes 2097152 | tf_op jit(solution)/shard_map/add | solution.py:106
  315.2 5.7 %fusion.79 = bf16[32,8,2,1,128]{0,1,4,2,3:T(8,128)(2,1)S(1)} fusion(f32[32,32,2,128]{1,0,3,2:T(8,128)} %copy.207, f32[32,8,2,1,128]{0,1,4,2,3:T(8,128)S(1)} %copy-done.7, f32[8,2,128]{0,2,1:T(8,128)S(1)} %copy.205), kind=kOutput, calls=%fused_computation.105 | convolution fusion | flops 25296896 | bytes 1449984 | tf_op jit(solution)/shard_map/jlay,jkay->klay/dot_general | solution.py:107
  321.3 4.4 %copy.210 = f32[32,32,2,128]{1,0,3,2:T(8,128)} copy(f32[32,32,2,128]{3,1,2,0:T(8,128)S(1)} %get-tuple-element.91) | data formatting | bytes 2097152 | tf_op jit(solution)/shard_map/add | solution.py:106
  325.7 5.5 %fusion.78 = bf16[32,8,2,1,128]{0,1,4,2,3:T(8,128)(2,1)S(1)} fusion(f32[32,32,2,128]{1,0,3,2:T(8,128)} %copy.210, f32[32,8,2,1,128]{0,1,4,2,3:T(8,128)S(1)} %copy-done.6, f32[8,2,128]{0,2,1:T(8,128)S(1)} %copy.208), kind=kOutput, calls=%fused_computation.104 | convolution fusion | flops 25296896 | bytes 1449984 | tf_op jit(solution)/shard_map/jlay,jkay->klay/dot_general | solution.py:107
  (137 shorter events, 63.1 us)
Async XLA Ops:
  1.1 1.2 copy-start.9
  2.3 2.7 copy-start.4
  2.3 2.7 copy-start.15
  12.7 11.8 %copy-start.14 = (f32[1,1,1,8,256]{4,3,2,1,0:T(8,128)S(1)}, f32[1,1,1,8,256]{4,3,2,1,0:T(8,128)}, u32[]{:S(2)}) copy-start(f32[1,1,1,8,256]{4,3,2,1,0:T(8,128)} %param.15) | copy-start | bytes 24580
  12.7 13.3 %copy-start.16 = (f32[1,1,1,256]{3,2,1,0:T(1,128)S(1)}, f32[1,1,1,256]{3,2,1,0:T(1,128)}, u32[]{:S(2)}) copy-start(f32[1,1,1,256]{3,2,1,0:T(1,128)} %param.12) | copy-start | bytes 3076
  12.8 13.3 %copy-start.17 = (f32[1,1,1,256]{3,2,1,0:T(1,128)S(1)}, f32[1,1,1,256]{3,2,1,0:T(1,128)}, u32[]{:S(2)}) copy-start(f32[1,1,1,256]{3,2,1,0:T(1,128)} %param.11) | copy-start | bytes 3076
  28.1 7.7 %collective-permute-start = (f32[34,2,1,1,256]{4,1,3,2,0:T(2,128)S(1)}, f32[34,2,1,1,256]{4,1,3,2,0:T(2,128)S(1)}, u32[]{:S(2)}, u32[]{:S(2)}) collective-permute-start(f32[34,2,1,1,256]{4,1,3,2,0:T(2,128)S(1)} %bitcast.290), channel_id=1, source_target_pairs={{0,4},{4,8},{8,12},{12,0},{1,5},{5,9},{9,13},{13,1},{2,6},{6,10},{... | collective-permute-start | bytes 208904 | tf_op jit(solution)/shard_map/ppermute | solution.py:19
  31.1 5.5 %collective-permute-start.1 = (f32[34,2,1,1,256]{4,1,3,2,0:T(2,128)S(1)}, f32[34,2,1,1,256]{4,1,3,2,0:T(2,128)S(1)}, u32[]{:S(2)}, u32[]{:S(2)}) collective-permute-start(f32[34,2,1,1,256]{4,1,3,2,0:T(2,128)S(1)} %bitcast.291), channel_id=1, source_target_pairs={{4,0},{8,4},{12,8},{0,12},{5,1},{9,5},{13,9},{1,13},{6,2},{10,6},{... | collective-permute-start | bytes 208904 | tf_op jit(solution)/shard_map/ppermute | solution.py:20
  36.7 8.2 %collective-permute-start.2 = (f32[34,2,3,1,256]{4,1,3,2,0:T(2,128)S(1)}, f32[34,2,3,1,256]{4,1,3,2,0:T(2,128)S(1)}, u32[]{:S(2)}, u32[]{:S(2)}) collective-permute-start(f32[34,2,3,1,256]{4,1,3,2,0:T(2,128)S(1)} %pad_maximum_fusion.4), channel_id=1, source_target_pairs={{0,2},{2,0},{1,3},{3,1},{4,6},{6,4},{5,7},{7,5},{8,10},{10,8},{9,1... | collective-permute-start | bytes 626696 | tf_op jit(solution)/shard_map/ppermute | solution.py:19
  38.2 9.5 %collective-permute-start.3 = (f32[34,2,3,1,256]{4,1,3,2,0:T(2,128)S(1)}, f32[34,2,3,1,256]{4,1,3,2,0:T(2,128)S(1)}, u32[]{:S(2)}, u32[]{:S(2)}) collective-permute-start(f32[34,2,3,1,256]{4,1,3,2,0:T(2,128)S(1)} %pad_maximum_fusion.4), channel_id=1, source_target_pairs={{2,0},{0,2},{3,1},{1,3},{6,4},{4,6},{7,5},{5,7},{10,8},{8,10},{11,... | collective-permute-start | bytes 626696 | tf_op jit(solution)/shard_map/ppermute | solution.py:20
  38.7 10.3 %copy-start.12 = (s32[2,128,64]{1,2,0:T(8,128)S(1)}, s32[2,128,64]{1,2,0:T(8,128)}, u32[]{:S(2)}) copy-start(s32[2,128,64]{1,2,0:T(8,128)} %param.16) | copy-start | bytes 196612
  38.7 10.3 %copy-start.13 = (f32[2,128,64]{1,2,0:T(8,128)S(1)}, f32[2,128,64]{1,2,0:T(8,128)}, u32[]{:S(2)}) copy-start(f32[2,128,64]{1,2,0:T(8,128)} %param.17) | copy-start | bytes 196612
  83.7 4.4 %copy-start = (f32[34,8192]{0,1:T(8,128)}, f32[34,8192]{0,1:T(8,128)S(1)}, u32[]{:S(2)}) copy-start(f32[34,8192]{0,1:T(8,128)S(1)} %select_bitcast_fusion.2) | copy-start | bytes 3342340 | tf_op jit(solution)/shard_map/while
  92.6 2.8 copy-start.1
  94.5 9.1 %copy-start.3 = (f32[32,128,64]{2,1,0:T(8,128)}, f32[32,128,64]{2,1,0:T(8,128)S(1)}, u32[]{:S(2)}) copy-start(f32[32,128,64]{2,1,0:T(8,128)S(1)} %broadcast_multiply_fusion.4) | copy-start | bytes 3145732 | tf_op jit(solution)/shard_map/while
  131.6 6.2 %copy-start.2 = (f32[128,32,32]{2,1,0:T(8,128)S(1)}, f32[128,32,32]{2,1,0:T(8,128)}, u32[]{:S(2)}) copy-start(f32[128,32,32]{2,1,0:T(8,128)} %fusion.172) | copy-start | bytes 1572868 | tf_op jit(solution)/shard_map/while
  181.7 4.4 %copy-start = (f32[34,8192]{0,1:T(8,128)}, f32[34,8192]{0,1:T(8,128)S(1)}, u32[]{:S(2)}) copy-start(f32[34,8192]{0,1:T(8,128)S(1)} %select_bitcast_fusion.2) | copy-start | bytes 3342340 | tf_op jit(solution)/shard_map/while
  190.6 2.8 copy-start.1
  192.5 9.1 %copy-start.3 = (f32[32,128,64]{2,1,0:T(8,128)}, f32[32,128,64]{2,1,0:T(8,128)S(1)}, u32[]{:S(2)}) copy-start(f32[32,128,64]{2,1,0:T(8,128)S(1)} %broadcast_multiply_fusion.4) | copy-start | bytes 3145732 | tf_op jit(solution)/shard_map/while
  229.5 6.2 %copy-start.2 = (f32[128,32,32]{2,1,0:T(8,128)S(1)}, f32[128,32,32]{2,1,0:T(8,128)}, u32[]{:S(2)}) copy-start(f32[128,32,32]{2,1,0:T(8,128)} %fusion.172) | copy-start | bytes 1572868 | tf_op jit(solution)/shard_map/while
  254.8 5.3 %copy-start.5 = (f32[32,8,8,128]{3,1,2,0:T(8,128)S(1)}, f32[32,8,8,128]{3,1,2,0:T(8,128)}, u32[]{:S(2)}) copy-start(f32[32,8,8,128]{3,1,2,0:T(8,128)} %copy-done.4) | copy-start | bytes 3145732
  256.2 5.4 %copy-start.10 = (f32[8,8,128]{2,0,1:T(8,128)S(1)}, f32[8,8,128]{2,0,1:T(8,128)}, u32[]{:S(2)}) copy-start(f32[8,8,128]{2,0,1:T(8,128)} %copy-done.9) | copy-start | bytes 98308
  256.2 16.7 %collective-permute-start.4 = (f32[32,32,1,128]{3,1,2,0:T(8,128)S(1)}, f32[32,32,1,128]{3,1,2,0:T(8,128)S(1)}, u32[]{:S(2)}, u32[]{:S(2)}) collective-permute-start(f32[32,32,1,128]{3,1,2,0:T(8,128)S(1)} %get-tuple-element.93), channel_id=1, source_target_pairs={{0,4},{4,8},{8,12},{12,0},{1,5},{5,9},{9,13},{13,1},{2,6},{6,10},{... | collective-permute-start | bytes 1572872 | tf_op jit(solution)/shard_map/ppermute | solution.py:19
  258.0 23.8 %collective-permute-start.5 = (f32[32,32,1,128]{3,1,2,0:T(8,128)S(1)}, f32[32,32,1,128]{3,1,2,0:T(8,128)}, u32[]{:S(2)}, u32[]{:S(2)}) collective-permute-start(f32[32,32,1,128]{3,1,2,0:T(8,128)S(1)} %get-tuple-element.94), channel_id=1, source_target_pairs={{4,0},{8,4},{12,8},{0,12},{5,1},{9,5},{13,9},{1,13},{6,2},{10,6},{... | collective-permute-start | bytes 1572872 | tf_op jit(solution)/shard_map/ppermute | solution.py:20
  272.9 0.8 copy-start.8
  310.7 4.4 %copy-start.7 = (f32[32,8,2,1,128]{0,1,4,2,3:T(8,128)S(1)}, f32[32,8,2,1,128]{0,1,4,2,3:T(8,128)}, u32[]{:S(2)}) copy-start(f32[32,8,2,1,128]{0,1,4,2,3:T(8,128)} %copy.243) | copy-start | bytes 786436
  321.3 4.4 %copy-start.6 = (f32[32,8,2,1,128]{0,1,4,2,3:T(8,128)S(1)}, f32[32,8,2,1,128]{0,1,4,2,3:T(8,128)}, u32[]{:S(2)}) copy-start(f32[32,8,2,1,128]{0,1,4,2,3:T(8,128)} %copy.244) | copy-start | bytes 786436
  325.7 5.9 %copy-start.11 = (bf16[32,8,2,1,128]{4,1,3,2,0:T(8,128)(2,1)S(1)}, bf16[32,8,2,1,128]{4,1,3,2,0:T(8,128)(2,1)}, u32[]{:S(2)}) copy-start(bf16[32,8,2,1,128]{4,1,3,2,0:T(8,128)(2,1)} %copy.211) | copy-start | bytes 393220
where the time goes:
time: 337 us; the launch traced here: 333 us
  local copies, waits for them, and re-layouts  138 us (41%)
  matrix products  116 us (34%)
  other arithmetic  27.2 us (8%)
  waiting for transfers between devices  26.5 us (8%)
  starting transfers between devices  11 us (3%)
  loops' own time  11 us (3%)
    gather x2, local copies, waits for them, and re-layouts, transforms(): jnp.take(nearby, list_ids.reshape(-1), axis=1)  55.5 us
    dot_general x22, matrix products, batched_product(): jnp.einsum('ijp,jkp->ikp', first_mat, second_mat, precision=lax.Precision...  55.5 us
    dot_general x4, matrix products, per_device(): jnp.einsum('jlay,jkay->klay', pert_cols[:, :, :, column], blend, precisio...  24.5 us
    add x4, local copies, waits for them, and re-layouts, per_device(): blend = (1.0 - abs(index_shift)) * centre + abs(index_shift) * beside  18.6 us
    dot_general x2, matrix products, transforms(): jnp.einsum('sfe,bfe->sbf', scaled_product, observed_perturbation, precisi...  16.4 us
    ppermute x3, waiting for transfers between devices, extended(): before = lax.ppermute(last, axis, up)  14.8 us
    select_n x4, other arithmetic, transforms(): jnp.take(nearby, list_ids.reshape(-1), axis=1)  12.5 us
    dot_general x2, matrix products, transforms(): jnp.einsum('ipm,pm->ip', scaled_product, innovation, precision=lax.Precis...  12.4 us
  transfers between devices with their start and end apart: 6, of which 6 were waited for; matrix products, arithmetic and copies ran while one was open for 2% of the time, Pallas kernels for 0%

commit v1 on v0

v1 whole, which is shorter than its diff:
```python
import functools
import math

import jax
import jax.numpy as jnp
from jax import lax
from jax.experimental import pallas as pl
from jax.experimental.pallas import tpu as pltpu
from jax.sharding import PartitionSpec as P

PX = 4
F32 = jnp.float32
BF16 = jnp.bfloat16
LANES = 128
SUB = 8
VMEM_LIMIT = 40 << 20


def params():
    return pltpu.CompilerParams(vmem_limit_bytes=VMEM_LIMIT)


def spread(ref, row):
    return ref[pl.ds(row, SUB, stride=0), :]


def block_base(ens):
    nb = ens // SUB
    base, at = [], 0
    for i in range(ens):
        base.append(at)
        at += SUB * (nb - i // SUB)
    return base, at


def observe_kernel(count_ref, members_ref, cell_ref, weight_ref, value_ref, rinv_ref, out_ref, wx, pick, part):
    ens, levels, width_x, width_y = members_ref.shape
    slots = cell_ref.shape[1]
    sten = cell_ref.shape[0]
    cell = cell_ref[...]
    low = jnp.bitwise_and(cell, width_y - 1)
    high = lax.shift_right_logical(cell, width_y.bit_length() - 1)
    low0 = jnp.min(low, axis=0, keepdims=True)
    code = high * 2 + (low - low0)
    weight = weight_ref[...]
    x_iota = lax.broadcasted_iota(jnp.int32, (width_x, slots), 0)
    for level in range(levels):
        for c in range(2):
            want = (level * width_x + x_iota) * 2 + c
            total = jnp.zeros((width_x, slots), F32)
            for s in range(sten):
                total = total + jnp.where(code[s : s + 1] == want, weight[s : s + 1], 0.0)
            wx[c, level * width_x : (level + 1) * width_x, :] = total
    y_iota = lax.broadcasted_iota(jnp.int32, (width_y, slots), 0)
    pick[:, :slots] = jnp.where(y_iota == low0, 1.0, 0.0).astype(BF16)
    pick[:, slots:] = jnp.where(y_iota == low0 + 1, 1.0, 0.0).astype(BF16)

    def member(k, _):
        rows = members_ref[k].astype(F32).reshape(levels * width_x, width_y).astype(BF16)
        got = jnp.dot(rows, pick[...], preferred_element_type=F32)
        term = got[:, :slots] * wx[0] + got[:, slots:] * wx[1]
        total = term[:SUB]
        for q in range(1, levels * width_x // SUB):
            total = total + term[q * SUB : (q + 1) * SUB]
        for half in range(slots // LANES):
            part[half, pl.ds(pl.multiple_of(k * SUB, SUB), SUB), :] = total[:, half * LANES : (half + 1) * LANES]
        return 0

    lax.fori_loop(0, ens, member, 0, unroll=2)
    groups = []
    for kb in range(ens // SUB):
        halves = []
        for half in range(slots // LANES):
            total = part[half, pl.ds(kb * SUB * SUB, SUB, stride=SUB), :]
            for s in range(1, SUB):
                total = total + part[half, pl.ds(kb * SUB * SUB + s, SUB, stride=SUB), :]
            halves.append(total)
        groups.append(jnp.concatenate(halves, axis=1))
    total = groups[0]
    for group in groups[1:]:
        total = total + group
    mean = jnp.sum(total, axis=0, keepdims=True) / ens
    for kb in range(ens // SUB):
        out_ref[kb * SUB : (kb + 1) * SUB, :] = groups[kb] - mean
    live = lax.broadcasted_iota(jnp.int32, (1, slots), 1) < count_ref[0]
    innovation = value_ref[...] - mean
    rinv = jnp.where(live, rinv_ref[...], 0.0)
    row = lax.broadcasted_iota(jnp.int32, (SUB, slots), 0)
    out_ref[ens : ens + SUB, :] = jnp.where(row == 0, innovation, jnp.where(row == 1, rinv, 0.0))


def observe(members, cell, weight, value, rinv, count):
    ens, levels, width_x, width_y = members.shape
    sten, slots = cell.shape
    vmem = pl.BlockSpec(memory_space=pltpu.VMEM)
    return pl.pallas_call(
        observe_kernel,
        out_shape=jax.ShapeDtypeStruct((ens + SUB, slots), F32),
        in_specs=[pl.BlockSpec(memory_space=pltpu.SMEM)] + [vmem] * 5,
        out_specs=vmem,
        scratch_shapes=[
            pltpu.VMEM((2, levels * width_x, slots), F32),
            pltpu.VMEM((width_y, 2 * slots), BF16),
            pltpu.VMEM((slots // LANES, ens * SUB, LANES), F32),
        ],
        compiler_params=params(),
        name="observe",
    )(count, members, cell, weight, value, rinv)


def taper_kernel(gz_ref, own_ref, halo_ref, high_ref, low_ref, code_s, slot_s, taper_s, *, n_x, n_y, slots):
    patches, mloc = own_ref.shape[0], own_ref.shape[1] // 2
    batch = patches // SUB
    gz = gz_ref[0]
    n_buf = 2 * n_x * n_y
    lanes = SUB * mloc
    for r, ref in enumerate((own_ref, halo_ref)):
        shift = 0 if r == 0 else jnp.where(gz == 0, -1, 1)
        pairs = [ref[pl.ds(q, batch, stride=SUB), :] for q in range(SUB)]
        ids = jnp.concatenate([pair[:, :mloc] for pair in pairs], axis=1).astype(jnp.int32)
        taper = jnp.concatenate([pair[:, mloc:] for pair in pairs], axis=1)
        slot = jnp.bitwise_and(ids, slots - 1)
        tile = lax.shift_right_logical(ids, slots.bit_length() - 1)
        upper = (tile >= 9).astype(jnp.int32)
        tile = tile - 9 * upper
        a = (tile >= 3).astype(jnp.int32) + (tile >= 6).astype(jnp.int32)
        b = tile - 3 * a
        other = jnp.where(upper == gz, 0, 1)
        x = lax.rem(a - 1 + shift + 2 * n_x, n_x)
        y = lax.rem(b - 1 + n_y, n_y)
        patch = lax.shift_right_logical(lax.broadcasted_iota(jnp.int32, ids.shape, 1), mloc.bit_length() - 1)
        rows = pl.ds(r * batch, batch)
        code_s[rows, :] = ((other * n_x + x) * n_y + y) * SUB + patch
        slot_s[rows, :] = slot
        taper_s[rows, :] = taper

    def dense(it):
        code = code_s[pl.ds(it, 1), :]
        slot = slot_s[pl.ds(it, 1), :]
        taper = taper_s[pl.ds(it, 1), :]
        hit = lax.broadcasted_iota(jnp.int32, (n_buf * SUB, lanes), 0) == code
        coarse = taper.astype(BF16).astype(F32)
        left = jnp.concatenate(
            [jnp.where(hit, coarse, 0.0).astype(BF16), jnp.where(hit, taper - coarse, 0.0).astype(BF16)], axis=0
        )
        right = jnp.where(lax.broadcasted_iota(jnp.int32, (slots, lanes), 0) == slot, 1.0, 0.0).astype(BF16)
        both = lax.dot_general(left, right, (((1,), (1,)), ((), ())), preferred_element_type=F32)
        return both[: n_buf * SUB] + both[n_buf * SUB :]

    def body(it, _):
        first = dense(2 * it)
        second = dense(2 * it + 1)
        for n in range(n_buf):
            rows = slice(n * SUB, (n + 1) * SUB)
            block = jnp.concatenate([first[rows], second[rows]], axis=0)
            high = block.astype(BF16)
            at = pl.ds(pl.multiple_of(it * 2 * SUB, 2 * SUB), 2 * SUB)
            high_ref[n, at, :] = high
            low_ref[n, at, :] = (block - high.astype(F32)).astype(BF16)
        return 0

    lax.fori_loop(0, batch, body, 0)


def dense_tapers(gz, own, halo, n_x, n_y, slots):
    patches, mloc = own.shape[0], own.shape[1] // 2
    vmem = pl.BlockSpec(memory_space=pltpu.VMEM)
    n_buf = 2 * n_x * n_y
    shape = jax.ShapeDtypeStruct((n_buf, 2 * patches, slots), BF16)
    batch = patches // SUB
    return pl.pallas_call(
        functools.partial(taper_kernel, n_x=n_x, n_y=n_y, slots=slots),
        out_shape=(shape, shape),
        in_specs=[pl.BlockSpec(memory_space=pltpu.SMEM), vmem, vmem],
        out_specs=(vmem, vmem),
        scratch_shapes=[
            pltpu.VMEM((2 * batch, SUB * mloc), jnp.int32),
            pltpu.VMEM((2 * batch, SUB * mloc), jnp.int32),
            pltpu.VMEM((2 * batch, SUB * mloc), F32),
        ],
        compiler_params=params(),
        name="dense_tapers",
    )(gz, own, halo)


def gram_kernel(*refs, ens, n_stack):
    stacks = refs[:n_stack]
    high_ref, low_ref, out_ref, z_s, zr_s = refs[n_stack:]
    nb = ens // SUB
    slots = stacks[0].shape[2]
    base, tri = block_base(ens)
    rows = tri + ens
    nt = (((1,), (1,)), ((), ()))
    first = True
    n = 0
    for stack in stacks:
        for t in range(stack.shape[0]):
            ob = stack[t, :ens, :]
            rinv = stack[t, ens + 1 : ens + 2, :]
            zr_s[...] = ob * rinv
            wi = stack[t, ens : ens + 1, :]
            for i in range(0, ens, 2):
                ib = i // SUB
                part = jnp.concatenate(
                    [ob[kb * SUB : (kb + 1) * SUB] * zr_s[q : q + 1, :] for q in (i, i + 1) for kb in range(ib, nb)], axis=0
                )
                high = part.astype(BF16)
                z_s[base[i] : base[i] + part.shape[0], :] = high
                z_s[rows + base[i] : rows + base[i] + part.shape[0], :] = (part - high.astype(F32)).astype(BF16)
            part = zr_s[...] * wi
            high = part.astype(BF16)
            z_s[tri:rows, :] = high
            z_s[rows + tri : 2 * rows, :] = (part - high.astype(F32)).astype(BF16)
            got = lax.dot_general(z_s[...], high_ref[n], nt, preferred_element_type=F32)
            more = lax.dot_general(z_s[:rows, :], low_ref[n], nt, preferred_element_type=F32)
            total = got[:rows] + (got[rows:] + more)
            out_ref[...] = total if first else out_ref[...] + total
            first = False
            n += 1


def grams(stacks, high, low, ens):
    vmem = pl.BlockSpec(memory_space=pltpu.VMEM)
    _, tri = block_base(ens)
    rows = tri + ens
    patches, slots = high.shape[1:]
    return pl.pallas_call(
        functools.partial(gram_kernel, ens=ens, n_stack=len(stacks)),
        out_shape=jax.ShapeDtypeStruct((rows, patches), F32),
        in_specs=[vmem] * (len(stacks) + 2),
        out_specs=vmem,
        scratch_shapes=[pltpu.VMEM((2 * rows, slots), BF16), pltpu.VMEM((ens, slots), F32)],
        compiler_params=params(),
        name="grams",
    )(*stacks, high, low)


def product(ens, a, b, dests, epilogue):
    nb = ens // SUB
    for ib in range(nb):
        n = nb - ib
        rows = 4 if n > 2 else 8

        def body(step, _, ib=ib, n=n, rows=rows):
            i0 = ib * SUB + step * rows
            acc = [[None] * n for _ in range(rows)]
            for j in range(ens):
                right = [b[j * ens + SUB * kb : j * ens + SUB * (kb + 1), :] for kb in range(ib, nb)]
                for ii in range(rows):
                    left = spread(a, (i0 + ii) * ens + j)
                    for q in range(n):
                        term = left * right[q]
                        acc[ii][q] = term if j == 0 else acc[ii][q] + term
            for ii in range(rows):
                for q in range(n):
                    kb = ib + q
                    eye = None
                    if q == 0:
                        eye = lax.broadcasted_iota(jnp.int32, (SUB, LANES), 0) == step * rows + ii
                    outs = epilogue(acc[ii][q], pl.ds((i0 + ii) * ens + SUB * kb, SUB), eye)
                    for dest, value in zip(dests, outs):
                        dest[pl.ds((i0 + ii) * ens + SUB * kb, SUB), :] = value
                        if kb > ib:
                            dest[pl.ds(SUB * kb * ens + i0 + ii, SUB, stride=ens), :] = value
            return 0

        lax.fori_loop(0, SUB // rows, body, 0)


def root_kernel(gram_ref, out_ref, s_a, s_b, s_c, s_d, vec, *, ens):
    nb = ens // SUB
    base, tri = block_base(ens)
    diag = gram_ref[0:1, :]
    for i in range(1, ens):
        at = base[i] + i % SUB
        diag = diag + gram_ref[at : at + 1, :]
    half = 0.5 * (diag + (ens - 1.0) * ens)
    scale = jnp.broadcast_to(1.0 / half, (SUB, LANES))
    iota = lax.broadcasted_iota(jnp.int32, (SUB, LANES), 0)
    for i in range(ens):
        for kb in range(i // SUB, nb):
            at = base[i] + SUB * (kb - i // SUB)
            value = gram_ref[at : at + SUB, :]
            if kb == i // SUB:
                value = jnp.where(iota == i % SUB, value + (ens - 1.0), value)
            value = value * scale
            s_a[i * ens + SUB * kb : i * ens + SUB * (kb + 1), :] = value
            if kb > i // SUB:
                s_a[pl.ds(SUB * kb * ens + i, SUB, stride=ens), :] = value

    def plain(acc, at, eye):
        return (acc,)

    def quadratic(lin):
        def epilogue(acc, at, eye):
            rest = 0.0625 * acc - 0.5625 * lin[at, :]
            if eye is not None:
                rest = jnp.where(eye, rest + 1.6875, rest)
            return (acc, rest)

        return epilogue

    def quartic(lin):
        def epilogue(acc, at, eye):
            rest = acc - 2.4375 * lin[at, :]
            if eye is not None:
                rest = jnp.where(eye, rest + 2.25, rest)
            return (rest,)

        return epilogue

    product(ens, s_a, s_a, (s_b, s_c), quadratic(s_a))
    product(ens, s_b, s_c, (s_d,), quartic(s_a))
    product(ens, s_d, s_d, (s_b,), plain)
    product(ens, s_a, s_b, (s_c,), plain)
    product(ens, s_c, s_c, (s_a, s_b), quadratic(s_c))
    product(ens, s_a, s_b, (vec.at[pl.ds(0, ens * ens)],), quartic(s_c))
    product(ens, s_d, vec.at[pl.ds(0, ens * ens)], (s_a,), plain)

    right = ens * ens
    vec[right : right + ens, :] = gram_ref[tri : tri + ens, :]

    def apply(source):
        sums = [None] * nb
        for i in range(ens):
            left = spread(vec, source + i)
            for kb in range(nb):
                term = left * s_a[i * ens + SUB * kb : i * ens + SUB * (kb + 1), :]
                sums[kb] = term if i == 0 else sums[kb] + term
        return sums

    inner = apply(right)
    for kb in range(nb):
        vec[right + ens + SUB * kb : right + ens + SUB * (kb + 1), :] = inner[kb]
    outer = apply(right + ens)
    for kb in range(nb):
        out_ref[tri + SUB * kb : tri + SUB * (kb + 1), :] = outer[kb] * scale
    factor = jnp.broadcast_to(math.sqrt(ens - 1.0) / jnp.sqrt(half), (SUB, LANES))
    for i in range(ens):
        for kb in range(i // SUB, nb):
            at = base[i] + SUB * (kb - i // SUB)
            out_ref[at : at + SUB, :] = s_a[i * ens + SUB * kb : i * ens + SUB * (kb + 1), :] * factor


def roots(gram, row, ens):
    rows = gram.shape[0]
    square = pltpu.VMEM((ens * ens, LANES), F32)
    return pl.pallas_call(
        functools.partial(root_kernel, ens=ens),
        out_shape=jax.ShapeDtypeStruct((rows, LANES), F32),
        grid=(1,),
        in_specs=[pl.BlockSpec((rows, LANES), lambda g: (0, row))],
        out_specs=pl.BlockSpec((rows, LANES), lambda g: (0, 0)),
        scratch_shapes=[square] * 4 + [pltpu.VMEM((ens * ens + 2 * ens, LANES), F32)],
        compiler_params=params(),
        name="roots",
    )(gram)


def update_kernel(gz_ref, members_ref, own_ref, pair_ref, halo_ref, far_ref, out_ref, pert_s, mean_s, tx_s):
    ens, levels, width_x, width_y = members_ref.shape
    nb = ens // SUB
    base, tri = block_base(ens)
    column = lax.broadcasted_iota(jnp.int32, (width_x, width_y), 0)
    column = jnp.where(gz_ref[0] == 0, column, width_x - 1 - column).astype(F32)
    place = (column + 0.5) / PX - 0.5
    weights = [
        jnp.maximum(0.0, 1.0 - jnp.abs(place - centre)) for centre in (0.0, 1.0, -1.0, 2.0)
    ]
    sources = (own_ref, pair_ref, halo_ref, far_ref)

    def blend(row):
        total = weights[0] * spread(sources[0], row)
        for w, ref in zip(weights[1:], sources[1:]):
            total = total + w * spread(ref, row)
        return total

    for level in range(levels):
        total = members_ref[0, level].astype(F32)
        for k in range(1, ens):
            total = total + members_ref[k, level].astype(F32)
        mean = total / ens
        shift = mean
        for k in range(ens):
            pert = members_ref[k, level].astype(F32) - mean
            pert_s[k * levels + level] = pert
        mean_s[level] = shift
    for j in range(ens):
        shared = blend(tri + j)
        for level in range(levels):
            mean_s[level] = mean_s[level] + pert_s[j * levels + level] * shared

    for ib in range(nb):

        def rows(step, _, ib=ib):
            i = ib * SUB + step
            start = base[ib * SUB] + step * SUB * (nb - ib)
            for kb in range(ib, nb):
                for s in range(SUB):
                    value = blend(start + SUB * (kb - ib) + s)
                    tx_s[i * ens + SUB * kb + s] = value
                    if kb > ib:
                        tx_s[(SUB * kb + s) * ens + i] = value
            return 0

        lax.fori_loop(0, SUB, rows, 0)

    wide = 4

    def body(step, _):
        k0 = step * wide
        for l0 in range(0, levels, wide):
            acc = [[mean_s[l0 + l] for l in range(wide)] for _ in range(wide)]
            for j in range(ens):
                pert = [pert_s[j * levels + l0 + l] for l in range(wide)]
                for k in range(wide):
                    t = tx_s[j * ens + k0 + k]
                    for l in range(wide):
                        acc[k][l] = acc[k][l] + t * pert[l]
            for k in range(wide):
                for l in range(wide):
                    out_ref[k0 + k, l0 + l] = acc[k][l].astype(BF16)
        return 0

    lax.fori_loop(0, ens // wide, body, 0)


def update(gz, members, own, pair, halo, far):
    ens, levels, width_x, width_y = members.shape
    vmem = pl.BlockSpec(memory_space=pltpu.VMEM)
    tile = (width_x, width_y)
    return pl.pallas_call(
        update_kernel,
        out_shape=jax.ShapeDtypeStruct(members.shape, BF16),
        in_specs=[pl.BlockSpec(memory_space=pltpu.SMEM)] + [vmem] * 5,
        out_specs=vmem,
        scratch_shapes=[
            pltpu.VMEM((ens * levels,) + tile, F32),
            pltpu.VMEM((levels,) + tile, F32),
            pltpu.VMEM((ens * ens,) + tile, F32),
        ],
        compiler_params=params(),
        name="update",
    )(gz, members, own, pair, halo, far)


def shifted(x, axis, shift):
    size = lax.axis_size(axis)
    return lax.ppermute(x, axis, [((i + shift) % size, i) for i in range(size)])


def swapped(x):
    return lax.ppermute(x, "gz", [(0, 1), (1, 0)])


def signed(index, count):
    return index if index <= count // 2 else index - count


def per_device(
    members, obs_value, obs_rinv, obs_count, stencil_cell, stencil_weight, patch_list, patch_taper
):
    ens = members.shape[0]
    slots = obs_value.shape[-1]
    size_x, size_y = lax.axis_size("gx"), lax.axis_size("gy")
    n_x, n_y = min(size_x, 5), min(size_y, 3)
    gz = lax.axis_index("gz")
    gz_arg = gz.reshape(1).astype(jnp.int32)

    lists = jnp.concatenate([patch_list.astype(F32), patch_taper], axis=-1)
    own_list = lax.dynamic_index_in_dim(lists, gz, 0, keepdims=False)
    sent_list = lax.dynamic_index_in_dim(lists, 1 - gz, 0, keepdims=False)
    turn = [(2 * i, 2 * ((i + 1) % size_x)) for i in range(size_x)]
    turn += [(2 * i + 1, 2 * ((i - 1) % size_x) + 1) for i in range(size_x)]
    halo_list = lax.ppermute(sent_list, ("gx", "gz"), turn)

    packet = observe(
        members,
        stencil_cell.reshape(-1, slots),
        stencil_weight.reshape(-1, slots),
        obs_value.reshape(1, slots),
        obs_rinv.reshape(1, slots),
        obs_count.reshape(1),
    )
    high, low = dense_tapers(gz_arg, own_list, halo_list, n_x, n_y, slots)

    along = [packet] + [shifted(packet, "gx", signed(x, n_x)) for x in range(1, n_x)]
    along = jnp.stack(along, axis=0)
    across = [along] + [shifted(along, "gy", signed(y, n_y)) for y in range(1, n_y)]
    here = jnp.stack(across, axis=1).reshape(n_x * n_y, ens + SUB, slots)
    there = swapped(here)

    gram = grams((here, there), high, low, ens)
    own = roots(gram, 0, ens)
    pair = swapped(own)
    halo = roots(gram, 1, ens)
    far = swapped(halo)
    return update(gz_arg, members, own, pair, halo, far)


def solution(mesh):
    return jax.shard_map(
        per_device,
        mesh=mesh,
        in_specs=(
            P("groups", "gz", "gx", "gy"),
            P(("groups", "gz"), "gx", "gy", None),
            P(("groups", "gz"), "gx", "gy", None),
            P(("groups", "gz"), "gx", "gy"),
            P(("groups", "gz"), "gx", "gy", None, None),
            P(("groups", "gz"), "gx", "gy", None, None),
            P(("groups", "gx"), "gy", None),
            P(("groups", "gx"), "gy", None),
        ),
        out_specs=P("groups", "gz", "gx", "gy"),
        check_vma=False,
    )
```

time: 337 us -> 59.8 us (0.18); the launches traced: 333 us -> 59.5 us
  local copies, waits for them, and re-layouts: 138 us -> 4 us
  matrix products: 116 us -> 0 us
  Pallas kernels: 0 us -> 31.3 us
  other arithmetic: 27.2 us -> 0.07 us
  waiting for transfers between devices: 26.5 us -> 13.7 us
  loops' own time: 11 us -> 0 us
    dot_general x34 -> x0, matrix products: 116 us -> none  [the longest x22 55.5 us: batched_product(): jnp.einsum('ijp,jkp->ikp', first_mat, second_mat, precision=lax.Precision...]
    gather x5 -> x0, local copies, waits for them, and re-layouts: 75 us -> none  [the longest x2 55.5 us: transforms(): jnp.take(nearby, list_ids.reshape(-1), axis=1)]
    pallas_call x0 -> x6, Pallas kernels: none -> 31.3 us  [the longest x2 13.4 us: roots(): pl.pallas_call(functools.partial(root_kernel, ens=ens), out_shape=jax.Sha...]
    add x9 -> x0, local copies, waits for them, and re-layouts: 19.7 us -> none  [the longest x4 18.6 us: per_device(): blend = (1.0 - abs(index_shift)) * centre + abs(index_shift) * beside]
    slice x6 -> x0, local copies, waits for them, and re-layouts: 18.9 us -> none  [the longest x2 8.81 us: transforms(): innovation = picked[ensemble]]
    ppermute x6 -> x8, waiting for transfers between devices: 26.5 us -> 13.7 us  [the longest x4 6.47 us: shifted(): return lax.ppermute(x, axis, [((i + shift) % size, i) for i in range(size)])]
    select_n x4 -> x0, other arithmetic: 12.5 us -> none  [transforms(): jnp.take(nearby, list_ids.reshape(-1), axis=1)]
    another operation x1 -> x0, loops' own time: 11 us -> none  [row_transforms(): stacked = lax.map(one_row, (list_ids, tapers))]
  transfers between devices with their start and end apart: 6 -> 8, of which waited for: 6 -> 7; matrix products, arithmetic and copies ran while one was open for 2% -> 0% of each run, Pallas kernels for 0% -> 10%
where the time goes in v1:
time: 59.8 us; the launch traced here: 59.5 us
  Pallas kernels  31.3 us (52%)
  waiting for transfers between devices  13.7 us (23%)
  starting transfers between devices  9.6 us (16%)
  local copies, waits for them, and re-layouts  4 us (7%)
  between operations  0.8 us (1%)
    pallas_call x2, Pallas kernels, roots(): pl.pallas_call(functools.partial(root_kernel, ens=ens), out_shape=jax.Sha...  13.4 us
    ppermute x4, starting transfers between devices, shifted(): return lax.ppermute(x, axis, [((i + shift) % size, i) for i in range(size)])  8.58 us
    ppermute x4, waiting for transfers between devices, shifted(): return lax.ppermute(x, axis, [((i + shift) % size, i) for i in range(size)])  6.47 us
    pallas_call x1, Pallas kernels, dense_tapers(): pl.pallas_call(functools.partial(taper_kernel, n_x=n_x, n_y=n_y, slots=sl...  5.79 us
    ppermute x1, waiting for transfers between devices, per_device(): halo_list = lax.ppermute(sent_list, ('gx', 'gz'), turn)  5.64 us
    pallas_call x1, Pallas kernels, grams(): pl.pallas_call(functools.partial(gram_kernel, ens=ens, n_stack=len(stacks...  4.55 us
    pallas_call x1, Pallas kernels, update(): pl.pallas_call(update_kernel, out_shape=jax.ShapeDtypeStruct(members.shap...  4.48 us
    unnamed x16, local copies, waits for them, and re-layouts  3.8 us
  transfers between devices with their start and end apart: 8, of which 7 were waited for; matrix products, arithmetic and copies ran while one was open for 0% of the time, Pallas kernels for 10%

profile of v1, /device:TPU:0, one launch (start us, length us, event | category | flops | bytes accessed | tf_op | source)
XLA Modules:
  0.0 59.5 jit_solution(8891928254250311298)
XLA Ops:
  0.7 0.0 copy-start
  0.7 1.0 %copy-done = bf16[32,8,8,128]{3,2,1,0:T(8,128)(2,1)S(1)} copy-done((bf16[32,8,8,128]{3,2,1,0:T(8,128)(2,1)S(1)}, bf16[32,8,8,128]{3,2,1,0:T(8,128)(2,1)}, u32[]{:S(2)}) %copy-start) | copy-done | bytes 524312
  1.7 0.0 copy-start.2
  1.7 0.7 %copy-done.2 = s32[1,1,1,8,256]{4,3,2,1,0:T(8,128)S(1)} copy-done((s32[1,1,1,8,256]{4,3,2,1,0:T(8,128)S(1)}, s32[1,1,1,8,256]{4,3,2,1,0:T(8,128)}, u32[]{:S(2)}) %copy-start.2) | copy-done | bytes 8216
  2.4 0.0 copy-start.3
  2.4 0.7 %copy-done.3 = f32[1,1,1,8,256]{4,3,2,1,0:T(8,128)S(1)} copy-done((f32[1,1,1,8,256]{4,3,2,1,0:T(8,128)S(1)}, f32[1,1,1,8,256]{4,3,2,1,0:T(8,128)}, u32[]{:S(2)}) %copy-start.3) | copy-done | bytes 8216
  3.1 0.0 copy-start.4
  3.1 0.7 %copy-done.4 = f32[1,1,1,256]{3,2,1,0:T(1,128)S(1)} copy-done((f32[1,1,1,256]{3,2,1,0:T(1,128)S(1)}, f32[1,1,1,256]{3,2,1,0:T(1,128)}, u32[]{:S(2)}) %copy-start.4) | copy-done | bytes 1048
  3.8 0.0 copy-start.5
  3.8 0.7 %copy-done.5 = f32[1,1,1,256]{3,2,1,0:T(1,128)S(1)} copy-done((f32[1,1,1,256]{3,2,1,0:T(1,128)S(1)}, f32[1,1,1,256]{3,2,1,0:T(1,128)}, u32[]{:S(2)}) %copy-start.5) | copy-done | bytes 1048
  4.5 0.0 copy-start.6
  4.5 0.0 copy-start.7
  4.5 3.0 %observe.1 = f32[40,256]{1,0:T(8,128)S(1)} custom-call(s32[1]{0:T(128)} %bitcast.16.count_ref, bf16[32,8,8,128]{3,2,1,0:T(8,128)(2,1)S(1)} %copy-done, s32[8,256]{1,0:T(8,128)S(1)} %bitcast.21, f32[8,256]{1,0:T(8,128)S(1)} %bitcast.22, f32[1,256]{1,0:T(1,128)S(1)} %bitcast.23, f32[1,256]{1,0:T(1,128)S(1)} %bitcast.24), custom_call_target="tpu_custom_call" | custom-call | tf_op jit(solution)/shard_map/observe/pallas_call | solution.py:96
  7.5 3.1 %collective-permute-start.2 = (f32[40,256]{1,0:T(8,128)S(1)}, f32[40,256]{1,0:T(8,128)S(1)}, u32[]{:S(2)}, u32[]{:S(2)}) collective-permute-start(f32[40,256]{1,0:T(8,128)S(1)} %observe.1), channel_id=1, source_target_pairs={{12,0},{0,4},{4,8},{8,12},{13,1},{1,5},{5,9},{9,13},{14,2},{2,6},{... | collective-permute-start | bytes 122888 | tf_op jit(solution)/shard_map/ppermute | solution.py:449
  10.6 2.6 %collective-permute-start.1 = (f32[40,256]{1,0:T(8,128)S(1)}, f32[40,256]{1,0:T(8,128)S(1)}, u32[]{:S(2)}, u32[]{:S(2)}) collective-permute-start(f32[40,256]{1,0:T(8,128)S(1)} %observe.1), channel_id=1, source_target_pairs={{8,0},{12,4},{0,8},{4,12},{9,1},{13,5},{1,9},{5,13},{10,2},{14,6},... | collective-permute-start | bytes 122888 | tf_op jit(solution)/shard_map/ppermute | solution.py:449
  13.1 1.4 %collective-permute-start = (f32[40,256]{1,0:T(8,128)S(1)}, f32[40,256]{1,0:T(8,128)S(1)}, u32[]{:S(2)}, u32[]{:S(2)}) collective-permute-start(f32[40,256]{1,0:T(8,128)S(1)} %observe.1), channel_id=1, source_target_pairs={{4,0},{8,4},{12,8},{0,12},{5,1},{9,5},{13,9},{1,13},{6,2},{10,6},{... | collective-permute-start | bytes 122888 | tf_op jit(solution)/shard_map/ppermute | solution.py:449
  14.5 0.1 collective-permute-done.2
  14.6 1.4 %collective-permute-done.1 = f32[40,256]{1,0:T(8,128)S(1)} collective-permute-done((f32[40,256]{1,0:T(8,128)S(1)}, f32[40,256]{1,0:T(8,128)S(1)}, u32[]{:S(2)}, u32[]{:S(2)}) %collective-permute-start.1) | collective-permute-done | bytes 40992 | tf_op jit(solution)/shard_map/ppermute | solution.py:449
  15.9 1.2 %collective-permute-done = f32[40,256]{1,0:T(8,128)S(1)} collective-permute-done((f32[40,256]{1,0:T(8,128)S(1)}, f32[40,256]{1,0:T(8,128)S(1)}, u32[]{:S(2)}, u32[]{:S(2)}) %collective-permute-start) | collective-permute-done | bytes 40992 | tf_op jit(solution)/shard_map/ppermute | solution.py:449
  17.2 1.6 %collective-permute-start.3 = (f32[4,40,256]{2,1,0:T(8,128)S(1)}, f32[4,40,256]{2,1,0:T(8,128)S(1)}, u32[]{:S(2)}, u32[]{:S(2)}) collective-permute-start(f32[4,40,256]{2,1,0:T(8,128)S(1)} %get-tuple-element.10), channel_id=1, source_target_pairs={{2,0},{0,2},{3,1},{1,3},{6,4},{4,6},{7,5},{5,7},{10,8},{8,10},{11,... | collective-permute-start | bytes 491528 | tf_op jit(solution)/shard_map/ppermute | solution.py:449
  18.7 3.8 %collective-permute-done.3 = f32[4,40,256]{2,1,0:T(8,128)S(1)} collective-permute-done((f32[4,40,256]{2,1,0:T(8,128)S(1)}, f32[4,40,256]{2,1,0:T(8,128)S(1)}, u32[]{:S(2)}, u32[]{:S(2)}) %collective-permute-start.3) | collective-permute-done | bytes 163872 | tf_op jit(solution)/shard_map/ppermute | solution.py:449
  22.6 0.1 collective-permute-start.4
  22.7 0.0 copy-done.6
  22.7 0.0 copy-done.7
  22.8 0.1 copy.11
  22.9 0.4 collective-permute-start.5
  23.2 0.1 copy.10
  23.3 5.6 %collective-permute-done.5.halo_ref = f32[128,128]{1,0:T(8,128)S(1)} collective-permute-done((f32[128,128]{1,0:T(8,128)S(1)}, f32[128,128]{1,0:T(8,128)S(1)}, u32[]{:S(2)}, u32[]{:S(2)}) %collective-permute-start.5) | collective-permute-done | bytes 65568 | tf_op jit(solution)/shard_map/ppermute | solution.py:475
  29.0 5.8 %dense_tapers.1 = (bf16[16,256,256]{2,1,0:T(8,128)(2,1)S(1)}, bf16[16,256,256]{2,1,0:T(8,128)(2,1)S(1)}) custom-call(s32[1]{0:T(128)} %bitcast.gz_ref, f32[128,128]{1,0:T(8,128)S(1)} %bitcast.19, f32[128,128]{1,0:T(8,128)S(1)} %collective-permute-done.5.halo_ref), custom_call_target="tpu_custom_call" | custom-call | tf_op jit(solution)/shard_map/dense_tapers/pallas_call | solution.py:171
  34.8 0.0 collective-permute-done.4.refs_1_
  34.8 4.6 %grams.1.gram_ref = f32[672,256]{1,0:T(8,128)S(1)} custom-call(f32[8,40,256]{2,1,0:T(8,128)S(1)} %bitcast.18, f32[8,40,256]{2,1,0:T(8,128)S(1)} %collective-permute-done.4.refs_1_, bf16[16,256,256]{2,1,0:T(8,128)(2,1)S(1)} %get-tuple-element.7.refs_2_, bf16[16,256,256]{2,1,0:T(8,128)(2,1)S(1)} %get-tuple-element.8.refs_3_), custom_call_target="tpu_custom_call" | custom-call | tf_op jit(solution)/shard_map/grams/pallas_call | solution.py:227
  39.3 0.0 copy-start.1
  39.4 6.7 %roots.3.halo_ref = f32[672,128]{1,0:T(8,128)S(1)} custom-call(f32[672,256]{1,0:T(8,128)S(1)} %grams.1.gram_ref), custom_call_target="tpu_custom_call" | custom-call | tf_op jit(solution)/shard_map/roots/pallas_call | solution.py:348
  46.1 6.7 %roots.2.own_ref = f32[672,128]{1,0:T(8,128)S(1)} custom-call(f32[672,256]{1,0:T(8,128)S(1)} %grams.1.gram_ref), custom_call_target="tpu_custom_call" | custom-call | tf_op jit(solution)/shard_map/roots/pallas_call | solution.py:348
  52.8 0.1 collective-permute-start.6
  52.9 0.5 collective-permute-start.7
  53.4 1.1 %collective-permute-done.6.pair_ref = f32[672,128]{1,0:T(8,128)S(1)} collective-permute-done((f32[672,128]{1,0:T(8,128)S(1)}, f32[672,128]{1,0:T(8,128)S(1)}, u32[]{:S(2)}, u32[]{:S(2)}) %collective-permute-start.6) | collective-permute-done | bytes 344096 | tf_op jit(solution)/shard_map/ppermute | solution.py:453
  54.5 0.5 collective-permute-done.7.far_ref
  55.0 0.0 copy-done.1
  55.0 4.5 %update.1 = bf16[32,8,8,128]{3,2,1,0:T(8,128)(2,1)} custom-call(s32[1]{0:T(128)} %bitcast.gz_ref, bf16[32,8,8,128]{3,2,1,0:T(8,128)(2,1)S(1)} %copy-done.1, f32[672,128]{1,0:T(8,128)S(1)} %roots.2.own_ref, f32[672,128]{1,0:T(8,128)S(1)} %collective-permute-done.6.pair_ref, f32[672,128]{1,0:T(8,128)S(1)} %roots.3.halo_ref, ...), custom_call_target="tpu_custom_call" | custom-call | tf_op jit(solution)/shard_map/update/pallas_call | solution.py:432
  (5 shorter events, 0.1 us)
Async XLA Ops:
  0.7 1.0 %copy-start = (bf16[32,8,8,128]{3,2,1,0:T(8,128)(2,1)S(1)}, bf16[32,8,8,128]{3,2,1,0:T(8,128)(2,1)}, u32[]{:S(2)}) copy-start(bf16[32,8,8,128]{3,2,1,0:T(8,128)(2,1)} %members_ref.3) | copy-start | bytes 1572868
  1.7 0.7 %copy-start.2 = (s32[1,1,1,8,256]{4,3,2,1,0:T(8,128)S(1)}, s32[1,1,1,8,256]{4,3,2,1,0:T(8,128)}, u32[]{:S(2)}) copy-start(s32[1,1,1,8,256]{4,3,2,1,0:T(8,128)} %param.12) | copy-start | bytes 24580
  2.4 0.7 %copy-start.3 = (f32[1,1,1,8,256]{4,3,2,1,0:T(8,128)S(1)}, f32[1,1,1,8,256]{4,3,2,1,0:T(8,128)}, u32[]{:S(2)}) copy-start(f32[1,1,1,8,256]{4,3,2,1,0:T(8,128)} %param.13) | copy-start | bytes 24580
  3.1 0.7 %copy-start.4 = (f32[1,1,1,256]{3,2,1,0:T(1,128)S(1)}, f32[1,1,1,256]{3,2,1,0:T(1,128)}, u32[]{:S(2)}) copy-start(f32[1,1,1,256]{3,2,1,0:T(1,128)} %param.9) | copy-start | bytes 3076
  3.8 0.7 %copy-start.5 = (f32[1,1,1,256]{3,2,1,0:T(1,128)S(1)}, f32[1,1,1,256]{3,2,1,0:T(1,128)}, u32[]{:S(2)}) copy-start(f32[1,1,1,256]{3,2,1,0:T(1,128)} %param.10) | copy-start | bytes 3076
  4.5 18.2 %copy-start.6 = (s32[2,128,64]{1,2,0:T(8,128)S(1)}, s32[2,128,64]{1,2,0:T(8,128)}, u32[]{:S(2)}) copy-start(s32[2,128,64]{1,2,0:T(8,128)} %param.14) | copy-start | bytes 196612
  4.5 18.3 %copy-start.7 = (f32[2,128,64]{1,2,0:T(8,128)S(1)}, f32[2,128,64]{1,2,0:T(8,128)}, u32[]{:S(2)}) copy-start(f32[2,128,64]{1,2,0:T(8,128)} %param.15) | copy-start | bytes 196612
  7.5 7.1 %collective-permute-start.2 = (f32[40,256]{1,0:T(8,128)S(1)}, f32[40,256]{1,0:T(8,128)S(1)}, u32[]{:S(2)}, u32[]{:S(2)}) collective-permute-start(f32[40,256]{1,0:T(8,128)S(1)} %observe.1), channel_id=1, source_target_pairs={{12,0},{0,4},{4,8},{8,12},{13,1},{1,5},{5,9},{9,13},{14,2},{2,6},{... | collective-permute-start | bytes 122888 | tf_op jit(solution)/shard_map/ppermute | solution.py:449
  10.6 5.4 %collective-permute-start.1 = (f32[40,256]{1,0:T(8,128)S(1)}, f32[40,256]{1,0:T(8,128)S(1)}, u32[]{:S(2)}, u32[]{:S(2)}) collective-permute-start(f32[40,256]{1,0:T(8,128)S(1)} %observe.1), channel_id=1, source_target_pairs={{8,0},{12,4},{0,8},{4,12},{9,1},{13,5},{1,9},{5,13},{10,2},{14,6},... | collective-permute-start | bytes 122888 | tf_op jit(solution)/shard_map/ppermute | solution.py:449
  13.1 4.0 %collective-permute-start = (f32[40,256]{1,0:T(8,128)S(1)}, f32[40,256]{1,0:T(8,128)S(1)}, u32[]{:S(2)}, u32[]{:S(2)}) collective-permute-start(f32[40,256]{1,0:T(8,128)S(1)} %observe.1), channel_id=1, source_target_pairs={{4,0},{8,4},{12,8},{0,12},{5,1},{9,5},{13,9},{1,13},{6,2},{10,6},{... | collective-permute-start | bytes 122888 | tf_op jit(solution)/shard_map/ppermute | solution.py:449
  17.2 5.4 %collective-permute-start.3 = (f32[4,40,256]{2,1,0:T(8,128)S(1)}, f32[4,40,256]{2,1,0:T(8,128)S(1)}, u32[]{:S(2)}, u32[]{:S(2)}) collective-permute-start(f32[4,40,256]{2,1,0:T(8,128)S(1)} %get-tuple-element.10), channel_id=1, source_target_pairs={{2,0},{0,2},{3,1},{1,3},{6,4},{4,6},{7,5},{5,7},{10,8},{8,10},{11,... | collective-permute-start | bytes 491528 | tf_op jit(solution)/shard_map/ppermute | solution.py:449
  22.6 12.2 %collective-permute-start.4 = (f32[8,40,256]{2,1,0:T(8,128)S(1)}, f32[8,40,256]{2,1,0:T(8,128)S(1)}, u32[]{:S(2)}, u32[]{:S(2)}) collective-permute-start(f32[8,40,256]{2,1,0:T(8,128)S(1)} %bitcast.17), channel_id=1, source_target_pairs={{0,1},{1,0},{2,3},{3,2},{4,5},{5,4},{6,7},{7,6},{8,9},{9,8},{10,11... | collective-permute-start | bytes 983048 | tf_op jit(solution)/shard_map/ppermute | solution.py:453
  22.9 6.1 %collective-permute-start.5 = (f32[128,128]{1,0:T(8,128)S(1)}, f32[128,128]{1,0:T(8,128)S(1)}, u32[]{:S(2)}, u32[]{:S(2)}) collective-permute-start(f32[128,128]{1,0:T(8,128)S(1)} %bitcast.26), channel_id=1, source_target_pairs={{0,4},{4,8},{8,12},{12,0},{1,13},{5,1},{9,5},{13,9},{2,6},{6,10},{... | collective-permute-start | bytes 196616 | tf_op jit(solution)/shard_map/ppermute | solution.py:475
  39.3 15.7 %copy-start.1 = (bf16[32,8,8,128]{3,2,1,0:T(8,128)(2,1)S(1)}, bf16[32,8,8,128]{3,2,1,0:T(8,128)(2,1)}, u32[]{:S(2)}) copy-start(bf16[32,8,8,128]{3,2,1,0:T(8,128)(2,1)} %members_ref.3) | copy-start | bytes 1572868
  52.8 1.7 %collective-permute-start.6 = (f32[672,128]{1,0:T(8,128)S(1)}, f32[672,128]{1,0:T(8,128)S(1)}, u32[]{:S(2)}, u32[]{:S(2)}) collective-permute-start(f32[672,128]{1,0:T(8,128)S(1)} %roots.2.own_ref), channel_id=1, source_target_pairs={{0,1},{1,0},{2,3},{3,2},{4,5},{5,4},{6,7},{7,6},{8,9},{9,8},{10,11... | collective-permute-start | bytes 1032200 | tf_op jit(solution)/shard_map/ppermute | solution.py:453
  52.9 2.1 %collective-permute-start.7 = (f32[672,128]{1,0:T(8,128)S(1)}, f32[672,128]{1,0:T(8,128)S(1)}, u32[]{:S(2)}, u32[]{:S(2)}) collective-permute-start(f32[672,128]{1,0:T(8,128)S(1)} %roots.3.halo_ref), channel_id=1, source_target_pairs={{0,1},{1,0},{2,3},{3,2},{4,5},{5,4},{6,7},{7,6},{8,9},{9,8},{10,11... | collective-permute-start | bytes 1032200 | tf_op jit(solution)/shard_map/ppermute | solution.py:453

commit v2 on v1

--- a/solution.py
+++ b/solution.py
@@ -18,6 +18,10 @@
 
 def params():
     return pltpu.CompilerParams(vmem_limit_bytes=VMEM_LIMIT)
+
+
+def micros(time):
+    return pl.CostEstimate(flops=int(time * 1e9), bytes_accessed=int(time * 3e6), transcendentals=0)
 
 
 def spread(ref, row):
@@ -33,7 +37,18 @@
     return base, at
 
 
-def observe_kernel(count_ref, members_ref, cell_ref, weight_ref, value_ref, rinv_ref, out_ref, wx, pick, part):
+def observe_kernel(
+    gz_ref, count_ref, members_in, cell_in, weight_in, value_in, rinv_in, ids_in, tapers_in,
+    out_ref, sent_ref, own_ref,
+    members_ref, cell_ref, weight_ref, value_ref, rinv_ref, ids_ref, tapers_ref, wx, pick, part, sems,
+):
+    ins = (cell_in, weight_in, members_in, value_in, rinv_in, ids_in, tapers_in)
+    here = (cell_ref, weight_ref, members_ref, value_ref, rinv_ref, ids_ref, tapers_ref)
+    copies = [pltpu.make_async_copy(src, dst, sems.at[n]) for n, (src, dst) in enumerate(zip(ins, here))]
+    for copy in copies:
+        copy.start()
+    copies[0].wait()
+    copies[1].wait()
     ens, levels, width_x, width_y = members_ref.shape
     slots = cell_ref.shape[1]
     sten = cell_ref.shape[0]
@@ -54,6 +69,7 @@
     y_iota = lax.broadcasted_iota(jnp.int32, (width_y, slots), 0)
     pick[:, :slots] = jnp.where(y_iota == low0, 1.0, 0.0).astype(BF16)
     pick[:, slots:] = jnp.where(y_iota == low0 + 1, 1.0, 0.0).astype(BF16)
+    copies[2].wait()
 
     def member(k, _):
         rows = members_ref[k].astype(F32).reshape(levels * width_x, width_y).astype(BF16)
@@ -82,57 +98,84 @@
     mean = jnp.sum(total, axis=0, keepdims=True) / ens
     for kb in range(ens // SUB):
         out_ref[kb * SUB : (kb + 1) * SUB, :] = groups[kb] - mean
+    for copy in copies[3:]:
+        copy.wait()
     live = lax.broadcasted_iota(jnp.int32, (1, slots), 1) < count_ref[0]
     innovation = value_ref[...] - mean
     rinv = jnp.where(live, rinv_ref[...], 0.0)
     row = lax.broadcasted_iota(jnp.int32, (SUB, slots), 0)
     out_ref[ens : ens + SUB, :] = jnp.where(row == 0, innovation, jnp.where(row == 1, rinv, 0.0))
-
-
-def observe(members, cell, weight, value, rinv, count):
+    sent_ref[: ens + SUB, :] = out_ref[...]
+    gz = gz_ref[0]
+    own_ref[...] = jnp.concatenate([ids_ref[gz].astype(F32), tapers_ref[gz]], axis=1)
+    other = jnp.concatenate([ids_ref[1 - gz].astype(F32), tapers_ref[1 - gz]], axis=1)
+    parts = slots // other.shape[1]
+    rows = other.shape[0] // parts
+    for q in range(parts):
+        lanes = slice(q * other.shape[1], (q + 1) * other.shape[1])
+        sent_ref[ens + SUB :, lanes] = other[q * rows : (q + 1) * rows]
+
+
+def observe(gz, count, members, cell, weight, value, rinv, ids, tapers):
     ens, levels, width_x, width_y = members.shape
     sten, slots = cell.shape
+    _, patches, mloc = ids.shape
     vmem = pl.BlockSpec(memory_space=pltpu.VMEM)
+    smem = pl.BlockSpec(memory_space=pltpu.SMEM)
+    extra = patches * 2 * mloc // slots
     return pl.pallas_call(
         observe_kernel,
-        out_shape=jax.ShapeDtypeStruct((ens + SUB, slots), F32),
-        in_specs=[pl.BlockSpec(memory_space=pltpu.SMEM)] + [vmem] * 5,
-        out_specs=vmem,
+        out_shape=(
+            jax.ShapeDtypeStruct((ens + SUB, slots), F32),
+            jax.ShapeDtypeStruct((ens + SUB + extra, slots), F32),
+            jax.ShapeDtypeStruct((patches, 2 * mloc), F32),
+        ),
+        in_specs=[smem, smem] + [pl.BlockSpec(memory_space=pl.ANY)] * 7,
+        out_specs=(vmem, vmem, vmem),
         scratch_shapes=[
+            pltpu.VMEM(members.shape, members.dtype),
+            pltpu.VMEM(cell.shape, cell.dtype),
+            pltpu.VMEM(weight.shape, F32),
+            pltpu.VMEM(value.shape, F32),
+            pltpu.VMEM(rinv.shape, F32),
+            pltpu.VMEM(ids.shape, ids.dtype),
+            pltpu.VMEM(tapers.shape, F32),
             pltpu.VMEM((2, levels * width_x, slots), F32),
             pltpu.VMEM((width_y, 2 * slots), BF16),
             pltpu.VMEM((slots // LANES, ens * SUB, LANES), F32),
+            pltpu.SemaphoreType.DMA((7,)),
         ],
         compiler_params=params(),
+        cost_estimate=micros(3),
         name="observe",
-    )(count, members, cell, weight, value, rinv)
-
-
-def taper_kernel(gz_ref, own_ref, halo_ref, high_ref, low_ref, code_s, slot_s, taper_s, *, n_x, n_y, slots):
-    patches, mloc = own_ref.shape[0], own_ref.shape[1] // 2
+    )(gz, count, members, cell, weight, value, rinv, ids, tapers)
+
+
+def taper_kernel(gz_ref, list_ref, high_ref, low_ref, list_s, code_s, slot_s, taper_s, *, shift, n_x, n_y, slots, mloc):
+    patches = high_ref.shape[1]
     batch = patches // SUB
     gz = gz_ref[0]
     n_buf = 2 * n_x * n_y
     lanes = SUB * mloc
-    for r, ref in enumerate((own_ref, halo_ref)):
-        shift = 0 if r == 0 else jnp.where(gz == 0, -1, 1)
-        pairs = [ref[pl.ds(q, batch, stride=SUB), :] for q in range(SUB)]
-        ids = jnp.concatenate([pair[:, :mloc] for pair in pairs], axis=1).astype(jnp.int32)
-        taper = jnp.concatenate([pair[:, mloc:] for pair in pairs], axis=1)
-        slot = jnp.bitwise_and(ids, slots - 1)
-        tile = lax.shift_right_logical(ids, slots.bit_length() - 1)
-        upper = (tile >= 9).astype(jnp.int32)
-        tile = tile - 9 * upper
-        a = (tile >= 3).astype(jnp.int32) + (tile >= 6).astype(jnp.int32)
-        b = tile - 3 * a
-        other = jnp.where(upper == gz, 0, 1)
-        x = lax.rem(a - 1 + shift + 2 * n_x, n_x)
-        y = lax.rem(b - 1 + n_y, n_y)
-        patch = lax.shift_right_logical(lax.broadcasted_iota(jnp.int32, ids.shape, 1), mloc.bit_length() - 1)
-        rows = pl.ds(r * batch, batch)
-        code_s[rows, :] = ((other * n_x + x) * n_y + y) * SUB + patch
-        slot_s[rows, :] = slot
-        taper_s[rows, :] = taper
+    span = list_ref.shape[0]
+    for n in range(patches // span):
+        list_s[n * span : (n + 1) * span, :] = list_ref[:, n * 2 * mloc : (n + 1) * 2 * mloc]
+    pairs = [list_s[pl.ds(q, batch, stride=SUB), :] for q in range(SUB)]
+    ids = jnp.concatenate([pair[:, :mloc] for pair in pairs], axis=1).astype(jnp.int32)
+    taper = jnp.concatenate([pair[:, mloc:] for pair in pairs], axis=1)
+    tile = lax.shift_right_logical(ids, slots.bit_length() - 1)
+    upper = (tile >= 9).astype(jnp.int32)
+    tile = tile - 9 * upper
+    a = (tile >= 3).astype(jnp.int32) + (tile >= 6).astype(jnp.int32)
+    b = tile - 3 * a
+    other = jnp.where(upper == gz, 0, 1)
+    x = jnp.where(gz == 0, a - 1, 1 - a) + shift
+    x = lax.rem(jnp.where(other == 0, x, -x) + 2 * n_x, n_x)
+    y = lax.rem(b - 1 + n_y, n_y)
+    patch = lax.shift_right_logical(lax.broadcasted_iota(jnp.int32, ids.shape, 1), mloc.bit_length() - 1)
+    code_s[...] = ((other * n_x + x) * n_y + y) * SUB + patch
+    slot_s[...] = jnp.bitwise_and(ids, slots - 1)
+    taper_s[...] = taper
 
     def dense(it):
         code = code_s[pl.ds(it, 1), :]
@@ -159,40 +202,41 @@
             low_ref[n, at, :] = (block - high.astype(F32)).astype(BF16)
         return 0
 
-    lax.fori_loop(0, batch, body, 0)
-
-
-def dense_tapers(gz, own, halo, n_x, n_y, slots):
-    patches, mloc = own.shape[0], own.shape[1] // 2
+    lax.fori_loop(0, batch // 2, body, 0)
+
+
+def dense_tapers(gz, lists, shift, patches, mloc, n_x, n_y, slots):
     vmem = pl.BlockSpec(memory_space=pltpu.VMEM)
     n_buf = 2 * n_x * n_y
-    shape = jax.ShapeDtypeStruct((n_buf, 2 * patches, slots), BF16)
+    shape = jax.ShapeDtypeStruct((n_buf, patches, slots), BF16)
     batch = patches // SUB
     return pl.pallas_call(
-        functools.partial(taper_kernel, n_x=n_x, n_y=n_y, slots=slots),
+        functools.partial(taper_kernel, shift=shift, n_x=n_x, n_y=n_y, slots=slots, mloc=mloc),
         out_shape=(shape, shape),
-        in_specs=[pl.BlockSpec(memory_space=pltpu.SMEM), vmem, vmem],
+        in_specs=[pl.BlockSpec(memory_space=pltpu.SMEM), vmem],
         out_specs=(vmem, vmem),
         scratch_shapes=[
-            pltpu.VMEM((2 * batch, SUB * mloc), jnp.int32),
-            pltpu.VMEM((2 * batch, SUB * mloc), jnp.int32),
-            pltpu.VMEM((2 * batch, SUB * mloc), F32),
+            pltpu.VMEM((patches, 2 * mloc), F32),
+            pltpu.VMEM((batch, SUB * mloc), jnp.int32),
+            pltpu.VMEM((batch, SUB * mloc), jnp.int32),
+            pltpu.VMEM((batch, SUB * mloc), F32),
         ],
         compiler_params=params(),
+        cost_estimate=micros(3),
         name="dense_tapers",
-    )(gz, own, halo)
-
-
-def gram_kernel(*refs, ens, n_stack):
-    stacks = refs[:n_stack]
-    high_ref, low_ref, out_ref, z_s, zr_s = refs[n_stack:]
+    )(gz, lists)
+
+
+def gram_kernel(*refs, ens, n_parts, first_buf, carry):
+    refs = list(refs)
+    before = refs.pop(0) if carry else None
+    stacks = refs[:n_parts]
+    own_high, own_low, halo_high, halo_low, out_ref, z_s, zr_s = refs[n_parts:]
     nb = ens // SUB
-    slots = stacks[0].shape[2]
     base, tri = block_base(ens)
     rows = tri + ens
     nt = (((1,), (1,)), ((), ()))
-    first = True
-    n = 0
+    n = first_buf
     for stack in stacks:
         for t in range(stack.shape[0]):
             ob = stack[t, :ens, :]
@@ -211,28 +255,36 @@
             high = part.astype(BF16)
             z_s[tri:rows, :] = high
             z_s[rows + tri : 2 * rows, :] = (part - high.astype(F32)).astype(BF16)
-            got = lax.dot_general(z_s[...], high_ref[n], nt, preferred_element_type=F32)
-            more = lax.dot_general(z_s[:rows, :], low_ref[n], nt, preferred_element_type=F32)
+            right = jnp.concatenate([own_high[n], halo_high[n]], axis=0)
+            got = lax.dot_general(z_s[...], right, nt, preferred_element_type=F32)
+            right = jnp.concatenate([own_low[n], halo_low[n]], axis=0)
+            more = lax.dot_general(z_s[:rows, :], right, nt, preferred_element_type=F32)
             total = got[:rows] + (got[rows:] + more)
-            out_ref[...] = total if first else out_ref[...] + total
-            first = False
+            if n > first_buf:
+                total = out_ref[...] + total
+            elif carry:
+                total = before[...] + total
+            out_ref[...] = total
             n += 1
 
 
-def grams(stacks, high, low, ens):
+def grams(stacks, tapers, ens, first_buf, before=None):
     vmem = pl.BlockSpec(memory_space=pltpu.VMEM)
     _, tri = block_base(ens)
     rows = tri + ens
-    patches, slots = high.shape[1:]
+    _, patches, slots = tapers[0].shape
+    carry = before is not None
+    args = ((before,) if carry else ()) + tuple(stacks) + tuple(tapers)
     return pl.pallas_call(
-        functools.partial(gram_kernel, ens=ens, n_stack=len(stacks)),
-        out_shape=jax.ShapeDtypeStruct((rows, patches), F32),
-        in_specs=[vmem] * (len(stacks) + 2),
+        functools.partial(gram_kernel, ens=ens, n_parts=len(stacks), first_buf=first_buf, carry=carry),
+        out_shape=jax.ShapeDtypeStruct((rows, 2 * patches), F32),
+        in_specs=[vmem] * len(args),
         out_specs=vmem,
         scratch_shapes=[pltpu.VMEM((2 * rows, slots), BF16), pltpu.VMEM((ens, slots), F32)],
         compiler_params=params(),
+        cost_estimate=micros(2),
         name="grams",
-    )(*stacks, high, low)
+    )(*args)
 
 
 def product(ens, a, b, dests, epilogue):
@@ -353,6 +405,7 @@
         out_specs=pl.BlockSpec((rows, LANES), lambda g: (0, 0)),
         scratch_shapes=[square] * 4 + [pltpu.VMEM((ens * ens + 2 * ens, LANES), F32)],
         compiler_params=params(),
+        cost_estimate=micros(7),
         name="roots",
     )(gram)
 
@@ -440,6 +493,7 @@
             pltpu.VMEM((ens * ens,) + tile, F32),
         ],
         compiler_params=params(),
+        cost_estimate=micros(4),
         name="update",
     )(gz, members, own, pair, halo, far)
 
@@ -449,12 +503,23 @@
     return lax.ppermute(x, axis, [((i + shift) % size, i) for i in range(size)])
 
 
+def turned(x, shift):
+    size = lax.axis_size("gx")
+    pairs = [(2 * ((i + shift) % size), 2 * i) for i in range(size)]
+    pairs += [(2 * ((i - shift) % size) + 1, 2 * i + 1) for i in range(size)]
+    return lax.ppermute(x, ("gx", "gz"), pairs)
+
+
 def swapped(x):
     return lax.ppermute(x, "gz", [(0, 1), (1, 0)])
 
 
 def signed(index, count):
     return index if index <= count // 2 else index - count
+
+
+def after(x, *others):
+    return lax.optimization_barrier((x,) + others)[0]
 
 
 def per_device(
@@ -462,40 +527,43 @@
 ):
     ens = members.shape[0]
     slots = obs_value.shape[-1]
+    _, patches, mloc = patch_list.shape
     size_x, size_y = lax.axis_size("gx"), lax.axis_size("gy")
     n_x, n_y = min(size_x, 5), min(size_y, 3)
-    gz = lax.axis_index("gz")
-    gz_arg = gz.reshape(1).astype(jnp.int32)
-
-    lists = jnp.concatenate([patch_list.astype(F32), patch_taper], axis=-1)
-    own_list = lax.dynamic_index_in_dim(lists, gz, 0, keepdims=False)
-    sent_list = lax.dynamic_index_in_dim(lists, 1 - gz, 0, keepdims=False)
-    turn = [(2 * i, 2 * ((i + 1) % size_x)) for i in range(size_x)]
-    turn += [(2 * i + 1, 2 * ((i - 1) % size_x) + 1) for i in range(size_x)]
-    halo_list = lax.ppermute(sent_list, ("gx", "gz"), turn)
-
-    packet = observe(
+    gz = lax.axis_index("gz").reshape(1).astype(jnp.int32)
+    packet, sent, own_list = observe(
+        gz,
+        obs_count.reshape(1),
         members,
         stencil_cell.reshape(-1, slots),
         stencil_weight.reshape(-1, slots),
         obs_value.reshape(1, slots),
         obs_rinv.reshape(1, slots),
-        obs_count.reshape(1),
+        patch_list,
+        patch_taper,
     )
-    high, low = dense_tapers(gz_arg, own_list, halo_list, n_x, n_y, slots)
-
-    along = [packet] + [shifted(packet, "gx", signed(x, n_x)) for x in range(1, n_x)]
-    along = jnp.stack(along, axis=0)
+    rows = ens + SUB
+    along = {x: turned(packet, signed(x, n_x)) for x in range(1, n_x - 1)}
+    halo = turned(sent, -1)
+    along[n_x - 1] = halo[:rows]
+    along[0] = packet
+    halo_list = halo[rows:]
+    own_tapers = dense_tapers(gz, own_list, 0, patches, mloc, n_x, n_y, slots)
+    along = jnp.stack([along[x] for x in range(n_x)], axis=0)
+    along = after(along, *own_tapers)
     across = [along] + [shifted(along, "gy", signed(y, n_y)) for y in range(1, n_y)]
-    here = jnp.stack(across, axis=1).reshape(n_x * n_y, ens + SUB, slots)
+    halo_tapers = dense_tapers(gz, halo_list, -1, patches, mloc, n_x, n_y, slots)
+    here = jnp.stack(across, axis=1).reshape(n_x * n_y, rows, slots)
+    here = after(here, *halo_tapers)
     there = swapped(here)
-
-    gram = grams((here, there), high, low, ens)
+    tapers = own_tapers + halo_tapers
+    gram = grams((here,), tapers, ens, 0)
+    gram = grams((there,), tapers, ens, n_x * n_y, gram)
     own = roots(gram, 0, ens)
     pair = swapped(own)
-    halo = roots(gram, 1, ens)
+    halo = roots(after(gram, own), 1, ens)
     far = swapped(halo)
-    return update(gz_arg, members, own, pair, halo, far)
+    return update(gz, members, own, pair, halo, far)
 
 
 def solution(mesh):

time: 59.8 us -> 50.3 us (0.84)
  waiting for transfers between devices: 13.7 us -> 5.43 us
  Pallas kernels: 31.3 us -> 32.6 us
  starting transfers between devices: 9.6 us -> 8.39 us
  local copies, waits for them, and re-layouts: 4 us -> 2.84 us
    ppermute x4 -> x1, starting transfers between devices: 8.58 us -> 1.56 us  [shifted(): return lax.ppermute(x, axis, [((i + shift) % size, i) for i in range(size)])]
    ppermute x1 -> x3, starting transfers between devices: 0.38 us -> 6.12 us  [turned(): return lax.ppermute(x, ('gx', 'gz'), pairs)]
    ppermute x4 -> x1, waiting for transfers between devices: 6.47 us -> 0.86 us  [shifted(): return lax.ppermute(x, axis, [((i + shift) % size, i) for i in range(size)])]
    ppermute x1 -> x3, waiting for transfers between devices: 5.64 us -> 2.87 us  [turned(): return lax.ppermute(x, ('gx', 'gz'), pairs)]
    pallas_call x3 -> x5, Pallas kernels: 13.4 us -> 14.5 us  [the longest x2 5.9 us: dense_tapers(): pl.pallas_call(functools.partial(taper_kernel, shift=shift, n_x=n_x, n_y=...]
    unnamed x16, local copies, waits for them, and re-layouts: 3.8 us -> 2.81 us
  transfers between devices with their start and end apart: 8 -> 7, of which waited for: 7 -> 4; matrix products, arithmetic and copies ran while one was open for 0% -> 0% of each run, Pallas kernels for 10% -> 17%
where the time goes in v2:
time: 50.3 us; the launch traced here: 50.1 us
  Pallas kernels  32.6 us (65%)
  starting transfers between devices  8.39 us (17%)
  waiting for transfers between devices  5.43 us (11%)
  local copies, waits for them, and re-layouts  2.84 us (6%)
  between operations  0.83 us (2%)
    pallas_call x2, Pallas kernels, roots(): pl.pallas_call(functools.partial(root_kernel, ens=ens), out_shape=jax.Sha...  13.6 us
    ppermute x3, starting transfers between devices, turned(): return lax.ppermute(x, ('gx', 'gz'), pairs)  6.12 us
    pallas_call x2, Pallas kernels, dense_tapers(): pl.pallas_call(functools.partial(taper_kernel, shift=shift, n_x=n_x, n_y=...  5.9 us
    pallas_call x2, Pallas kernels, grams(): pl.pallas_call(functools.partial(gram_kernel, ens=ens, n_parts=len(stacks...  4.99 us
    pallas_call x1, Pallas kernels, update(): pl.pallas_call(update_kernel, out_shape=jax.ShapeDtypeStruct(members.shap...  4.48 us
    pallas_call x1, Pallas kernels, observe(): pl.pallas_call(observe_kernel, out_shape=(jax.ShapeDtypeStruct((ens + SUB...  3.57 us
    ppermute x3, waiting for transfers between devices, turned(): return lax.ppermute(x, ('gx', 'gz'), pairs)  2.87 us
    unnamed x16, local copies, waits for them, and re-layouts  2.81 us
  transfers between devices with their start and end apart: 7, of which 4 were waited for; matrix products, arithmetic and copies ran while one was open for 0% of the time, Pallas kernels for 17%

profile of v2, /device:TPU:0, one launch (start us, length us, event | category | flops | bytes accessed | tf_op | source)
XLA Modules:
  0.0 50.1 jit_solution(10235100253725027977)
XLA Ops:
  0.7 0.0 copy-start.6
  0.7 1.0 %copy.9.ids_in = s32[2,128,64]{2,1,0:T(8,128)S(1)} copy(s32[2,128,64]{1,2,0:T(8,128)} %param.14) | data formatting | bytes 131072 | tf_op args[6]
  1.6 0.0 copy-done.6
  1.6 0.0 copy-start.3
  1.7 0.1 copy.10.tapers_in
  1.8 0.0 copy-start.2
  1.8 0.0 copy-start.5
  1.8 0.0 copy-start.4
  1.8 0.5 %copy-done.3 = f32[1,1,1,8,256]{4,3,2,1,0:T(8,128)S(1)} copy-done((f32[1,1,1,8,256]{4,3,2,1,0:T(8,128)S(1)}, f32[1,1,1,8,256]{4,3,2,1,0:T(8,128)}, u32[]{:S(2)}) %copy-start.3) | copy-done | bytes 8216
  2.3 0.1 copy-done.2
  2.5 0.0 copy-done.5
  2.5 0.0 copy-done.4
  2.5 0.0 copy-start
  2.5 1.0 %copy-done = bf16[32,8,8,128]{3,2,1,0:T(8,128)(2,1)S(1)} copy-done((bf16[32,8,8,128]{3,2,1,0:T(8,128)(2,1)S(1)}, bf16[32,8,8,128]{3,2,1,0:T(8,128)(2,1)}, u32[]{:S(2)}) %copy-start) | copy-done | bytes 524312
  3.5 3.6 %observe.1 = (f32[40,256]{1,0:T(8,128)S(1)}, f32[104,256]{1,0:T(8,128)S(1)}, f32[128,128]{1,0:T(8,128)S(1)}) custom-call(s32[1]{0:T(128)} %bitcast.gz_ref, s32[1]{0:T(128)} %bitcast.14.count_ref, bf16[32,8,8,128]{3,2,1,0:T(8,128)(2,1)S(1)} %copy-done, s32[8,256]{1,0:T(8,128)S(1)} %bitcast.18, f32[8,256]{1,0:T(8,128)S(1)} %bitcast.19, f32[1,256]{1,0:T(1,128)S(1)} %bitcast.20, ...), custom_call_target="tpu_custom_call" | custom-call | flops 3000000000 | bytes 9000000 | tf_op jit(solution)/shard_map/observe/pallas_call | solution.py:126
  7.1 4.1 %collective-permute-start.1 = (f32[40,256]{1,0:T(8,128)S(1)}, f32[40,256]{1,0:T(8,128)S(1)}, u32[]{:S(2)}, u32[]{:S(2)}) collective-permute-start(f32[40,256]{1,0:T(8,128)S(1)} %get-tuple-element.15), channel_id=1, source_target_pairs={{8,0},{12,4},{0,8},{4,12},{9,1},{13,5},{1,9},{5,13},{10,2},{14,6},... | collective-permute-start | bytes 122888 | tf_op jit(solution)/shard_map/ppermute | solution.py:510
  11.2 1.3 %collective-permute-start = (f32[40,256]{1,0:T(8,128)S(1)}, f32[40,256]{1,0:T(8,128)S(1)}, u32[]{:S(2)}, u32[]{:S(2)}) collective-permute-start(f32[40,256]{1,0:T(8,128)S(1)} %get-tuple-element.15), channel_id=1, source_target_pairs={{4,0},{8,4},{12,8},{0,12},{13,1},{1,5},{5,9},{9,13},{6,2},{10,6},{... | collective-permute-start | bytes 122888 | tf_op jit(solution)/shard_map/ppermute | solution.py:510
  12.5 0.7 %collective-permute-start.2 = (f32[104,256]{1,0:T(8,128)S(1)}, f32[104,256]{1,0:T(8,128)S(1)}, u32[]{:S(2)}, u32[]{:S(2)}) collective-permute-start(f32[104,256]{1,0:T(8,128)S(1)} %get-tuple-element.16), channel_id=1, source_target_pairs={{12,0},{0,4},{4,8},{8,12},{5,1},{9,5},{13,9},{1,13},{14,2},{2,6},{... | collective-permute-start | bytes 319496 | tf_op jit(solution)/shard_map/ppermute | solution.py:510
  13.2 2.9 %dense_tapers.2 = (bf16[16,128,256]{2,1,0:T(8,128)(2,1)S(1)}, bf16[16,128,256]{2,1,0:T(8,128)(2,1)S(1)}) custom-call(s32[1]{0:T(128)} %bitcast.gz_ref, f32[128,128]{1,0:T(8,128)S(1)} %get-tuple-element.17.list_ref), custom_call_target="tpu_custom_call" | custom-call | flops 3000000000 | bytes 9000000 | tf_op jit(solution)/shard_map/dense_tapers/pallas_call | solution.py:213
  16.2 2.9 %collective-permute-done.2 = f32[104,256]{1,0:T(8,128)S(1)} collective-permute-done((f32[104,256]{1,0:T(8,128)S(1)}, f32[104,256]{1,0:T(8,128)S(1)}, u32[]{:S(2)}, u32[]{:S(2)}) %collective-permute-start.2) | collective-permute-done | bytes 106528 | tf_op jit(solution)/shard_map/ppermute | solution.py:510
  19.1 0.0 collective-permute-done.1
  19.1 0.0 collective-permute-done
  19.1 1.6 %collective-permute-start.3 = (f32[4,40,256]{2,1,0:T(8,128)S(1)}, f32[4,40,256]{2,1,0:T(8,128)S(1)}, u32[]{:S(2)}, u32[]{:S(2)}) collective-permute-start(f32[4,40,256]{2,1,0:T(8,128)S(1)} %pad_maximum_fusion.1), channel_id=1, source_target_pairs={{2,0},{0,2},{3,1},{1,3},{6,4},{4,6},{7,5},{5,7},{10,8},{8,10},{11,... | collective-permute-start | bytes 491528 | tf_op jit(solution)/shard_map/ppermute | solution.py:503
  20.6 2.9 %dense_tapers.3 = (bf16[16,128,256]{2,1,0:T(8,128)(2,1)S(1)}, bf16[16,128,256]{2,1,0:T(8,128)(2,1)S(1)}) custom-call(s32[1]{0:T(128)} %bitcast.gz_ref, f32[64,256]{1,0:T(8,128)S(1)} %slice.9.list_ref), custom_call_target="tpu_custom_call" | custom-call | flops 3000000000 | bytes 9000000 | tf_op jit(solution)/shard_map/dense_tapers/pallas_call | solution.py:213
  23.6 0.9 %collective-permute-done.3 = f32[4,40,256]{2,1,0:T(8,128)S(1)} collective-permute-done((f32[4,40,256]{2,1,0:T(8,128)S(1)}, f32[4,40,256]{2,1,0:T(8,128)S(1)}, u32[]{:S(2)}, u32[]{:S(2)}) %collective-permute-start.3) | collective-permute-done | bytes 163872 | tf_op jit(solution)/shard_map/ppermute | solution.py:503
  24.5 0.1 collective-permute-start.4
  24.6 2.5 %grams.2.refs_0_ = f32[672,256]{1,0:T(8,128)S(1)} custom-call(f32[8,40,256]{2,1,0:T(8,128)S(1)} %bitcast.16, bf16[16,128,256]{2,1,0:T(8,128)(2,1)S(1)} %get-tuple-element.18.refs_1_.refs_2_, bf16[16,128,256]{2,1,0:T(8,128)(2,1)S(1)} %get-tuple-element.19.refs_2_.refs_3_, bf16[16,128,256]{2,1,0:T(8,128)(2,1)S(1)} %get-tuple-element.21.refs_3_.refs_4_, ...), custom_call_target="tpu_custom_call" | custom-call | flops 2000000000 | bytes 6000000 | tf_op jit(solution)/shard_map/grams/pallas_call | solution.py:278
  27.1 0.0 collective-permute-done.4.refs_1_
  27.1 2.5 %grams.3.gram_ref = f32[672,256]{1,0:T(8,128)S(1)} custom-call(f32[672,256]{1,0:T(8,128)S(1)} %grams.2.refs_0_, f32[8,40,256]{2,1,0:T(8,128)S(1)} %collective-permute-done.4.refs_1_, bf16[16,128,256]{2,1,0:T(8,128)(2,1)S(1)} %get-tuple-element.18.refs_1_.refs_2_, bf16[16,128,256]{2,1,0:T(8,128)(2,1)S(1)} %get-tuple-element.19.refs_2_.refs_3_, ...), custom_call_target="tpu_custom_call" | custom-call | flops 2000000000 | bytes 6000000 | tf_op jit(solution)/shard_map/grams/pallas_call | solution.py:278
  29.6 6.7 %roots.2.own_ref = f32[672,128]{1,0:T(8,128)S(1)} custom-call(f32[672,256]{1,0:T(8,128)S(1)} %grams.3.gram_ref), custom_call_target="tpu_custom_call" | custom-call | flops 7000000000 | bytes 21000000 | tf_op jit(solution)/shard_map/roots/pallas_call | solution.py:400
  36.3 0.0 copy-start.1
  36.4 6.9 %roots.3.halo_ref = f32[672,128]{1,0:T(8,128)S(1)} custom-call(f32[672,256]{1,0:T(8,128)S(1)} %grams.3.gram_ref), custom_call_target="tpu_custom_call" | custom-call | flops 7000000000 | bytes 21000000 | tf_op jit(solution)/shard_map/roots/pallas_call | solution.py:400
  43.3 0.6 %collective-permute-start.6 = (f32[672,128]{1,0:T(8,128)S(1)}, f32[672,128]{1,0:T(8,128)S(1)}, u32[]{:S(2)}, u32[]{:S(2)}) collective-permute-start(f32[672,128]{1,0:T(8,128)S(1)} %roots.3.halo_ref), channel_id=1, source_target_pairs={{0,1},{1,0},{2,3},{3,2},{4,5},{5,4},{6,7},{7,6},{8,9},{9,8},{10,11... | collective-permute-start | bytes 1032200 | tf_op jit(solution)/shard_map/ppermute | solution.py:514
  43.8 0.1 collective-permute-start.5
  43.9 1.2 %collective-permute-done.6.far_ref = f32[672,128]{1,0:T(8,128)S(1)} collective-permute-done((f32[672,128]{1,0:T(8,128)S(1)}, f32[672,128]{1,0:T(8,128)S(1)}, u32[]{:S(2)}, u32[]{:S(2)}) %collective-permute-start.6) | collective-permute-done | bytes 344096 | tf_op jit(solution)/shard_map/ppermute | solution.py:514
  45.1 0.5 collective-permute-done.5.pair_ref
  45.6 0.0 copy-done.1
  45.6 4.5 %update.1 = bf16[32,8,8,128]{3,2,1,0:T(8,128)(2,1)} custom-call(s32[1]{0:T(128)} %bitcast.gz_ref, bf16[32,8,8,128]{3,2,1,0:T(8,128)(2,1)S(1)} %copy-done.1, f32[672,128]{1,0:T(8,128)S(1)} %roots.2.own_ref, f32[672,128]{1,0:T(8,128)S(1)} %collective-permute-done.5.pair_ref, f32[672,128]{1,0:T(8,128)S(1)} %roots.3.halo_ref, ...), custom_call_target="tpu_custom_call" | custom-call | flops 4000000000 | bytes 12000000 | tf_op jit(solution)/shard_map/update/pallas_call | solution.py:485
  (5 shorter events, 0.1 us)
Async XLA Ops:
  0.7 1.0 %copy-start.6 = (f32[2,128,64]{1,2,0:T(8,128)S(1)}, f32[2,128,64]{1,2,0:T(8,128)}, u32[]{:S(2)}) copy-start(f32[2,128,64]{1,2,0:T(8,128)} %param.15) | copy-start | bytes 196612
  1.6 0.7 %copy-start.3 = (f32[1,1,1,8,256]{4,3,2,1,0:T(8,128)S(1)}, f32[1,1,1,8,256]{4,3,2,1,0:T(8,128)}, u32[]{:S(2)}) copy-start(f32[1,1,1,8,256]{4,3,2,1,0:T(8,128)} %param.13) | copy-start | bytes 24580
  1.8 0.7 %copy-start.2 = (s32[1,1,1,8,256]{4,3,2,1,0:T(8,128)S(1)}, s32[1,1,1,8,256]{4,3,2,1,0:T(8,128)}, u32[]{:S(2)}) copy-start(s32[1,1,1,8,256]{4,3,2,1,0:T(8,128)} %param.12) | copy-start | bytes 24580
  1.8 0.7 %copy-start.5 = (f32[1,1,1,256]{3,2,1,0:T(1,128)S(1)}, f32[1,1,1,256]{3,2,1,0:T(1,128)}, u32[]{:S(2)}) copy-start(f32[1,1,1,256]{3,2,1,0:T(1,128)} %param.10) | copy-start | bytes 3076
  1.8 0.7 %copy-start.4 = (f32[1,1,1,256]{3,2,1,0:T(1,128)S(1)}, f32[1,1,1,256]{3,2,1,0:T(1,128)}, u32[]{:S(2)}) copy-start(f32[1,1,1,256]{3,2,1,0:T(1,128)} %param.9) | copy-start | bytes 3076
  2.5 1.0 %copy-start = (bf16[32,8,8,128]{3,2,1,0:T(8,128)(2,1)S(1)}, bf16[32,8,8,128]{3,2,1,0:T(8,128)(2,1)}, u32[]{:S(2)}) copy-start(bf16[32,8,8,128]{3,2,1,0:T(8,128)(2,1)} %members_ref.1) | copy-start | bytes 1572868
  7.1 12.0 %collective-permute-start.1 = (f32[40,256]{1,0:T(8,128)S(1)}, f32[40,256]{1,0:T(8,128)S(1)}, u32[]{:S(2)}, u32[]{:S(2)}) collective-permute-start(f32[40,256]{1,0:T(8,128)S(1)} %get-tuple-element.15), channel_id=1, source_target_pairs={{8,0},{12,4},{0,8},{4,12},{9,1},{13,5},{1,9},{5,13},{10,2},{14,6},... | collective-permute-start | bytes 122888 | tf_op jit(solution)/shard_map/ppermute | solution.py:510
  11.2 7.9 %collective-permute-start = (f32[40,256]{1,0:T(8,128)S(1)}, f32[40,256]{1,0:T(8,128)S(1)}, u32[]{:S(2)}, u32[]{:S(2)}) collective-permute-start(f32[40,256]{1,0:T(8,128)S(1)} %get-tuple-element.15), channel_id=1, source_target_pairs={{4,0},{8,4},{12,8},{0,12},{13,1},{1,5},{5,9},{9,13},{6,2},{10,6},{... | collective-permute-start | bytes 122888 | tf_op jit(solution)/shard_map/ppermute | solution.py:510
  12.5 6.5 %collective-permute-start.2 = (f32[104,256]{1,0:T(8,128)S(1)}, f32[104,256]{1,0:T(8,128)S(1)}, u32[]{:S(2)}, u32[]{:S(2)}) collective-permute-start(f32[104,256]{1,0:T(8,128)S(1)} %get-tuple-element.16), channel_id=1, source_target_pairs={{12,0},{0,4},{4,8},{8,12},{5,1},{9,5},{13,9},{1,13},{14,2},{2,6},{... | collective-permute-start | bytes 319496 | tf_op jit(solution)/shard_map/ppermute | solution.py:510
  19.1 5.4 %collective-permute-start.3 = (f32[4,40,256]{2,1,0:T(8,128)S(1)}, f32[4,40,256]{2,1,0:T(8,128)S(1)}, u32[]{:S(2)}, u32[]{:S(2)}) collective-permute-start(f32[4,40,256]{2,1,0:T(8,128)S(1)} %pad_maximum_fusion.1), channel_id=1, source_target_pairs={{2,0},{0,2},{3,1},{1,3},{6,4},{4,6},{7,5},{5,7},{10,8},{8,10},{11,... | collective-permute-start | bytes 491528 | tf_op jit(solution)/shard_map/ppermute | solution.py:503
  24.5 2.6 %collective-permute-start.4 = (f32[8,40,256]{2,1,0:T(8,128)S(1)}, f32[8,40,256]{2,1,0:T(8,128)S(1)}, u32[]{:S(2)}, u32[]{:S(2)}) collective-permute-start(f32[8,40,256]{2,1,0:T(8,128)S(1)} %bitcast.15), channel_id=1, source_target_pairs={{0,1},{1,0},{2,3},{3,2},{4,5},{5,4},{6,7},{7,6},{8,9},{9,8},{10,11... | collective-permute-start | bytes 983048 | tf_op jit(solution)/shard_map/ppermute | solution.py:514
  36.3 9.2 %copy-start.1 = (bf16[32,8,8,128]{3,2,1,0:T(8,128)(2,1)S(1)}, bf16[32,8,8,128]{3,2,1,0:T(8,128)(2,1)}, u32[]{:S(2)}) copy-start(bf16[32,8,8,128]{3,2,1,0:T(8,128)(2,1)} %members_ref.1) | copy-start | bytes 1572868
  43.3 1.8 %collective-permute-start.6 = (f32[672,128]{1,0:T(8,128)S(1)}, f32[672,128]{1,0:T(8,128)S(1)}, u32[]{:S(2)}, u32[]{:S(2)}) collective-permute-start(f32[672,128]{1,0:T(8,128)S(1)} %roots.3.halo_ref), channel_id=1, source_target_pairs={{0,1},{1,0},{2,3},{3,2},{4,5},{5,4},{6,7},{7,6},{8,9},{9,8},{10,11... | collective-permute-start | bytes 1032200 | tf_op jit(solution)/shard_map/ppermute | solution.py:514
  43.8 1.8 %collective-permute-start.5 = (f32[672,128]{1,0:T(8,128)S(1)}, f32[672,128]{1,0:T(8,128)S(1)}, u32[]{:S(2)}, u32[]{:S(2)}) collective-permute-start(f32[672,128]{1,0:T(8,128)S(1)} %roots.2.own_ref), channel_id=1, source_target_pairs={{0,1},{1,0},{2,3},{3,2},{4,5},{5,4},{6,7},{7,6},{8,9},{9,8},{10,11... | collective-permute-start | bytes 1032200 | tf_op jit(solution)/shard_map/ppermute | solution.py:514

commit v3 on v2

--- a/solution.py
+++ b/solution.py
@@ -14,10 +14,11 @@
 LANES = 128
 SUB = 8
 VMEM_LIMIT = 40 << 20
-
-
-def params():
-    return pltpu.CompilerParams(vmem_limit_bytes=VMEM_LIMIT)
+WHOLE_VMEM = (64 << 20) - (256 << 10)
+
+
+def params(limit=VMEM_LIMIT):
+    return pltpu.CompilerParams(vmem_limit_bytes=limit)
 
 
 def micros(time):
@@ -82,7 +83,7 @@
             part[half, pl.ds(pl.multiple_of(k * SUB, SUB), SUB), :] = total[:, half * LANES : (half + 1) * LANES]
         return 0
 
-    lax.fori_loop(0, ens, member, 0, unroll=2)
+    lax.fori_loop(0, ens, member, 0, unroll=8)
     groups = []
     for kb in range(ens // SUB):
         halves = []
@@ -105,32 +106,25 @@
     rinv = jnp.where(live, rinv_ref[...], 0.0)
     row = lax.broadcasted_iota(jnp.int32, (SUB, slots), 0)
     out_ref[ens : ens + SUB, :] = jnp.where(row == 0, innovation, jnp.where(row == 1, rinv, 0.0))
-    sent_ref[: ens + SUB, :] = out_ref[...]
     gz = gz_ref[0]
-    own_ref[...] = jnp.concatenate([ids_ref[gz].astype(F32), tapers_ref[gz]], axis=1)
-    other = jnp.concatenate([ids_ref[1 - gz].astype(F32), tapers_ref[1 - gz]], axis=1)
-    parts = slots // other.shape[1]
-    rows = other.shape[0] // parts
-    for q in range(parts):
-        lanes = slice(q * other.shape[1], (q + 1) * other.shape[1])
-        sent_ref[ens + SUB :, lanes] = other[q * rows : (q + 1) * rows]
+    own_ref[...] = jnp.concatenate([ids_ref[gz].astype(F32), tapers_ref[gz]], axis=0).T
+    sent_ref[...] = jnp.concatenate([ids_ref[1 - gz].astype(F32), tapers_ref[1 - gz]], axis=0).T
 
 
 def observe(gz, count, members, cell, weight, value, rinv, ids, tapers):
     ens, levels, width_x, width_y = members.shape
     sten, slots = cell.shape
-    _, patches, mloc = ids.shape
+    _, mloc, patches = ids.shape
     vmem = pl.BlockSpec(memory_space=pltpu.VMEM)
     smem = pl.BlockSpec(memory_space=pltpu.SMEM)
-    extra = patches * 2 * mloc // slots
     return pl.pallas_call(
         observe_kernel,
         out_shape=(
             jax.ShapeDtypeStruct((ens + SUB, slots), F32),
-            jax.ShapeDtypeStruct((ens + SUB + extra, slots), F32),
+            jax.ShapeDtypeStruct((patches, 2 * mloc), F32),
             jax.ShapeDtypeStruct((patches, 2 * mloc), F32),
         ),
-        in_specs=[smem, smem] + [pl.BlockSpec(memory_space=pl.ANY)] * 7,
+        in_specs=[smem, smem] + [pl.BlockSpec(memory_space=pltpu.HBM)] * 7,
         out_specs=(vmem, vmem, vmem),
         scratch_shapes=[
             pltpu.VMEM(members.shape, members.dtype),
@@ -145,22 +139,19 @@
             pltpu.VMEM((slots // LANES, ens * SUB, LANES), F32),
             pltpu.SemaphoreType.DMA((7,)),
         ],
-        compiler_params=params(),
+        compiler_params=params(WHOLE_VMEM),
         cost_estimate=micros(3),
         name="observe",
     )(gz, count, members, cell, weight, value, rinv, ids, tapers)
 
 
-def taper_kernel(gz_ref, list_ref, high_ref, low_ref, list_s, code_s, slot_s, taper_s, *, shift, n_x, n_y, slots, mloc):
+def taper_kernel(gz_ref, list_ref, high_ref, low_ref, code_s, slot_s, taper_s, *, shift, n_x, n_y, slots, mloc):
     patches = high_ref.shape[1]
     batch = patches // SUB
     gz = gz_ref[0]
     n_buf = 2 * n_x * n_y
     lanes = SUB * mloc
-    span = list_ref.shape[0]
-    for n in range(patches // span):
-        list_s[n * span : (n + 1) * span, :] = list_ref[:, n * 2 * mloc : (n + 1) * 2 * mloc]
-    pairs = [list_s[pl.ds(q, batch, stride=SUB), :] for q in range(SUB)]
+    pairs = [list_ref[pl.ds(q, batch, stride=SUB), :] for q in range(SUB)]
     ids = jnp.concatenate([pair[:, :mloc] for pair in pairs], axis=1).astype(jnp.int32)
     taper = jnp.concatenate([pair[:, mloc:] for pair in pairs], axis=1)
     tile = lax.shift_right_logical(ids, slots.bit_length() - 1)
@@ -173,20 +164,22 @@
     x = lax.rem(jnp.where(other == 0, x, -x) + 2 * n_x, n_x)
     y = lax.rem(b - 1 + n_y, n_y)
     patch = lax.shift_right_logical(lax.broadcasted_iota(jnp.int32, ids.shape, 1), mloc.bit_length() - 1)
-    code_s[...] = ((other * n_x + x) * n_y + y) * SUB + patch
-    slot_s[...] = jnp.bitwise_and(ids, slots - 1)
+    code_s[...] = (((other * n_y + y) * n_x + x) * SUB + patch).astype(F32)
+    slot_s[...] = jnp.bitwise_and(ids, slots - 1).astype(F32)
     taper_s[...] = taper
+    code_iota = lax.broadcasted_iota(jnp.int32, (n_buf * SUB, lanes), 0).astype(F32).astype(BF16)
+    slot_iota = lax.broadcasted_iota(jnp.int32, (slots, lanes), 0).astype(F32).astype(BF16)
+    zero, one = jnp.zeros((), BF16), jnp.ones((), BF16)
 
     def dense(it):
-        code = code_s[pl.ds(it, 1), :]
-        slot = slot_s[pl.ds(it, 1), :]
+        code = code_s[pl.ds(it, 1), :].astype(BF16)
+        slot = slot_s[pl.ds(it, 1), :].astype(BF16)
         taper = taper_s[pl.ds(it, 1), :]
-        hit = lax.broadcasted_iota(jnp.int32, (n_buf * SUB, lanes), 0) == code
-        coarse = taper.astype(BF16).astype(F32)
-        left = jnp.concatenate(
-            [jnp.where(hit, coarse, 0.0).astype(BF16), jnp.where(hit, taper - coarse, 0.0).astype(BF16)], axis=0
-        )
-        right = jnp.where(lax.broadcasted_iota(jnp.int32, (slots, lanes), 0) == slot, 1.0, 0.0).astype(BF16)
+        coarse = taper.astype(BF16)
+        fine = (taper - coarse.astype(F32)).astype(BF16)
+        hit = code_iota == code
+        left = jnp.concatenate([jnp.where(hit, coarse, zero), jnp.where(hit, fine, zero)], axis=0)
+        right = jnp.where(slot_iota == slot, one, zero)
         both = lax.dot_general(left, right, (((1,), (1,)), ((), ())), preferred_element_type=F32)
         return both[: n_buf * SUB] + both[n_buf * SUB :]
 
@@ -202,7 +195,7 @@
             low_ref[n, at, :] = (block - high.astype(F32)).astype(BF16)
         return 0
 
-    lax.fori_loop(0, batch // 2, body, 0)
+    lax.fori_loop(0, batch // 2, body, 0, unroll=True)
 
 
 def dense_tapers(gz, lists, shift, patches, mloc, n_x, n_y, slots):
@@ -216,9 +209,8 @@
         in_specs=[pl.BlockSpec(memory_space=pltpu.SMEM), vmem],
         out_specs=(vmem, vmem),
         scratch_shapes=[
-            pltpu.VMEM((patches, 2 * mloc), F32),
-            pltpu.VMEM((batch, SUB * mloc), jnp.int32),
-            pltpu.VMEM((batch, SUB * mloc), jnp.int32),
+            pltpu.VMEM((batch, SUB * mloc), F32),
+            pltpu.VMEM((batch, SUB * mloc), F32),
             pltpu.VMEM((batch, SUB * mloc), F32),
         ],
         compiler_params=params(),
@@ -227,56 +219,52 @@
     )(gz, lists)
 
 
-def gram_kernel(*refs, ens, n_parts, first_buf, carry):
+def gram_kernel(*refs, ens, bufs, carry):
     refs = list(refs)
     before = refs.pop(0) if carry else None
-    stacks = refs[:n_parts]
-    own_high, own_low, halo_high, halo_low, out_ref, z_s, zr_s = refs[n_parts:]
+    stack, own_high, own_low, halo_high, halo_low, out_ref, z_s, zr_s = refs
     nb = ens // SUB
     base, tri = block_base(ens)
     rows = tri + ens
     nt = (((1,), (1,)), ((), ()))
-    n = first_buf
-    for stack in stacks:
-        for t in range(stack.shape[0]):
-            ob = stack[t, :ens, :]
-            rinv = stack[t, ens + 1 : ens + 2, :]
-            zr_s[...] = ob * rinv
-            wi = stack[t, ens : ens + 1, :]
-            for i in range(0, ens, 2):
-                ib = i // SUB
-                part = jnp.concatenate(
-                    [ob[kb * SUB : (kb + 1) * SUB] * zr_s[q : q + 1, :] for q in (i, i + 1) for kb in range(ib, nb)], axis=0
-                )
-                high = part.astype(BF16)
-                z_s[base[i] : base[i] + part.shape[0], :] = high
-                z_s[rows + base[i] : rows + base[i] + part.shape[0], :] = (part - high.astype(F32)).astype(BF16)
-            part = zr_s[...] * wi
+    for t, n in enumerate(bufs):
+        ob = stack[t, :ens, :]
+        rinv = stack[t, ens + 1 : ens + 2, :]
+        zr_s[...] = ob * rinv
+        wi = stack[t, ens : ens + 1, :]
+        for i in range(0, ens, 2):
+            ib = i // SUB
+            part = jnp.concatenate(
+                [ob[kb * SUB : (kb + 1) * SUB] * zr_s[q : q + 1, :] for q in (i, i + 1) for kb in range(ib, nb)], axis=0
+            )
             high = part.astype(BF16)
-            z_s[tri:rows, :] = high
-            z_s[rows + tri : 2 * rows, :] = (part - high.astype(F32)).astype(BF16)
-            right = jnp.concatenate([own_high[n], halo_high[n]], axis=0)
-            got = lax.dot_general(z_s[...], right, nt, preferred_element_type=F32)
-            right = jnp.concatenate([own_low[n], halo_low[n]], axis=0)
-            more = lax.dot_general(z_s[:rows, :], right, nt, preferred_element_type=F32)
-            total = got[:rows] + (got[rows:] + more)
-            if n > first_buf:
-                total = out_ref[...] + total
-            elif carry:
-                total = before[...] + total
-            out_ref[...] = total
-            n += 1
-
-
-def grams(stacks, tapers, ens, first_buf, before=None):
+            z_s[base[i] : base[i] + part.shape[0], :] = high
+            z_s[rows + base[i] : rows + base[i] + part.shape[0], :] = (part - high.astype(F32)).astype(BF16)
+        part = zr_s[...] * wi
+        high = part.astype(BF16)
+        z_s[tri:rows, :] = high
+        z_s[rows + tri : 2 * rows, :] = (part - high.astype(F32)).astype(BF16)
+        right = jnp.concatenate([own_high[n], halo_high[n]], axis=0)
+        got = lax.dot_general(z_s[...], right, nt, preferred_element_type=F32)
+        right = jnp.concatenate([own_low[n], halo_low[n]], axis=0)
+        more = lax.dot_general(z_s[:rows, :], right, nt, preferred_element_type=F32)
+        total = got[:rows] + (got[rows:] + more)
+        if t > 0:
+            total = out_ref[...] + total
+        elif carry:
+            total = before[...] + total
+        out_ref[...] = total
+
+
+def grams(stack, tapers, ens, bufs, before=None):
     vmem = pl.BlockSpec(memory_space=pltpu.VMEM)
     _, tri = block_base(ens)
     rows = tri + ens
     _, patches, slots = tapers[0].shape
     carry = before is not None
-    args = ((before,) if carry else ()) + tuple(stacks) + tuple(tapers)
+    args = ((before,) if carry else ()) + (stack,) + tuple(tapers)
     return pl.pallas_call(
-        functools.partial(gram_kernel, ens=ens, n_parts=len(stacks), first_buf=first_buf, carry=carry),
+        functools.partial(gram_kernel, ens=ens, bufs=tuple(bufs), carry=carry),
         out_shape=jax.ShapeDtypeStruct((rows, 2 * patches), F32),
         in_specs=[vmem] * len(args),
         out_specs=vmem,
@@ -386,12 +374,13 @@
         vec[right + ens + SUB * kb : right + ens + SUB * (kb + 1), :] = inner[kb]
     outer = apply(right + ens)
     for kb in range(nb):
-        out_ref[tri + SUB * kb : tri + SUB * (kb + 1), :] = outer[kb] * scale
+        vec[right + SUB * kb : right + SUB * (kb + 1), :] = outer[kb] * scale
     factor = jnp.broadcast_to(math.sqrt(ens - 1.0) / jnp.sqrt(half), (SUB, LANES))
-    for i in range(ens):
-        for kb in range(i // SUB, nb):
-            at = base[i] + SUB * (kb - i // SUB)
-            out_ref[at : at + SUB, :] = s_a[i * ens + SUB * kb : i * ens + SUB * (kb + 1), :] * factor
+    for j in range(ens):
+        weight = spread(vec, right + j)
+        for kb in range(nb):
+            at = slice(j * ens + SUB * kb, j * ens + SUB * (kb + 1))
+            out_ref[at, :] = weight + s_a[at, :] * factor
 
 
 def roots(gram, row, ens):
@@ -399,10 +388,10 @@
     square = pltpu.VMEM((ens * ens, LANES), F32)
     return pl.pallas_call(
         functools.partial(root_kernel, ens=ens),
-        out_shape=jax.ShapeDtypeStruct((rows, LANES), F32),
+        out_shape=jax.ShapeDtypeStruct((ens * ens, LANES), F32),
         grid=(1,),
         in_specs=[pl.BlockSpec((rows, LANES), lambda g: (0, row))],
-        out_specs=pl.BlockSpec((rows, LANES), lambda g: (0, 0)),
+        out_specs=pl.BlockSpec((ens * ens, LANES), lambda g: (0, 0)),
         scratch_shapes=[square] * 4 + [pltpu.VMEM((ens * ens + 2 * ens, LANES), F32)],
         compiler_params=params(),
         cost_estimate=micros(7),
@@ -410,92 +399,111 @@
     )(gram)
 
 
-def update_kernel(gz_ref, members_ref, own_ref, pair_ref, halo_ref, far_ref, out_ref, pert_s, mean_s, tx_s):
-    ens, levels, width_x, width_y = members_ref.shape
-    nb = ens // SUB
-    base, tri = block_base(ens)
-    column = lax.broadcasted_iota(jnp.int32, (width_x, width_y), 0)
-    column = jnp.where(gz_ref[0] == 0, column, width_x - 1 - column).astype(F32)
-    place = (column + 0.5) / PX - 0.5
-    weights = [
-        jnp.maximum(0.0, 1.0 - jnp.abs(place - centre)) for centre in (0.0, 1.0, -1.0, 2.0)
-    ]
-    sources = (own_ref, pair_ref, halo_ref, far_ref)
-
-    def blend(row):
-        total = weights[0] * spread(sources[0], row)
-        for w, ref in zip(weights[1:], sources[1:]):
-            total = total + w * spread(ref, row)
-        return total
-
+def center_kernel(members_ref, pert_ref, mean_ref):
+    ens, levels, width_x, _ = members_ref.shape
     for level in range(levels):
         total = members_ref[0, level].astype(F32)
         for k in range(1, ens):
             total = total + members_ref[k, level].astype(F32)
         mean = total / ens
-        shift = mean
+        mean_ref[level * width_x : (level + 1) * width_x, :] = mean
         for k in range(ens):
-            pert = members_ref[k, level].astype(F32) - mean
-            pert_s[k * levels + level] = pert
-        mean_s[level] = shift
-    for j in range(ens):
-        shared = blend(tri + j)
-        for level in range(levels):
-            mean_s[level] = mean_s[level] + pert_s[j * levels + level] * shared
-
-    for ib in range(nb):
-
-        def rows(step, _, ib=ib):
-            i = ib * SUB + step
-            start = base[ib * SUB] + step * SUB * (nb - ib)
-            for kb in range(ib, nb):
-                for s in range(SUB):
-                    value = blend(start + SUB * (kb - ib) + s)
-                    tx_s[i * ens + SUB * kb + s] = value
-                    if kb > ib:
-                        tx_s[(SUB * kb + s) * ens + i] = value
-            return 0
-
-        lax.fori_loop(0, SUB, rows, 0)
-
-    wide = 4
-
-    def body(step, _):
-        k0 = step * wide
-        for l0 in range(0, levels, wide):
-            acc = [[mean_s[l0 + l] for l in range(wide)] for _ in range(wide)]
-            for j in range(ens):
-                pert = [pert_s[j * levels + l0 + l] for l in range(wide)]
-                for k in range(wide):
-                    t = tx_s[j * ens + k0 + k]
-                    for l in range(wide):
-                        acc[k][l] = acc[k][l] + t * pert[l]
-            for k in range(wide):
-                for l in range(wide):
-                    out_ref[k0 + k, l0 + l] = acc[k][l].astype(BF16)
-        return 0
-
-    lax.fori_loop(0, ens // wide, body, 0)
-
-
-def update(gz, members, own, pair, halo, far):
+            at = (k * levels + level) * width_x
+            pert_ref[at : at + width_x, :] = members_ref[k, level].astype(F32) - mean
+
+
+def center(members):
     ens, levels, width_x, width_y = members.shape
     vmem = pl.BlockSpec(memory_space=pltpu.VMEM)
-    tile = (width_x, width_y)
+    cells = levels * width_x
     return pl.pallas_call(
-        update_kernel,
-        out_shape=jax.ShapeDtypeStruct(members.shape, BF16),
-        in_specs=[pl.BlockSpec(memory_space=pltpu.SMEM)] + [vmem] * 5,
+        center_kernel,
+        out_shape=(
+            jax.ShapeDtypeStruct((ens * cells, width_y), F32),
+            jax.ShapeDtypeStruct((cells, width_y), F32),
+        ),
+        in_specs=[vmem],
+        out_specs=(vmem, vmem),
+        compiler_params=params(),
+        cost_estimate=micros(1),
+        name="center",
+    )(members)
+
+
+def columns(gz, pert_ref, mean_ref, dest, main_ref, beside_ref, first, ens, levels, width_x):
+    nb = ens // SUB
+    near = first % PX
+
+    def body(step, _):
+        place = jnp.abs((near + step + 0.5) / PX - 0.5)
+        turned_x = first + step
+        x = jnp.where(gz == 0, turned_x, width_x - 1 - turned_x)
+        w_main = jnp.broadcast_to(1.0 - place, (SUB, LANES))
+        w_beside = jnp.broadcast_to(place, (SUB, LANES))
+        acc = [[spread(mean_ref, level * width_x + x)] * nb for level in range(levels)]
+        for j in range(ens):
+            blend = []
+            for kb in range(nb):
+                at = slice(j * ens + SUB * kb, j * ens + SUB * (kb + 1))
+                blend.append(w_main * main_ref[at, :] + w_beside * beside_ref[at, :])
+            for level in range(levels):
+                pert = spread(pert_ref, (j * levels + level) * width_x + x)
+                for kb in range(nb):
+                    acc[level][kb] = acc[level][kb] + pert * blend[kb]
+        for level in range(levels):
+            for kb in range(nb):
+                at = (SUB * kb * levels + level) * width_x + x
+                dest[pl.ds(at, SUB, stride=levels * width_x), :] = acc[level][kb]
+        return 0
+
+    lax.fori_loop(0, PX // 2, body, 0)
+
+
+def inner_kernel(gz_ref, pert_ref, mean_ref, own_ref, pair_ref, halo_ref, part_ref, *, ens, levels, width_x):
+    gz = gz_ref[0]
+    sizes = (ens, levels, width_x)
+    columns(gz, pert_ref, mean_ref, part_ref, own_ref, halo_ref, 0, *sizes)
+    columns(gz, pert_ref, mean_ref, part_ref, own_ref, pair_ref, PX // 2, *sizes)
+    columns(gz, pert_ref, mean_ref, part_ref, pair_ref, own_ref, PX, *sizes)
+
+
+def outer_kernel(gz_ref, pert_ref, mean_ref, pair_ref, far_ref, part_ref, out_ref, rest_s):
+    ens, levels, width_x, width_y = out_ref.shape
+    gz = gz_ref[0]
+    first = 3 * PX // 2
+    columns(gz, pert_ref, mean_ref, rest_s, pair_ref, far_ref, first, ens, levels, width_x)
+    x = lax.broadcasted_iota(jnp.int32, (width_x, width_y), 0)
+    inside = jnp.where(gz == 0, x, width_x - 1 - x) < first
+    for k in range(ens):
+        for level in range(levels):
+            at = slice((k * levels + level) * width_x, (k * levels + level + 1) * width_x)
+            out_ref[k, level] = jnp.where(inside, part_ref[at, :], rest_s[at, :]).astype(BF16)
+
+
+def update(gz, shape, centred, own, pair, halo, far):
+    ens, levels, width_x, width_y = shape
+    pert, mean = centred
+    vmem = pl.BlockSpec(memory_space=pltpu.VMEM)
+    smem = pl.BlockSpec(memory_space=pltpu.SMEM)
+    part = pl.pallas_call(
+        functools.partial(inner_kernel, ens=ens, levels=levels, width_x=width_x),
+        out_shape=jax.ShapeDtypeStruct(pert.shape, F32),
+        in_specs=[smem] + [vmem] * 5,
         out_specs=vmem,
-        scratch_shapes=[
-            pltpu.VMEM((ens * levels,) + tile, F32),
-            pltpu.VMEM((levels,) + tile, F32),
-            pltpu.VMEM((ens * ens,) + tile, F32),
-        ],
         compiler_params=params(),
-        cost_estimate=micros(4),
-        name="update",
-    )(gz, members, own, pair, halo, far)
+        cost_estimate=micros(3),
+        name="inner",
+    )(gz, pert, mean, own, pair, halo)
+    return pl.pallas_call(
+        outer_kernel,
+        out_shape=jax.ShapeDtypeStruct(shape, BF16),
+        in_specs=[smem] + [vmem] * 5,
+        out_specs=vmem,
+        scratch_shapes=[pltpu.VMEM(pert.shape, F32)],
+        compiler_params=params(),
+        cost_estimate=micros(1),
+        name="outer",
+    )(gz, pert, mean, pair, far, part)
 
 
 def shifted(x, axis, shift):
@@ -539,31 +547,30 @@
         stencil_weight.reshape(-1, slots),
         obs_value.reshape(1, slots),
         obs_rinv.reshape(1, slots),
-        patch_list,
-        patch_taper,
+        jnp.swapaxes(patch_list, 1, 2),
+        jnp.swapaxes(patch_taper, 1, 2),
     )
     rows = ens + SUB
-    along = {x: turned(packet, signed(x, n_x)) for x in range(1, n_x - 1)}
-    halo = turned(sent, -1)
-    along[n_x - 1] = halo[:rows]
-    along[0] = packet
-    halo_list = halo[rows:]
+    along = [packet] + [turned(packet, signed(x, n_x)) for x in range(1, n_x)]
+    halo_list = turned(sent, -1)
     own_tapers = dense_tapers(gz, own_list, 0, patches, mloc, n_x, n_y, slots)
-    along = jnp.stack([along[x] for x in range(n_x)], axis=0)
-    along = after(along, *own_tapers)
-    across = [along] + [shifted(along, "gy", signed(y, n_y)) for y in range(1, n_y)]
+    along = jnp.stack(along, axis=0)
+    centred = center(members)
+    along = after(along, *own_tapers, *centred)
+    beside = [shifted(along, "gy", signed(y, n_y)) for y in range(1, n_y)]
     halo_tapers = dense_tapers(gz, halo_list, -1, patches, mloc, n_x, n_y, slots)
-    here = jnp.stack(across, axis=1).reshape(n_x * n_y, rows, slots)
-    here = after(here, *halo_tapers)
+    tapers = own_tapers + halo_tapers
+    gram = grams(along, tapers, ens, range(n_x))
+    here = jnp.concatenate([along] + after(beside, gram), axis=0)
     there = swapped(here)
-    tapers = own_tapers + halo_tapers
-    gram = grams((here,), tapers, ens, 0)
-    gram = grams((there,), tapers, ens, n_x * n_y, gram)
+    if n_y > 1:
+        gram = grams(here[n_x:], tapers, ens, range(n_x, n_x * n_y), gram)
+    gram = grams(there, tapers, ens, range(n_x * n_y, 2 * n_x * n_y), gram)
     own = roots(gram, 0, ens)
     pair = swapped(own)
     halo = roots(after(gram, own), 1, ens)
     far = swapped(halo)
-    return update(gz, members, own, pair, halo, far)
+    return update(gz, members.shape, centred, own, pair, halo, far)
 
 
 def solution(mesh):

time: 50.3 us -> 44.3 us (0.88)
  Pallas kernels: 32.6 us -> 29.5 us
  waiting for transfers between devices: 5.43 us -> 2.5 us
  local copies, waits for them, and re-layouts: 2.84 us -> 1.22 us
  starting transfers between devices: 8.39 us -> 9.94 us
    pallas_call x2, Pallas kernels: 5.9 us -> 2.85 us  [dense_tapers(): pl.pallas_call(functools.partial(taper_kernel, shift=shift, n_x=n_x, n_y=...]
    ppermute x3 -> x4, waiting for transfers between devices: 2.87 us -> 1.13 us  [turned(): return lax.ppermute(x, ('gx', 'gz'), pairs)]
    unnamed x16 -> x6, local copies, waits for them, and re-layouts: 2.81 us -> 1.22 us
    ppermute x3 -> x4, starting transfers between devices: 6.12 us -> 7.68 us  [turned(): return lax.ppermute(x, ('gx', 'gz'), pairs)]
    ppermute x3, waiting for transfers between devices: 1.69 us -> 0.28 us  [swapped(): return lax.ppermute(x, 'gz', [(0, 1), (1, 0)])]
    pallas_call x3 -> x6, Pallas kernels: 9.47 us -> 9.89 us  [the longest x3 5.18 us: grams(): pl.pallas_call(functools.partial(gram_kernel, ens=ens, bufs=tuple(bufs),...]
  transfers between devices with their start and end apart: 7 -> 8, of which waited for: 4 -> 4; matrix products, arithmetic and copies ran while one was open for 0% -> 0% of each run, Pallas kernels for 17% -> 34%
where the time goes in v3:
time: 44.3 us; the launch traced here: 44 us
  Pallas kernels  29.5 us (67%)
  starting transfers between devices  9.94 us (22%)
  waiting for transfers between devices  2.5 us (6%)
  local copies, waits for them, and re-layouts  1.22 us (3%)
  between operations  0.79 us (2%)
    pallas_call x2, Pallas kernels, roots(): pl.pallas_call(functools.partial(root_kernel, ens=ens), out_shape=jax.Sha...  13.7 us
    ppermute x4, starting transfers between devices, turned(): return lax.ppermute(x, ('gx', 'gz'), pairs)  7.68 us
    pallas_call x3, Pallas kernels, grams(): pl.pallas_call(functools.partial(gram_kernel, ens=ens, bufs=tuple(bufs),...  5.18 us
    pallas_call x1, Pallas kernels, observe(): pl.pallas_call(observe_kernel, out_shape=(jax.ShapeDtypeStruct((ens + SUB...  3.13 us
    pallas_call x2, Pallas kernels, dense_tapers(): pl.pallas_call(functools.partial(taper_kernel, shift=shift, n_x=n_x, n_y=...  2.85 us
    pallas_call x1, Pallas kernels, update(): pl.pallas_call(functools.partial(inner_kernel, ens=ens, levels=levels, wi...  2.7 us
    pallas_call x1, Pallas kernels, update(): pl.pallas_call(outer_kernel, out_shape=jax.ShapeDtypeStruct(shape, BF16),...  1.8 us
    ppermute x1, starting transfers between devices, shifted(): return lax.ppermute(x, axis, [((i + shift) % size, i) for i in range(size)])  1.55 us
  transfers between devices with their start and end apart: 8, of which 4 were waited for; matrix products, arithmetic and copies ran while one was open for 0% of the time, Pallas kernels for 34%

profile of v3, /device:TPU:0, one launch (start us, length us, event | category | flops | bytes accessed | tf_op | source)
XLA Modules:
  0.0 44.0 jit_solution(10601676385050478102)
XLA Ops:
  0.7 3.1 %observe.1 = (f32[40,256]{1,0:T(8,128)}, f32[128,128]{1,0:T(8,128)}, f32[128,128]{1,0:T(8,128)}) custom-call(s32[1]{0:T(128)} %bitcast.gz_ref, s32[1]{0:T(128)} %bitcast.12.count_ref, bf16[32,8,8,128]{3,2,1,0:T(8,128)(2,1)} %members_in.1, s32[8,256]{1,0:T(8,128)} %bitcast.19, f32[8,256]{1,0:T(8,128)} %bitcast.20, f32[1,256]{1,0:T(1,128)} %bitcast.21, ...), custom_call_target="tpu_custom_call" | custom-call | flops 3000000000 | bytes 9000000 | tf_op jit(solution)/shard_map/observe/pallas_call | solution.py:120
  3.8 3.1 %collective-permute-start.2 = (f32[40,256]{1,0:T(8,128)}, f32[40,256]{1,0:T(8,128)S(1)}, u32[]{:S(2)}, u32[]{:S(2)}) collective-permute-start(f32[40,256]{1,0:T(8,128)} %get-tuple-element.19), channel_id=1, source_target_pairs={{12,0},{0,4},{4,8},{8,12},{5,1},{9,5},{13,9},{1,13},{14,2},{2,6},{... | collective-permute-start | bytes 122888 | tf_op jit(solution)/shard_map/ppermute | solution.py:518
  6.9 2.6 %collective-permute-start.1 = (f32[40,256]{1,0:T(8,128)}, f32[40,256]{1,0:T(8,128)S(1)}, u32[]{:S(2)}, u32[]{:S(2)}) collective-permute-start(f32[40,256]{1,0:T(8,128)} %get-tuple-element.19), channel_id=1, source_target_pairs={{8,0},{12,4},{0,8},{4,12},{9,1},{13,5},{1,9},{5,13},{10,2},{14,6},... | collective-permute-start | bytes 122888 | tf_op jit(solution)/shard_map/ppermute | solution.py:518
  9.4 1.3 %collective-permute-start = (f32[40,256]{1,0:T(8,128)}, f32[40,256]{1,0:T(8,128)S(1)}, u32[]{:S(2)}, u32[]{:S(2)}) collective-permute-start(f32[40,256]{1,0:T(8,128)} %get-tuple-element.19), channel_id=1, source_target_pairs={{4,0},{8,4},{12,8},{0,12},{13,1},{1,5},{5,9},{9,13},{6,2},{10,6},{... | collective-permute-start | bytes 122888 | tf_op jit(solution)/shard_map/ppermute | solution.py:518
  10.8 0.7 %collective-permute-start.3 = (f32[128,128]{1,0:T(8,128)}, f32[128,128]{1,0:T(8,128)S(1)}, u32[]{:S(2)}, u32[]{:S(2)}) collective-permute-start(f32[128,128]{1,0:T(8,128)} %get-tuple-element.24), channel_id=1, source_target_pairs={{12,0},{0,4},{4,8},{8,12},{5,1},{9,5},{13,9},{1,13},{14,2},{2,6},{... | collective-permute-start | bytes 196616 | tf_op jit(solution)/shard_map/ppermute | solution.py:518
  11.5 0.0 copy-start.1
  11.5 0.8 %copy-done.1 = f32[128,128]{1,0:T(8,128)S(1)} copy-done((f32[128,128]{1,0:T(8,128)S(1)}, f32[128,128]{1,0:T(8,128)}, u32[]{:S(2)}) %copy-start.1) | copy-done | bytes 65560
  12.3 0.0 copy-start
  12.3 1.4 %dense_tapers.2 = (bf16[16,128,256]{2,1,0:T(8,128)(2,1)S(1)}, bf16[16,128,256]{2,1,0:T(8,128)(2,1)S(1)}) custom-call(s32[1]{0:T(128)} %bitcast.gz_ref, f32[128,128]{1,0:T(8,128)S(1)} %copy-done.1), custom_call_target="tpu_custom_call" | custom-call | flops 3000000000 | bytes 9000000 | tf_op jit(solution)/shard_map/dense_tapers/pallas_call | solution.py:206
  13.7 0.0 copy-done
  13.8 0.0 copy-start.2
  13.8 0.2 center.1
  14.0 0.0 collective-permute-done.2
  14.0 0.0 collective-permute-done.1
  14.0 0.1 collective-permute-done
  14.2 0.4 copy-done.2
  14.6 1.5 %collective-permute-start.4 = (f32[4,40,256]{2,1,0:T(8,128)S(1)}, f32[4,40,256]{2,1,0:T(8,128)S(1)}, u32[]{:S(2)}, u32[]{:S(2)}) collective-permute-start(f32[4,40,256]{2,1,0:T(8,128)S(1)} %pad_maximum_fusion.1.refs_0_), channel_id=1, source_target_pairs={{2,0},{0,2},{3,1},{1,3},{6,4},{4,6},{7,5},{5,7},{10,8},{8,10},{11,... | collective-permute-start | bytes 491528 | tf_op jit(solution)/shard_map/ppermute | solution.py:511
  16.1 1.0 %collective-permute-done.3.list_ref = f32[128,128]{1,0:T(8,128)S(1)} collective-permute-done((f32[128,128]{1,0:T(8,128)}, f32[128,128]{1,0:T(8,128)S(1)}, u32[]{:S(2)}, u32[]{:S(2)}) %collective-permute-start.3) | collective-permute-done | bytes 65568 | tf_op jit(solution)/shard_map/ppermute | solution.py:518
  17.1 1.4 %dense_tapers.3 = (bf16[16,128,256]{2,1,0:T(8,128)(2,1)S(1)}, bf16[16,128,256]{2,1,0:T(8,128)(2,1)S(1)}) custom-call(s32[1]{0:T(128)} %bitcast.gz_ref, f32[128,128]{1,0:T(8,128)S(1)} %collective-permute-done.3.list_ref), custom_call_target="tpu_custom_call" | custom-call | flops 3000000000 | bytes 9000000 | tf_op jit(solution)/shard_map/dense_tapers/pallas_call | solution.py:206
  18.5 1.3 %grams.3.refs_0_ = f32[672,256]{1,0:T(8,128)S(1)} custom-call(f32[4,40,256]{2,1,0:T(8,128)S(1)} %pad_maximum_fusion.1.refs_0_, bf16[16,128,256]{2,1,0:T(8,128)(2,1)S(1)} %get-tuple-element.21.refs_1_.refs_2_, bf16[16,128,256]{2,1,0:T(8,128)(2,1)S(1)} %get-tuple-element.22.refs_2_.refs_3_, bf16[16,128,256]{2,1,0:T(8,128)(2,1)S(1)} %get-tuple-element.25.refs_3_.refs_4_, ...), custom_call_target="tpu_custom_call" | custom-call | flops 2000000000 | bytes 6000000 | tf_op jit(solution)/shard_map/grams/pallas_call | solution.py:266
  19.8 1.1 %collective-permute-done.4.refs_1_ = f32[4,40,256]{2,1,0:T(8,128)S(1)} collective-permute-done((f32[4,40,256]{2,1,0:T(8,128)S(1)}, f32[4,40,256]{2,1,0:T(8,128)S(1)}, u32[]{:S(2)}, u32[]{:S(2)}) %collective-permute-start.4) | collective-permute-done | bytes 163872 | tf_op jit(solution)/shard_map/ppermute | solution.py:511
  21.0 0.1 collective-permute-start.5
  21.1 1.3 %grams.4.refs_0_ = f32[672,256]{1,0:T(8,128)S(1)} custom-call(f32[672,256]{1,0:T(8,128)S(1)} %grams.3.refs_0_, f32[4,40,256]{2,1,0:T(8,128)S(1)} %collective-permute-done.4.refs_1_, bf16[16,128,256]{2,1,0:T(8,128)(2,1)S(1)} %get-tuple-element.21.refs_1_.refs_2_, bf16[16,128,256]{2,1,0:T(8,128)(2,1)S(1)} %get-tuple-element.22.refs_2_.refs_3_, ...), custom_call_target="tpu_custom_call" | custom-call | flops 2000000000 | bytes 6000000 | tf_op jit(solution)/shard_map/grams/pallas_call | solution.py:266
  22.4 0.3 collective-permute-done.5.refs_1_
  22.7 2.5 %grams.5.gram_ref = f32[672,256]{1,0:T(8,128)S(1)} custom-call(f32[672,256]{1,0:T(8,128)S(1)} %grams.4.refs_0_, f32[8,40,256]{2,1,0:T(8,128)S(1)} %collective-permute-done.5.refs_1_, bf16[16,128,256]{2,1,0:T(8,128)(2,1)S(1)} %get-tuple-element.21.refs_1_.refs_2_, bf16[16,128,256]{2,1,0:T(8,128)(2,1)S(1)} %get-tuple-element.22.refs_2_.refs_3_, ...), custom_call_target="tpu_custom_call" | custom-call | flops 2000000000 | bytes 6000000 | tf_op jit(solution)/shard_map/grams/pallas_call | solution.py:266
  25.2 6.9 %roots.2.own_ref = f32[1024,128]{1,0:T(8,128)S(1)} custom-call(f32[672,256]{1,0:T(8,128)S(1)} %grams.5.gram_ref), custom_call_target="tpu_custom_call" | custom-call | flops 7000000000 | bytes 21000000 | tf_op jit(solution)/shard_map/roots/pallas_call | solution.py:389
  32.1 0.3 collective-permute-start.6
  32.4 6.7 %roots.3.halo_ref = f32[1024,128]{1,0:T(8,128)S(1)} custom-call(f32[672,256]{1,0:T(8,128)S(1)} %grams.5.gram_ref), custom_call_target="tpu_custom_call" | custom-call | flops 7000000000 | bytes 21000000 | tf_op jit(solution)/shard_map/roots/pallas_call | solution.py:389
  39.2 0.3 collective-permute-start.7
  39.5 0.0 collective-permute-done.6.pair_ref
  39.5 2.7 %inner.1.part_ref = f32[2048,128]{1,0:T(8,128)S(1)} custom-call(s32[1]{0:T(128)} %bitcast.gz_ref, f32[2048,128]{1,0:T(8,128)S(1)} %get-tuple-element.17.pert_ref, f32[64,128]{1,0:T(8,128)S(1)} %get-tuple-element.18.mean_ref, f32[1024,128]{1,0:T(8,128)S(1)} %roots.2.own_ref, f32[1024,128]{1,0:T(8,128)S(1)} %collective-permute-done.6.pair_ref, ...), custom_call_target="tpu_custom_call" | custom-call | flops 3000000000 | bytes 9000000 | tf_op jit(solution)/shard_map/inner/pallas_call | solution.py:488
  42.2 0.0 collective-permute-done.7.far_ref
  42.2 1.8 %outer.1 = bf16[32,8,8,128]{3,2,1,0:T(8,128)(2,1)} custom-call(s32[1]{0:T(128)} %bitcast.gz_ref, f32[2048,128]{1,0:T(8,128)S(1)} %get-tuple-element.17.pert_ref, f32[64,128]{1,0:T(8,128)S(1)} %get-tuple-element.18.mean_ref, f32[1024,128]{1,0:T(8,128)S(1)} %collective-permute-done.6.pair_ref, f32[1024,128]{1,0:T(8,128)S(1)} %collective-permute-done.7.far_ref, ...), custom_call_target="tpu_custom_call" | custom-call | flops 1000000000 | bytes 3000000 | tf_op jit(solution)/shard_map/outer/pallas_call | solution.py:497
  (2 shorter events, 0.0 us)
Async XLA Ops:
  3.8 10.2 %collective-permute-start.2 = (f32[40,256]{1,0:T(8,128)}, f32[40,256]{1,0:T(8,128)S(1)}, u32[]{:S(2)}, u32[]{:S(2)}) collective-permute-start(f32[40,256]{1,0:T(8,128)} %get-tuple-element.19), channel_id=1, source_target_pairs={{12,0},{0,4},{4,8},{8,12},{5,1},{9,5},{13,9},{1,13},{14,2},{2,6},{... | collective-permute-start | bytes 122888 | tf_op jit(solution)/shard_map/ppermute | solution.py:518
  6.9 7.1 %collective-permute-start.1 = (f32[40,256]{1,0:T(8,128)}, f32[40,256]{1,0:T(8,128)S(1)}, u32[]{:S(2)}, u32[]{:S(2)}) collective-permute-start(f32[40,256]{1,0:T(8,128)} %get-tuple-element.19), channel_id=1, source_target_pairs={{8,0},{12,4},{0,8},{4,12},{9,1},{13,5},{1,9},{5,13},{10,2},{14,6},... | collective-permute-start | bytes 122888 | tf_op jit(solution)/shard_map/ppermute | solution.py:518
  9.4 4.7 %collective-permute-start = (f32[40,256]{1,0:T(8,128)}, f32[40,256]{1,0:T(8,128)S(1)}, u32[]{:S(2)}, u32[]{:S(2)}) collective-permute-start(f32[40,256]{1,0:T(8,128)} %get-tuple-element.19), channel_id=1, source_target_pairs={{4,0},{8,4},{12,8},{0,12},{13,1},{1,5},{5,9},{9,13},{6,2},{10,6},{... | collective-permute-start | bytes 122888 | tf_op jit(solution)/shard_map/ppermute | solution.py:518
  10.8 6.3 %collective-permute-start.3 = (f32[128,128]{1,0:T(8,128)}, f32[128,128]{1,0:T(8,128)S(1)}, u32[]{:S(2)}, u32[]{:S(2)}) collective-permute-start(f32[128,128]{1,0:T(8,128)} %get-tuple-element.24), channel_id=1, source_target_pairs={{12,0},{0,4},{4,8},{8,12},{5,1},{9,5},{13,9},{1,13},{14,2},{2,6},{... | collective-permute-start | bytes 196616 | tf_op jit(solution)/shard_map/ppermute | solution.py:518
  11.5 0.8 %copy-start.1 = (f32[128,128]{1,0:T(8,128)S(1)}, f32[128,128]{1,0:T(8,128)}, u32[]{:S(2)}) copy-start(f32[128,128]{1,0:T(8,128)} %get-tuple-element.20.list_ref) | copy-start | bytes 196612
  12.3 1.4 %copy-start = (bf16[32,8,8,128]{3,2,1,0:T(8,128)(2,1)S(1)}, bf16[32,8,8,128]{3,2,1,0:T(8,128)(2,1)}, u32[]{:S(2)}) copy-start(bf16[32,8,8,128]{3,2,1,0:T(8,128)(2,1)} %members_in.1) | copy-start | bytes 1572868
  13.8 0.8 %copy-start.2 = (f32[40,256]{1,0:T(8,128)S(1)}, f32[40,256]{1,0:T(8,128)}, u32[]{:S(2)}) copy-start(f32[40,256]{1,0:T(8,128)} %get-tuple-element.19) | copy-start | bytes 122884
  14.6 6.4 %collective-permute-start.4 = (f32[4,40,256]{2,1,0:T(8,128)S(1)}, f32[4,40,256]{2,1,0:T(8,128)S(1)}, u32[]{:S(2)}, u32[]{:S(2)}) collective-permute-start(f32[4,40,256]{2,1,0:T(8,128)S(1)} %pad_maximum_fusion.1.refs_0_), channel_id=1, source_target_pairs={{2,0},{0,2},{3,1},{1,3},{6,4},{4,6},{7,5},{5,7},{10,8},{8,10},{11,... | collective-permute-start | bytes 491528 | tf_op jit(solution)/shard_map/ppermute | solution.py:511
  21.0 1.7 %collective-permute-start.5 = (f32[8,40,256]{2,1,0:T(8,128)S(1)}, f32[8,40,256]{2,1,0:T(8,128)S(1)}, u32[]{:S(2)}, u32[]{:S(2)}) collective-permute-start(f32[8,40,256]{2,1,0:T(8,128)S(1)} %pad_maximum_fusion), channel_id=1, source_target_pairs={{0,1},{1,0},{2,3},{3,2},{4,5},{5,4},{6,7},{7,6},{8,9},{9,8},{10,11... | collective-permute-start | bytes 983048 | tf_op jit(solution)/shard_map/ppermute | solution.py:522
  32.1 7.4 %collective-permute-start.6 = (f32[1024,128]{1,0:T(8,128)S(1)}, f32[1024,128]{1,0:T(8,128)S(1)}, u32[]{:S(2)}, u32[]{:S(2)}) collective-permute-start(f32[1024,128]{1,0:T(8,128)S(1)} %roots.2.own_ref), channel_id=1, source_target_pairs={{0,1},{1,0},{2,3},{3,2},{4,5},{5,4},{6,7},{7,6},{8,9},{9,8},{10,11... | collective-permute-start | bytes 1572872 | tf_op jit(solution)/shard_map/ppermute | solution.py:522
  39.2 3.1 %collective-permute-start.7 = (f32[1024,128]{1,0:T(8,128)S(1)}, f32[1024,128]{1,0:T(8,128)S(1)}, u32[]{:S(2)}, u32[]{:S(2)}) collective-permute-start(f32[1024,128]{1,0:T(8,128)S(1)} %roots.3.halo_ref), channel_id=1, source_target_pairs={{0,1},{1,0},{2,3},{3,2},{4,5},{5,4},{6,7},{7,6},{8,9},{9,8},{10,11... | collective-permute-start | bytes 1572872 | tf_op jit(solution)/shard_map/ppermute | solution.py:522

commit v4 on v3

--- a/solution.py
+++ b/solution.py
@@ -9,6 +9,7 @@
 from jax.sharding import PartitionSpec as P
 
 PX = 4
+BATCH = 8
 F32 = jnp.float32
 BF16 = jnp.bfloat16
 LANES = 128
@@ -70,20 +71,31 @@
     y_iota = lax.broadcasted_iota(jnp.int32, (width_y, slots), 0)
     pick[:, :slots] = jnp.where(y_iota == low0, 1.0, 0.0).astype(BF16)
     pick[:, slots:] = jnp.where(y_iota == low0 + 1, 1.0, 0.0).astype(BF16)
+    for copy in copies[3:]:
+        copy.wait()
+    gz = gz_ref[0]
+    own_ref[...] = jnp.concatenate([ids_ref[gz].astype(F32), tapers_ref[gz]], axis=0).T
+    sent_ref[...] = jnp.concatenate([ids_ref[1 - gz].astype(F32), tapers_ref[1 - gz]], axis=0).T
     copies[2].wait()
 
-    def member(k, _):
-        rows = members_ref[k].astype(F32).reshape(levels * width_x, width_y).astype(BF16)
+    cells = levels * width_x
+
+    def batch(step, _):
+        rows = members_ref[pl.ds(step * BATCH, BATCH)].astype(F32).reshape(BATCH * cells, width_y).astype(BF16)
         got = jnp.dot(rows, pick[...], preferred_element_type=F32)
-        term = got[:, :slots] * wx[0] + got[:, slots:] * wx[1]
-        total = term[:SUB]
-        for q in range(1, levels * width_x // SUB):
-            total = total + term[q * SUB : (q + 1) * SUB]
-        for half in range(slots // LANES):
-            part[half, pl.ds(pl.multiple_of(k * SUB, SUB), SUB), :] = total[:, half * LANES : (half + 1) * LANES]
+        for q in range(BATCH):
+            total = None
+            for at in range(0, cells, SUB):
+                row = slice(q * cells + at, q * cells + at + SUB)
+                near = slice(at, at + SUB)
+                term = got[row, :slots] * wx[0, near] + got[row, slots:] * wx[1, near]
+                total = term if at == 0 else total + term
+            for half in range(slots // LANES):
+                at = pl.ds(pl.multiple_of((step * BATCH + q) * SUB, SUB), SUB)
+                part[half, at, :] = total[:, half * LANES : (half + 1) * LANES]
         return 0
 
-    lax.fori_loop(0, ens, member, 0, unroll=8)
+    lax.fori_loop(0, ens // BATCH, batch, 0, unroll=True)
     groups = []
     for kb in range(ens // SUB):
         halves = []
@@ -99,16 +111,11 @@
     mean = jnp.sum(total, axis=0, keepdims=True) / ens
     for kb in range(ens // SUB):
         out_ref[kb * SUB : (kb + 1) * SUB, :] = groups[kb] - mean
-    for copy in copies[3:]:
-        copy.wait()
     live = lax.broadcasted_iota(jnp.int32, (1, slots), 1) < count_ref[0]
     innovation = value_ref[...] - mean
     rinv = jnp.where(live, rinv_ref[...], 0.0)
     row = lax.broadcasted_iota(jnp.int32, (SUB, slots), 0)
     out_ref[ens : ens + SUB, :] = jnp.where(row == 0, innovation, jnp.where(row == 1, rinv, 0.0))
-    gz = gz_ref[0]
-    own_ref[...] = jnp.concatenate([ids_ref[gz].astype(F32), tapers_ref[gz]], axis=0).T
-    sent_ref[...] = jnp.concatenate([ids_ref[1 - gz].astype(F32), tapers_ref[1 - gz]], axis=0).T
 
 
 def observe(gz, count, members, cell, weight, value, rinv, ids, tapers):
@@ -304,23 +311,24 @@
                             dest[pl.ds(SUB * kb * ens + i0 + ii, SUB, stride=ens), :] = value
             return 0
 
-        lax.fori_loop(0, SUB // rows, body, 0)
-
-
-def root_kernel(gram_ref, out_ref, s_a, s_b, s_c, s_d, vec, *, ens):
+        lax.fori_loop(0, SUB // rows, body, 0, unroll=True)
+
+
+def root_kernel(gram_ref, out_ref, s_a, s_b, s_c, s_d, vec, *, ens, row):
     nb = ens // SUB
     base, tri = block_base(ens)
-    diag = gram_ref[0:1, :]
+    lanes = slice(row * LANES, (row + 1) * LANES)
+    diag = gram_ref[0:1, lanes]
     for i in range(1, ens):
         at = base[i] + i % SUB
-        diag = diag + gram_ref[at : at + 1, :]
+        diag = diag + gram_ref[at : at + 1, lanes]
     half = 0.5 * (diag + (ens - 1.0) * ens)
     scale = jnp.broadcast_to(1.0 / half, (SUB, LANES))
     iota = lax.broadcasted_iota(jnp.int32, (SUB, LANES), 0)
     for i in range(ens):
         for kb in range(i // SUB, nb):
             at = base[i] + SUB * (kb - i // SUB)
-            value = gram_ref[at : at + SUB, :]
+            value = gram_ref[at : at + SUB, lanes]
             if kb == i // SUB:
                 value = jnp.where(iota == i % SUB, value + (ens - 1.0), value)
             value = value * scale
@@ -358,7 +366,7 @@
     product(ens, s_d, vec.at[pl.ds(0, ens * ens)], (s_a,), plain)
 
     right = ens * ens
-    vec[right : right + ens, :] = gram_ref[tri : tri + ens, :]
+    vec[right : right + ens, :] = gram_ref[tri : tri + ens, lanes]
 
     def apply(source):
         sums = [None] * nb
@@ -384,14 +392,13 @@
 
 
 def roots(gram, row, ens):
-    rows = gram.shape[0]
     square = pltpu.VMEM((ens * ens, LANES), F32)
+    vmem = pl.BlockSpec(memory_space=pltpu.VMEM)
     return pl.pallas_call(
-        functools.partial(root_kernel, ens=ens),
+        functools.partial(root_kernel, ens=ens, row=row),
         out_shape=jax.ShapeDtypeStruct((ens * ens, LANES), F32),
-        grid=(1,),
-        in_specs=[pl.BlockSpec((rows, LANES), lambda g: (0, row))],
-        out_specs=pl.BlockSpec((ens * ens, LANES), lambda g: (0, 0)),
+        in_specs=[vmem],
+        out_specs=vmem,
         scratch_shapes=[square] * 4 + [pltpu.VMEM((ens * ens + 2 * ens, LANES), F32)],
         compiler_params=params(),
         cost_estimate=micros(7),

time: 44.3 us -> 43.3 us (0.977)
  Pallas kernels: 29.5 us -> 28.5 us
    pallas_call x1, Pallas kernels: 3.13 us -> 2.6 us  [observe(): pl.pallas_call(observe_kernel, out_shape=(jax.ShapeDtypeStruct((ens + SUB...]
    pallas_call x2, Pallas kernels: 13.7 us -> 13.2 us  [roots(): pl.pallas_call(functools.partial(root_kernel, ens=ens, row=row), out_shap...]
  transfers between devices with their start and end apart: 8 -> 8, of which waited for: 4 -> 4; matrix products, arithmetic and copies ran while one was open for 0% -> 0% of each run, Pallas kernels for 34% -> 35%
where the time goes in v4:
time: 43.3 us; the launch traced here: 43 us
  Pallas kernels  28.5 us (66%)
  starting transfers between devices  9.95 us (23%)
  waiting for transfers between devices  2.5 us (6%)
  local copies, waits for them, and re-layouts  1.23 us (3%)
  between operations  0.79 us (2%)
    pallas_call x2, Pallas kernels, roots(): pl.pallas_call(functools.partial(root_kernel, ens=ens, row=row), out_shap...  13.2 us
    ppermute x4, starting transfers between devices, turned(): return lax.ppermute(x, ('gx', 'gz'), pairs)  7.69 us
    pallas_call x3, Pallas kernels, grams(): pl.pallas_call(functools.partial(gram_kernel, ens=ens, bufs=tuple(bufs),...  5.18 us
    pallas_call x2, Pallas kernels, dense_tapers(): pl.pallas_call(functools.partial(taper_kernel, shift=shift, n_x=n_x, n_y=...  2.85 us
    pallas_call x1, Pallas kernels, update(): pl.pallas_call(functools.partial(inner_kernel, ens=ens, levels=levels, wi...  2.7 us
    pallas_call x1, Pallas kernels, observe(): pl.pallas_call(observe_kernel, out_shape=(jax.ShapeDtypeStruct((ens + SUB...  2.6 us
    pallas_call x1, Pallas kernels, update(): pl.pallas_call(outer_kernel, out_shape=jax.ShapeDtypeStruct(shape, BF16),...  1.8 us
    ppermute x1, starting transfers between devices, shifted(): return lax.ppermute(x, axis, [((i + shift) % size, i) for i in range(size)])  1.54 us
  transfers between devices with their start and end apart: 8, of which 4 were waited for; matrix products, arithmetic and copies ran while one was open for 0% of the time, Pallas kernels for 35%

profile of v4, /device:TPU:0, one launch (start us, length us, event | category | flops | bytes accessed | tf_op | source)
XLA Modules:
  0.0 43.0 jit_solution(4152698311962991380)
XLA Ops:
  0.7 2.6 %observe.1 = (f32[40,256]{1,0:T(8,128)}, f32[128,128]{1,0:T(8,128)}, f32[128,128]{1,0:T(8,128)}) custom-call(s32[1]{0:T(128)} %bitcast.gz_ref, s32[1]{0:T(128)} %bitcast.12.count_ref, bf16[32,8,8,128]{3,2,1,0:T(8,128)(2,1)} %members_in.1, s32[8,256]{1,0:T(8,128)} %bitcast.19, f32[8,256]{1,0:T(8,128)} %bitcast.20, f32[1,256]{1,0:T(1,128)} %bitcast.21, ...), custom_call_target="tpu_custom_call" | custom-call | flops 3000000000 | bytes 9000000 | tf_op jit(solution)/shard_map/observe/pallas_call | solution.py:127
  3.3 3.1 %collective-permute-start.2 = (f32[40,256]{1,0:T(8,128)}, f32[40,256]{1,0:T(8,128)S(1)}, u32[]{:S(2)}, u32[]{:S(2)}) collective-permute-start(f32[40,256]{1,0:T(8,128)} %get-tuple-element.19), channel_id=1, source_target_pairs={{12,0},{0,4},{4,8},{8,12},{5,1},{9,5},{13,9},{1,13},{14,2},{2,6},{... | collective-permute-start | bytes 122888 | tf_op jit(solution)/shard_map/ppermute | solution.py:525
  6.3 2.6 %collective-permute-start.1 = (f32[40,256]{1,0:T(8,128)}, f32[40,256]{1,0:T(8,128)S(1)}, u32[]{:S(2)}, u32[]{:S(2)}) collective-permute-start(f32[40,256]{1,0:T(8,128)} %get-tuple-element.19), channel_id=1, source_target_pairs={{8,0},{12,4},{0,8},{4,12},{9,1},{13,5},{1,9},{5,13},{10,2},{14,6},... | collective-permute-start | bytes 122888 | tf_op jit(solution)/shard_map/ppermute | solution.py:525
  8.9 1.3 %collective-permute-start = (f32[40,256]{1,0:T(8,128)}, f32[40,256]{1,0:T(8,128)S(1)}, u32[]{:S(2)}, u32[]{:S(2)}) collective-permute-start(f32[40,256]{1,0:T(8,128)} %get-tuple-element.19), channel_id=1, source_target_pairs={{4,0},{8,4},{12,8},{0,12},{13,1},{1,5},{5,9},{9,13},{6,2},{10,6},{... | collective-permute-start | bytes 122888 | tf_op jit(solution)/shard_map/ppermute | solution.py:525
  10.3 0.7 %collective-permute-start.3 = (f32[128,128]{1,0:T(8,128)}, f32[128,128]{1,0:T(8,128)S(1)}, u32[]{:S(2)}, u32[]{:S(2)}) collective-permute-start(f32[128,128]{1,0:T(8,128)} %get-tuple-element.24), channel_id=1, source_target_pairs={{12,0},{0,4},{4,8},{8,12},{5,1},{9,5},{13,9},{1,13},{14,2},{2,6},{... | collective-permute-start | bytes 196616 | tf_op jit(solution)/shard_map/ppermute | solution.py:525
  11.0 0.0 copy-start.1
  11.0 0.8 %copy-done.1 = f32[128,128]{1,0:T(8,128)S(1)} copy-done((f32[128,128]{1,0:T(8,128)S(1)}, f32[128,128]{1,0:T(8,128)}, u32[]{:S(2)}) %copy-start.1) | copy-done | bytes 65560
  11.8 0.0 copy-start
  11.8 1.4 %dense_tapers.2 = (bf16[16,128,256]{2,1,0:T(8,128)(2,1)S(1)}, bf16[16,128,256]{2,1,0:T(8,128)(2,1)S(1)}) custom-call(s32[1]{0:T(128)} %bitcast.gz_ref, f32[128,128]{1,0:T(8,128)S(1)} %copy-done.1), custom_call_target="tpu_custom_call" | custom-call | flops 3000000000 | bytes 9000000 | tf_op jit(solution)/shard_map/dense_tapers/pallas_call | solution.py:213
  13.2 0.0 copy-done
  13.2 0.0 copy-start.2
  13.3 0.2 center.1
  13.5 0.0 collective-permute-done.2
  13.5 0.0 collective-permute-done.1
  13.5 0.1 collective-permute-done
  13.6 0.4 copy-done.2
  14.0 1.5 %collective-permute-start.4 = (f32[4,40,256]{2,1,0:T(8,128)S(1)}, f32[4,40,256]{2,1,0:T(8,128)S(1)}, u32[]{:S(2)}, u32[]{:S(2)}) collective-permute-start(f32[4,40,256]{2,1,0:T(8,128)S(1)} %pad_maximum_fusion.1.refs_0_), channel_id=1, source_target_pairs={{2,0},{0,2},{3,1},{1,3},{6,4},{4,6},{7,5},{5,7},{10,8},{8,10},{11,... | collective-permute-start | bytes 491528 | tf_op jit(solution)/shard_map/ppermute | solution.py:518
  15.6 1.0 %collective-permute-done.3.list_ref = f32[128,128]{1,0:T(8,128)S(1)} collective-permute-done((f32[128,128]{1,0:T(8,128)}, f32[128,128]{1,0:T(8,128)S(1)}, u32[]{:S(2)}, u32[]{:S(2)}) %collective-permute-start.3) | collective-permute-done | bytes 65568 | tf_op jit(solution)/shard_map/ppermute | solution.py:525
  16.6 1.4 %dense_tapers.3 = (bf16[16,128,256]{2,1,0:T(8,128)(2,1)S(1)}, bf16[16,128,256]{2,1,0:T(8,128)(2,1)S(1)}) custom-call(s32[1]{0:T(128)} %bitcast.gz_ref, f32[128,128]{1,0:T(8,128)S(1)} %collective-permute-done.3.list_ref), custom_call_target="tpu_custom_call" | custom-call | flops 3000000000 | bytes 9000000 | tf_op jit(solution)/shard_map/dense_tapers/pallas_call | solution.py:213
  18.0 1.3 %grams.3.refs_0_ = f32[672,256]{1,0:T(8,128)S(1)} custom-call(f32[4,40,256]{2,1,0:T(8,128)S(1)} %pad_maximum_fusion.1.refs_0_, bf16[16,128,256]{2,1,0:T(8,128)(2,1)S(1)} %get-tuple-element.21.refs_1_.refs_2_, bf16[16,128,256]{2,1,0:T(8,128)(2,1)S(1)} %get-tuple-element.22.refs_2_.refs_3_, bf16[16,128,256]{2,1,0:T(8,128)(2,1)S(1)} %get-tuple-element.25.refs_3_.refs_4_, ...), custom_call_target="tpu_custom_call" | custom-call | flops 2000000000 | bytes 6000000 | tf_op jit(solution)/shard_map/grams/pallas_call | solution.py:273
  19.3 1.1 %collective-permute-done.4.refs_1_ = f32[4,40,256]{2,1,0:T(8,128)S(1)} collective-permute-done((f32[4,40,256]{2,1,0:T(8,128)S(1)}, f32[4,40,256]{2,1,0:T(8,128)S(1)}, u32[]{:S(2)}, u32[]{:S(2)}) %collective-permute-start.4) | collective-permute-done | bytes 163872 | tf_op jit(solution)/shard_map/ppermute | solution.py:518
  20.5 0.1 collective-permute-start.5
  20.5 1.3 %grams.4.refs_0_ = f32[672,256]{1,0:T(8,128)S(1)} custom-call(f32[672,256]{1,0:T(8,128)S(1)} %grams.3.refs_0_, f32[4,40,256]{2,1,0:T(8,128)S(1)} %collective-permute-done.4.refs_1_, bf16[16,128,256]{2,1,0:T(8,128)(2,1)S(1)} %get-tuple-element.21.refs_1_.refs_2_, bf16[16,128,256]{2,1,0:T(8,128)(2,1)S(1)} %get-tuple-element.22.refs_2_.refs_3_, ...), custom_call_target="tpu_custom_call" | custom-call | flops 2000000000 | bytes 6000000 | tf_op jit(solution)/shard_map/grams/pallas_call | solution.py:273
  21.9 0.3 collective-permute-done.5.refs_1_
  22.1 2.5 %grams.5.gram_ref = f32[672,256]{1,0:T(8,128)S(1)} custom-call(f32[672,256]{1,0:T(8,128)S(1)} %grams.4.refs_0_, f32[8,40,256]{2,1,0:T(8,128)S(1)} %collective-permute-done.5.refs_1_, bf16[16,128,256]{2,1,0:T(8,128)(2,1)S(1)} %get-tuple-element.21.refs_1_.refs_2_, bf16[16,128,256]{2,1,0:T(8,128)(2,1)S(1)} %get-tuple-element.22.refs_2_.refs_3_, ...), custom_call_target="tpu_custom_call" | custom-call | flops 2000000000 | bytes 6000000 | tf_op jit(solution)/shard_map/grams/pallas_call | solution.py:273
  24.7 6.7 %roots.2.own_ref = f32[1024,128]{1,0:T(8,128)S(1)} custom-call(f32[672,256]{1,0:T(8,128)S(1)} %grams.5.gram_ref), custom_call_target="tpu_custom_call" | custom-call | flops 7000000000 | bytes 21000000 | tf_op jit(solution)/shard_map/roots/pallas_call | solution.py:397
  31.4 0.3 collective-permute-start.6
  31.7 6.5 %roots.3.halo_ref = f32[1024,128]{1,0:T(8,128)S(1)} custom-call(f32[672,256]{1,0:T(8,128)S(1)} %grams.5.gram_ref), custom_call_target="tpu_custom_call" | custom-call | flops 7000000000 | bytes 21000000 | tf_op jit(solution)/shard_map/roots/pallas_call | solution.py:397
  38.2 0.3 collective-permute-start.7
  38.5 0.0 collective-permute-done.6.pair_ref
  38.5 2.7 %inner.1.part_ref = f32[2048,128]{1,0:T(8,128)S(1)} custom-call(s32[1]{0:T(128)} %bitcast.gz_ref, f32[2048,128]{1,0:T(8,128)S(1)} %get-tuple-element.17.pert_ref, f32[64,128]{1,0:T(8,128)S(1)} %get-tuple-element.18.mean_ref, f32[1024,128]{1,0:T(8,128)S(1)} %roots.2.own_ref, f32[1024,128]{1,0:T(8,128)S(1)} %collective-permute-done.6.pair_ref, ...), custom_call_target="tpu_custom_call" | custom-call | flops 3000000000 | bytes 9000000 | tf_op jit(solution)/shard_map/inner/pallas_call | solution.py:495
  41.2 0.0 collective-permute-done.7.far_ref
  41.2 1.8 %outer.1 = bf16[32,8,8,128]{3,2,1,0:T(8,128)(2,1)} custom-call(s32[1]{0:T(128)} %bitcast.gz_ref, f32[2048,128]{1,0:T(8,128)S(1)} %get-tuple-element.17.pert_ref, f32[64,128]{1,0:T(8,128)S(1)} %get-tuple-element.18.mean_ref, f32[1024,128]{1,0:T(8,128)S(1)} %collective-permute-done.6.pair_ref, f32[1024,128]{1,0:T(8,128)S(1)} %collective-permute-done.7.far_ref, ...), custom_call_target="tpu_custom_call" | custom-call | flops 1000000000 | bytes 3000000 | tf_op jit(solution)/shard_map/outer/pallas_call | solution.py:504
  (2 shorter events, 0.0 us)
Async XLA Ops:
  3.3 10.2 %collective-permute-start.2 = (f32[40,256]{1,0:T(8,128)}, f32[40,256]{1,0:T(8,128)S(1)}, u32[]{:S(2)}, u32[]{:S(2)}) collective-permute-start(f32[40,256]{1,0:T(8,128)} %get-tuple-element.19), channel_id=1, source_target_pairs={{12,0},{0,4},{4,8},{8,12},{5,1},{9,5},{13,9},{1,13},{14,2},{2,6},{... | collective-permute-start | bytes 122888 | tf_op jit(solution)/shard_map/ppermute | solution.py:525
  6.3 7.2 %collective-permute-start.1 = (f32[40,256]{1,0:T(8,128)}, f32[40,256]{1,0:T(8,128)S(1)}, u32[]{:S(2)}, u32[]{:S(2)}) collective-permute-start(f32[40,256]{1,0:T(8,128)} %get-tuple-element.19), channel_id=1, source_target_pairs={{8,0},{12,4},{0,8},{4,12},{9,1},{13,5},{1,9},{5,13},{10,2},{14,6},... | collective-permute-start | bytes 122888 | tf_op jit(solution)/shard_map/ppermute | solution.py:525
  8.9 4.7 %collective-permute-start = (f32[40,256]{1,0:T(8,128)}, f32[40,256]{1,0:T(8,128)S(1)}, u32[]{:S(2)}, u32[]{:S(2)}) collective-permute-start(f32[40,256]{1,0:T(8,128)} %get-tuple-element.19), channel_id=1, source_target_pairs={{4,0},{8,4},{12,8},{0,12},{13,1},{1,5},{5,9},{9,13},{6,2},{10,6},{... | collective-permute-start | bytes 122888 | tf_op jit(solution)/shard_map/ppermute | solution.py:525
  10.3 6.3 %collective-permute-start.3 = (f32[128,128]{1,0:T(8,128)}, f32[128,128]{1,0:T(8,128)S(1)}, u32[]{:S(2)}, u32[]{:S(2)}) collective-permute-start(f32[128,128]{1,0:T(8,128)} %get-tuple-element.24), channel_id=1, source_target_pairs={{12,0},{0,4},{4,8},{8,12},{5,1},{9,5},{13,9},{1,13},{14,2},{2,6},{... | collective-permute-start | bytes 196616 | tf_op jit(solution)/shard_map/ppermute | solution.py:525
  11.0 0.8 %copy-start.1 = (f32[128,128]{1,0:T(8,128)S(1)}, f32[128,128]{1,0:T(8,128)}, u32[]{:S(2)}) copy-start(f32[128,128]{1,0:T(8,128)} %get-tuple-element.20.list_ref) | copy-start | bytes 196612
  11.8 1.4 %copy-start = (bf16[32,8,8,128]{3,2,1,0:T(8,128)(2,1)S(1)}, bf16[32,8,8,128]{3,2,1,0:T(8,128)(2,1)}, u32[]{:S(2)}) copy-start(bf16[32,8,8,128]{3,2,1,0:T(8,128)(2,1)} %members_in.1) | copy-start | bytes 1572868
  13.2 0.8 %copy-start.2 = (f32[40,256]{1,0:T(8,128)S(1)}, f32[40,256]{1,0:T(8,128)}, u32[]{:S(2)}) copy-start(f32[40,256]{1,0:T(8,128)} %get-tuple-element.19) | copy-start | bytes 122884
  14.0 6.4 %collective-permute-start.4 = (f32[4,40,256]{2,1,0:T(8,128)S(1)}, f32[4,40,256]{2,1,0:T(8,128)S(1)}, u32[]{:S(2)}, u32[]{:S(2)}) collective-permute-start(f32[4,40,256]{2,1,0:T(8,128)S(1)} %pad_maximum_fusion.1.refs_0_), channel_id=1, source_target_pairs={{2,0},{0,2},{3,1},{1,3},{6,4},{4,6},{7,5},{5,7},{10,8},{8,10},{11,... | collective-permute-start | bytes 491528 | tf_op jit(solution)/shard_map/ppermute | solution.py:518
  20.5 1.7 %collective-permute-start.5 = (f32[8,40,256]{2,1,0:T(8,128)S(1)}, f32[8,40,256]{2,1,0:T(8,128)S(1)}, u32[]{:S(2)}, u32[]{:S(2)}) collective-permute-start(f32[8,40,256]{2,1,0:T(8,128)S(1)} %pad_maximum_fusion), channel_id=1, source_target_pairs={{0,1},{1,0},{2,3},{3,2},{4,5},{5,4},{6,7},{7,6},{8,9},{9,8},{10,11... | collective-permute-start | bytes 983048 | tf_op jit(solution)/shard_map/ppermute | solution.py:529
  31.4 7.2 %collective-permute-start.6 = (f32[1024,128]{1,0:T(8,128)S(1)}, f32[1024,128]{1,0:T(8,128)S(1)}, u32[]{:S(2)}, u32[]{:S(2)}) collective-permute-start(f32[1024,128]{1,0:T(8,128)S(1)} %roots.2.own_ref), channel_id=1, source_target_pairs={{0,1},{1,0},{2,3},{3,2},{4,5},{5,4},{6,7},{7,6},{8,9},{9,8},{10,11... | collective-permute-start | bytes 1572872 | tf_op jit(solution)/shard_map/ppermute | solution.py:529
  38.2 3.1 %collective-permute-start.7 = (f32[1024,128]{1,0:T(8,128)S(1)}, f32[1024,128]{1,0:T(8,128)S(1)}, u32[]{:S(2)}, u32[]{:S(2)}) collective-permute-start(f32[1024,128]{1,0:T(8,128)S(1)} %roots.3.halo_ref), channel_id=1, source_target_pairs={{0,1},{1,0},{2,3},{3,2},{4,5},{5,4},{6,7},{7,6},{8,9},{9,8},{10,11... | collective-permute-start | bytes 1572872 | tf_op jit(solution)/shard_map/ppermute | solution.py:529

commit v5 on v4

--- a/solution.py
+++ b/solution.py
@@ -9,6 +9,7 @@
 from jax.sharding import PartitionSpec as P
 
 PX = 4
+PIT = 40
 BATCH = 8
 F32 = jnp.float32
 BF16 = jnp.bfloat16
@@ -292,9 +293,9 @@
             i0 = ib * SUB + step * rows
             acc = [[None] * n for _ in range(rows)]
             for j in range(ens):
-                right = [b[j * ens + SUB * kb : j * ens + SUB * (kb + 1), :] for kb in range(ib, nb)]
+                right = [b[j * PIT + SUB * kb : j * PIT + SUB * (kb + 1), :] for kb in range(ib, nb)]
                 for ii in range(rows):
-                    left = spread(a, (i0 + ii) * ens + j)
+                    left = spread(a, (i0 + ii) * PIT + j)
                     for q in range(n):
                         term = left * right[q]
                         acc[ii][q] = term if j == 0 else acc[ii][q] + term
@@ -304,11 +305,11 @@
                     eye = None
                     if q == 0:
                         eye = lax.broadcasted_iota(jnp.int32, (SUB, LANES), 0) == step * rows + ii
-                    outs = epilogue(acc[ii][q], pl.ds((i0 + ii) * ens + SUB * kb, SUB), eye)
+                    outs = epilogue(acc[ii][q], pl.ds((i0 + ii) * PIT + SUB * kb, SUB), eye)
                     for dest, value in zip(dests, outs):
-                        dest[pl.ds((i0 + ii) * ens + SUB * kb, SUB), :] = value
+                        dest[pl.ds((i0 + ii) * PIT + SUB * kb, SUB), :] = value
                         if kb > ib:
-                            dest[pl.ds(SUB * kb * ens + i0 + ii, SUB, stride=ens), :] = value
+                            dest[pl.ds(SUB * kb * PIT + i0 + ii, SUB, stride=PIT), :] = value
             return 0
 
         lax.fori_loop(0, SUB // rows, body, 0, unroll=True)
@@ -332,9 +333,9 @@
             if kb == i // SUB:
                 value = jnp.where(iota == i % SUB, value + (ens - 1.0), value)
             value = value * scale
-            s_a[i * ens + SUB * kb : i * ens + SUB * (kb + 1), :] = value
+            s_a[i * PIT + SUB * kb : i * PIT + SUB * (kb + 1), :] = value
             if kb > i // SUB:
-                s_a[pl.ds(SUB * kb * ens + i, SUB, stride=ens), :] = value
+                s_a[pl.ds(SUB * kb * PIT + i, SUB, stride=PIT), :] = value
 
     def plain(acc, at, eye):
         return (acc,)
@@ -362,10 +363,10 @@
     product(ens, s_d, s_d, (s_b,), plain)
     product(ens, s_a, s_b, (s_c,), plain)
     product(ens, s_c, s_c, (s_a, s_b), quadratic(s_c))
-    product(ens, s_a, s_b, (vec.at[pl.ds(0, ens * ens)],), quartic(s_c))
-    product(ens, s_d, vec.at[pl.ds(0, ens * ens)], (s_a,), plain)
-
-    right = ens * ens
+    product(ens, s_a, s_b, (vec.at[pl.ds(0, ens * PIT)],), quartic(s_c))
+    product(ens, s_d, vec.at[pl.ds(0, ens * PIT)], (s_a,), plain)
+
+    right = ens * PIT
     vec[right : right + ens, :] = gram_ref[tri : tri + ens, lanes]
 
     def apply(source):
@@ -373,7 +374,7 @@
         for i in range(ens):
             left = spread(vec, source + i)
             for kb in range(nb):
-                term = left * s_a[i * ens + SUB * kb : i * ens + SUB * (kb + 1), :]
+                term = left * s_a[i * PIT + SUB * kb : i * PIT + SUB * (kb + 1), :]
                 sums[kb] = term if i == 0 else sums[kb] + term
         return sums
 
@@ -387,19 +388,19 @@
     for j in range(ens):
         weight = spread(vec, right + j)
         for kb in range(nb):
-            at = slice(j * ens + SUB * kb, j * ens + SUB * (kb + 1))
-            out_ref[at, :] = weight + s_a[at, :] * factor
+            at = slice(j * PIT + SUB * kb, j * PIT + SUB * (kb + 1))
+            out_ref[j * ens + SUB * kb : j * ens + SUB * (kb + 1), :] = weight + s_a[at, :] * factor
 
 
 def roots(gram, row, ens):
-    square = pltpu.VMEM((ens * ens, LANES), F32)
+    square = pltpu.VMEM((ens * PIT, LANES), F32)
     vmem = pl.BlockSpec(memory_space=pltpu.VMEM)
     return pl.pallas_call(
         functools.partial(root_kernel, ens=ens, row=row),
         out_shape=jax.ShapeDtypeStruct((ens * ens, LANES), F32),
         in_specs=[vmem],
         out_specs=vmem,
-        scratch_shapes=[square] * 4 + [pltpu.VMEM((ens * ens + 2 * ens, LANES), F32)],
+        scratch_shapes=[square] * 4 + [pltpu.VMEM((ens * PIT + 2 * ens, LANES), F32)],
         compiler_params=params(),
         cost_estimate=micros(7),
         name="roots",
@@ -440,6 +441,7 @@
 def columns(gz, pert_ref, mean_ref, dest, main_ref, beside_ref, first, ens, levels, width_x):
     nb = ens // SUB
     near = first % PX
+    step_k = levels * width_x + SUB
 
     def body(step, _):
         place = jnp.abs((near + step + 0.5) / PX - 0.5)
@@ -459,8 +461,8 @@
                     acc[level][kb] = acc[level][kb] + pert * blend[kb]
         for level in range(levels):
             for kb in range(nb):
-                at = (SUB * kb * levels + level) * width_x + x
-                dest[pl.ds(at, SUB, stride=levels * width_x), :] = acc[level][kb]
+                at = SUB * kb * step_k + level * width_x + x
+                dest[pl.ds(at, SUB, stride=step_k), :] = acc[level][kb]
         return 0
 
     lax.fori_loop(0, PX // 2, body, 0)
@@ -478,12 +480,13 @@
     ens, levels, width_x, width_y = out_ref.shape
     gz = gz_ref[0]
     first = 3 * PX // 2
+    step_k = levels * width_x + SUB
     columns(gz, pert_ref, mean_ref, rest_s, pair_ref, far_ref, first, ens, levels, width_x)
     x = lax.broadcasted_iota(jnp.int32, (width_x, width_y), 0)
     inside = jnp.where(gz == 0, x, width_x - 1 - x) < first
     for k in range(ens):
         for level in range(levels):
-            at = slice((k * levels + level) * width_x, (k * levels + level + 1) * width_x)
+            at = slice(k * step_k + level * width_x, k * step_k + (level + 1) * width_x)
             out_ref[k, level] = jnp.where(inside, part_ref[at, :], rest_s[at, :]).astype(BF16)
 
 
@@ -494,7 +497,7 @@
     smem = pl.BlockSpec(memory_space=pltpu.SMEM)
     part = pl.pallas_call(
         functools.partial(inner_kernel, ens=ens, levels=levels, width_x=width_x),
-        out_shape=jax.ShapeDtypeStruct(pert.shape, F32),
+        out_shape=jax.ShapeDtypeStruct((ens * (levels * width_x + SUB), width_y), F32),
         in_specs=[smem] + [vmem] * 5,
         out_specs=vmem,
         compiler_params=params(),
@@ -506,7 +509,7 @@
         out_shape=jax.ShapeDtypeStruct(shape, BF16),
         in_specs=[smem] + [vmem] * 5,
         out_specs=vmem,
-        scratch_shapes=[pltpu.VMEM(pert.shape, F32)],
+        scratch_shapes=[pltpu.VMEM((ens * (levels * width_x + SUB), width_y), F32)],
         compiler_params=params(),
         cost_estimate=micros(1),
         name="outer",

time: 43.3 us -> 40.2 us (0.928)
  Pallas kernels: 28.5 us -> 25.5 us
    pallas_call x2, Pallas kernels: 13.2 us -> 10.4 us  [roots(): pl.pallas_call(functools.partial(root_kernel, ens=ens, row=row), out_shap...]
  transfers between devices with their start and end apart: 8 -> 8, of which waited for: 4 -> 4; matrix products, arithmetic and copies ran while one was open for 0% -> 0% of each run, Pallas kernels for 35% -> 33%
where the time goes in v5:
time: 40.2 us; the launch traced here: 40 us
  Pallas kernels  25.5 us (63%)
  starting transfers between devices  9.95 us (25%)
  waiting for transfers between devices  2.5 us (6%)
  local copies, waits for them, and re-layouts  1.23 us (3%)
  between operations  0.79 us (2%)
    pallas_call x2, Pallas kernels, roots(): pl.pallas_call(functools.partial(root_kernel, ens=ens, row=row), out_shap...  10.4 us
    ppermute x4, starting transfers between devices, turned(): return lax.ppermute(x, ('gx', 'gz'), pairs)  7.69 us
    pallas_call x3, Pallas kernels, grams(): pl.pallas_call(functools.partial(gram_kernel, ens=ens, bufs=tuple(bufs),...  5.18 us
    pallas_call x2, Pallas kernels, dense_tapers(): pl.pallas_call(functools.partial(taper_kernel, shift=shift, n_x=n_x, n_y=...  2.85 us
    pallas_call x1, Pallas kernels, observe(): pl.pallas_call(observe_kernel, out_shape=(jax.ShapeDtypeStruct((ens + SUB...  2.6 us
    pallas_call x1, Pallas kernels, update(): pl.pallas_call(functools.partial(inner_kernel, ens=ens, levels=levels, wi...  2.46 us
    pallas_call x1, Pallas kernels, update(): pl.pallas_call(outer_kernel, out_shape=jax.ShapeDtypeStruct(shape, BF16),...  1.72 us
    ppermute x1, starting transfers between devices, shifted(): return lax.ppermute(x, axis, [((i + shift) % size, i) for i in range(size)])  1.54 us
  transfers between devices with their start and end apart: 8, of which 4 were waited for; matrix products, arithmetic and copies ran while one was open for 0% of the time, Pallas kernels for 33%

profile of v5, /device:TPU:0, one launch (start us, length us, event | category | flops | bytes accessed | tf_op | source)
XLA Modules:
  0.0 40.0 jit_solution(12786121843941978235)
XLA Ops:
  0.7 2.6 %observe.1 = (f32[40,256]{1,0:T(8,128)}, f32[128,128]{1,0:T(8,128)}, f32[128,128]{1,0:T(8,128)}) custom-call(s32[1]{0:T(128)} %bitcast.gz_ref, s32[1]{0:T(128)} %bitcast.12.count_ref, bf16[32,8,8,128]{3,2,1,0:T(8,128)(2,1)} %members_in.1, s32[8,256]{1,0:T(8,128)} %bitcast.19, f32[8,256]{1,0:T(8,128)} %bitcast.20, f32[1,256]{1,0:T(1,128)} %bitcast.21, ...), custom_call_target="tpu_custom_call" | custom-call | flops 3000000000 | bytes 9000000 | tf_op jit(solution)/shard_map/observe/pallas_call | solution.py:128
  3.3 3.1 %collective-permute-start.2 = (f32[40,256]{1,0:T(8,128)}, f32[40,256]{1,0:T(8,128)S(1)}, u32[]{:S(2)}, u32[]{:S(2)}) collective-permute-start(f32[40,256]{1,0:T(8,128)} %get-tuple-element.19), channel_id=1, source_target_pairs={{12,0},{0,4},{4,8},{8,12},{5,1},{9,5},{13,9},{1,13},{14,2},{2,6},{... | collective-permute-start | bytes 122888 | tf_op jit(solution)/shard_map/ppermute | solution.py:528
  6.3 2.6 %collective-permute-start.1 = (f32[40,256]{1,0:T(8,128)}, f32[40,256]{1,0:T(8,128)S(1)}, u32[]{:S(2)}, u32[]{:S(2)}) collective-permute-start(f32[40,256]{1,0:T(8,128)} %get-tuple-element.19), channel_id=1, source_target_pairs={{8,0},{12,4},{0,8},{4,12},{9,1},{13,5},{1,9},{5,13},{10,2},{14,6},... | collective-permute-start | bytes 122888 | tf_op jit(solution)/shard_map/ppermute | solution.py:528
  8.9 1.3 %collective-permute-start = (f32[40,256]{1,0:T(8,128)}, f32[40,256]{1,0:T(8,128)S(1)}, u32[]{:S(2)}, u32[]{:S(2)}) collective-permute-start(f32[40,256]{1,0:T(8,128)} %get-tuple-element.19), channel_id=1, source_target_pairs={{4,0},{8,4},{12,8},{0,12},{13,1},{1,5},{5,9},{9,13},{6,2},{10,6},{... | collective-permute-start | bytes 122888 | tf_op jit(solution)/shard_map/ppermute | solution.py:528
  10.3 0.7 %collective-permute-start.3 = (f32[128,128]{1,0:T(8,128)}, f32[128,128]{1,0:T(8,128)S(1)}, u32[]{:S(2)}, u32[]{:S(2)}) collective-permute-start(f32[128,128]{1,0:T(8,128)} %get-tuple-element.24), channel_id=1, source_target_pairs={{12,0},{0,4},{4,8},{8,12},{5,1},{9,5},{13,9},{1,13},{14,2},{2,6},{... | collective-permute-start | bytes 196616 | tf_op jit(solution)/shard_map/ppermute | solution.py:528
  11.0 0.0 copy-start.1
  11.0 0.8 %copy-done.1 = f32[128,128]{1,0:T(8,128)S(1)} copy-done((f32[128,128]{1,0:T(8,128)S(1)}, f32[128,128]{1,0:T(8,128)}, u32[]{:S(2)}) %copy-start.1) | copy-done | bytes 65560
  11.8 0.0 copy-start
  11.8 1.4 %dense_tapers.2 = (bf16[16,128,256]{2,1,0:T(8,128)(2,1)S(1)}, bf16[16,128,256]{2,1,0:T(8,128)(2,1)S(1)}) custom-call(s32[1]{0:T(128)} %bitcast.gz_ref, f32[128,128]{1,0:T(8,128)S(1)} %copy-done.1), custom_call_target="tpu_custom_call" | custom-call | flops 3000000000 | bytes 9000000 | tf_op jit(solution)/shard_map/dense_tapers/pallas_call | solution.py:214
  13.2 0.0 copy-done
  13.2 0.0 copy-start.2
  13.3 0.2 center.1
  13.5 0.0 collective-permute-done.2
  13.5 0.0 collective-permute-done.1
  13.5 0.1 collective-permute-done
  13.6 0.4 copy-done.2
  14.0 1.5 %collective-permute-start.4 = (f32[4,40,256]{2,1,0:T(8,128)S(1)}, f32[4,40,256]{2,1,0:T(8,128)S(1)}, u32[]{:S(2)}, u32[]{:S(2)}) collective-permute-start(f32[4,40,256]{2,1,0:T(8,128)S(1)} %pad_maximum_fusion.1.refs_0_), channel_id=1, source_target_pairs={{2,0},{0,2},{3,1},{1,3},{6,4},{4,6},{7,5},{5,7},{10,8},{8,10},{11,... | collective-permute-start | bytes 491528 | tf_op jit(solution)/shard_map/ppermute | solution.py:521
  15.6 1.0 %collective-permute-done.3.list_ref = f32[128,128]{1,0:T(8,128)S(1)} collective-permute-done((f32[128,128]{1,0:T(8,128)}, f32[128,128]{1,0:T(8,128)S(1)}, u32[]{:S(2)}, u32[]{:S(2)}) %collective-permute-start.3) | collective-permute-done | bytes 65568 | tf_op jit(solution)/shard_map/ppermute | solution.py:528
  16.6 1.4 %dense_tapers.3 = (bf16[16,128,256]{2,1,0:T(8,128)(2,1)S(1)}, bf16[16,128,256]{2,1,0:T(8,128)(2,1)S(1)}) custom-call(s32[1]{0:T(128)} %bitcast.gz_ref, f32[128,128]{1,0:T(8,128)S(1)} %collective-permute-done.3.list_ref), custom_call_target="tpu_custom_call" | custom-call | flops 3000000000 | bytes 9000000 | tf_op jit(solution)/shard_map/dense_tapers/pallas_call | solution.py:214
  18.0 1.3 %grams.3.refs_0_ = f32[672,256]{1,0:T(8,128)S(1)} custom-call(f32[4,40,256]{2,1,0:T(8,128)S(1)} %pad_maximum_fusion.1.refs_0_, bf16[16,128,256]{2,1,0:T(8,128)(2,1)S(1)} %get-tuple-element.21.refs_1_.refs_2_, bf16[16,128,256]{2,1,0:T(8,128)(2,1)S(1)} %get-tuple-element.22.refs_2_.refs_3_, bf16[16,128,256]{2,1,0:T(8,128)(2,1)S(1)} %get-tuple-element.25.refs_3_.refs_4_, ...), custom_call_target="tpu_custom_call" | custom-call | flops 2000000000 | bytes 6000000 | tf_op jit(solution)/shard_map/grams/pallas_call | solution.py:274
  19.3 1.1 %collective-permute-done.4.refs_1_ = f32[4,40,256]{2,1,0:T(8,128)S(1)} collective-permute-done((f32[4,40,256]{2,1,0:T(8,128)S(1)}, f32[4,40,256]{2,1,0:T(8,128)S(1)}, u32[]{:S(2)}, u32[]{:S(2)}) %collective-permute-start.4) | collective-permute-done | bytes 163872 | tf_op jit(solution)/shard_map/ppermute | solution.py:521
  20.5 0.1 collective-permute-start.5
  20.5 1.3 %grams.4.refs_0_ = f32[672,256]{1,0:T(8,128)S(1)} custom-call(f32[672,256]{1,0:T(8,128)S(1)} %grams.3.refs_0_, f32[4,40,256]{2,1,0:T(8,128)S(1)} %collective-permute-done.4.refs_1_, bf16[16,128,256]{2,1,0:T(8,128)(2,1)S(1)} %get-tuple-element.21.refs_1_.refs_2_, bf16[16,128,256]{2,1,0:T(8,128)(2,1)S(1)} %get-tuple-element.22.refs_2_.refs_3_, ...), custom_call_target="tpu_custom_call" | custom-call | flops 2000000000 | bytes 6000000 | tf_op jit(solution)/shard_map/grams/pallas_call | solution.py:274
  21.9 0.3 collective-permute-done.5.refs_1_
  22.1 2.5 %grams.5.gram_ref = f32[672,256]{1,0:T(8,128)S(1)} custom-call(f32[672,256]{1,0:T(8,128)S(1)} %grams.4.refs_0_, f32[8,40,256]{2,1,0:T(8,128)S(1)} %collective-permute-done.5.refs_1_, bf16[16,128,256]{2,1,0:T(8,128)(2,1)S(1)} %get-tuple-element.21.refs_1_.refs_2_, bf16[16,128,256]{2,1,0:T(8,128)(2,1)S(1)} %get-tuple-element.22.refs_2_.refs_3_, ...), custom_call_target="tpu_custom_call" | custom-call | flops 2000000000 | bytes 6000000 | tf_op jit(solution)/shard_map/grams/pallas_call | solution.py:274
  24.7 5.3 %roots.2.own_ref = f32[1024,128]{1,0:T(8,128)S(1)} custom-call(f32[672,256]{1,0:T(8,128)S(1)} %grams.5.gram_ref), custom_call_target="tpu_custom_call" | custom-call | flops 7000000000 | bytes 21000000 | tf_op jit(solution)/shard_map/roots/pallas_call | solution.py:398
  30.0 0.3 collective-permute-start.6
  30.3 5.1 %roots.3.halo_ref = f32[1024,128]{1,0:T(8,128)S(1)} custom-call(f32[672,256]{1,0:T(8,128)S(1)} %grams.5.gram_ref), custom_call_target="tpu_custom_call" | custom-call | flops 7000000000 | bytes 21000000 | tf_op jit(solution)/shard_map/roots/pallas_call | solution.py:398
  35.4 0.3 collective-permute-start.7
  35.8 0.0 collective-permute-done.6.pair_ref
  35.8 2.5 %inner.1.part_ref = f32[2304,128]{1,0:T(8,128)S(1)} custom-call(s32[1]{0:T(128)} %bitcast.gz_ref, f32[2048,128]{1,0:T(8,128)S(1)} %get-tuple-element.17.pert_ref, f32[64,128]{1,0:T(8,128)S(1)} %get-tuple-element.18.mean_ref, f32[1024,128]{1,0:T(8,128)S(1)} %roots.2.own_ref, f32[1024,128]{1,0:T(8,128)S(1)} %collective-permute-done.6.pair_ref, ...), custom_call_target="tpu_custom_call" | custom-call | flops 3000000000 | bytes 9000000 | tf_op jit(solution)/shard_map/inner/pallas_call | solution.py:498
  38.2 0.0 collective-permute-done.7.far_ref
  38.2 1.7 %outer.1 = bf16[32,8,8,128]{3,2,1,0:T(8,128)(2,1)} custom-call(s32[1]{0:T(128)} %bitcast.gz_ref, f32[2048,128]{1,0:T(8,128)S(1)} %get-tuple-element.17.pert_ref, f32[64,128]{1,0:T(8,128)S(1)} %get-tuple-element.18.mean_ref, f32[1024,128]{1,0:T(8,128)S(1)} %collective-permute-done.6.pair_ref, f32[1024,128]{1,0:T(8,128)S(1)} %collective-permute-done.7.far_ref, ...), custom_call_target="tpu_custom_call" | custom-call | flops 1000000000 | bytes 3000000 | tf_op jit(solution)/shard_map/outer/pallas_call | solution.py:507
  (2 shorter events, 0.0 us)
Async XLA Ops:
  3.3 10.2 %collective-permute-start.2 = (f32[40,256]{1,0:T(8,128)}, f32[40,256]{1,0:T(8,128)S(1)}, u32[]{:S(2)}, u32[]{:S(2)}) collective-permute-start(f32[40,256]{1,0:T(8,128)} %get-tuple-element.19), channel_id=1, source_target_pairs={{12,0},{0,4},{4,8},{8,12},{5,1},{9,5},{13,9},{1,13},{14,2},{2,6},{... | collective-permute-start | bytes 122888 | tf_op jit(solution)/shard_map/ppermute | solution.py:528
  6.3 7.2 %collective-permute-start.1 = (f32[40,256]{1,0:T(8,128)}, f32[40,256]{1,0:T(8,128)S(1)}, u32[]{:S(2)}, u32[]{:S(2)}) collective-permute-start(f32[40,256]{1,0:T(8,128)} %get-tuple-element.19), channel_id=1, source_target_pairs={{8,0},{12,4},{0,8},{4,12},{9,1},{13,5},{1,9},{5,13},{10,2},{14,6},... | collective-permute-start | bytes 122888 | tf_op jit(solution)/shard_map/ppermute | solution.py:528
  8.9 4.7 %collective-permute-start = (f32[40,256]{1,0:T(8,128)}, f32[40,256]{1,0:T(8,128)S(1)}, u32[]{:S(2)}, u32[]{:S(2)}) collective-permute-start(f32[40,256]{1,0:T(8,128)} %get-tuple-element.19), channel_id=1, source_target_pairs={{4,0},{8,4},{12,8},{0,12},{13,1},{1,5},{5,9},{9,13},{6,2},{10,6},{... | collective-permute-start | bytes 122888 | tf_op jit(solution)/shard_map/ppermute | solution.py:528
  10.3 6.3 %collective-permute-start.3 = (f32[128,128]{1,0:T(8,128)}, f32[128,128]{1,0:T(8,128)S(1)}, u32[]{:S(2)}, u32[]{:S(2)}) collective-permute-start(f32[128,128]{1,0:T(8,128)} %get-tuple-element.24), channel_id=1, source_target_pairs={{12,0},{0,4},{4,8},{8,12},{5,1},{9,5},{13,9},{1,13},{14,2},{2,6},{... | collective-permute-start | bytes 196616 | tf_op jit(solution)/shard_map/ppermute | solution.py:528
  11.0 0.8 %copy-start.1 = (f32[128,128]{1,0:T(8,128)S(1)}, f32[128,128]{1,0:T(8,128)}, u32[]{:S(2)}) copy-start(f32[128,128]{1,0:T(8,128)} %get-tuple-element.20.list_ref) | copy-start | bytes 196612
  11.8 1.4 %copy-start = (bf16[32,8,8,128]{3,2,1,0:T(8,128)(2,1)S(1)}, bf16[32,8,8,128]{3,2,1,0:T(8,128)(2,1)}, u32[]{:S(2)}) copy-start(bf16[32,8,8,128]{3,2,1,0:T(8,128)(2,1)} %members_in.1) | copy-start | bytes 1572868
  13.2 0.8 %copy-start.2 = (f32[40,256]{1,0:T(8,128)S(1)}, f32[40,256]{1,0:T(8,128)}, u32[]{:S(2)}) copy-start(f32[40,256]{1,0:T(8,128)} %get-tuple-element.19) | copy-start | bytes 122884
  14.0 6.4 %collective-permute-start.4 = (f32[4,40,256]{2,1,0:T(8,128)S(1)}, f32[4,40,256]{2,1,0:T(8,128)S(1)}, u32[]{:S(2)}, u32[]{:S(2)}) collective-permute-start(f32[4,40,256]{2,1,0:T(8,128)S(1)} %pad_maximum_fusion.1.refs_0_), channel_id=1, source_target_pairs={{2,0},{0,2},{3,1},{1,3},{6,4},{4,6},{7,5},{5,7},{10,8},{8,10},{11,... | collective-permute-start | bytes 491528 | tf_op jit(solution)/shard_map/ppermute | solution.py:521
  20.5 1.7 %collective-permute-start.5 = (f32[8,40,256]{2,1,0:T(8,128)S(1)}, f32[8,40,256]{2,1,0:T(8,128)S(1)}, u32[]{:S(2)}, u32[]{:S(2)}) collective-permute-start(f32[8,40,256]{2,1,0:T(8,128)S(1)} %pad_maximum_fusion), channel_id=1, source_target_pairs={{0,1},{1,0},{2,3},{3,2},{4,5},{5,4},{6,7},{7,6},{8,9},{9,8},{10,11... | collective-permute-start | bytes 983048 | tf_op jit(solution)/shard_map/ppermute | solution.py:532
  30.0 5.8 %collective-permute-start.6 = (f32[1024,128]{1,0:T(8,128)S(1)}, f32[1024,128]{1,0:T(8,128)S(1)}, u32[]{:S(2)}, u32[]{:S(2)}) collective-permute-start(f32[1024,128]{1,0:T(8,128)S(1)} %roots.2.own_ref), channel_id=1, source_target_pairs={{0,1},{1,0},{2,3},{3,2},{4,5},{5,4},{6,7},{7,6},{8,9},{9,8},{10,11... | collective-permute-start | bytes 1572872 | tf_op jit(solution)/shard_map/ppermute | solution.py:532
  35.4 2.8 %collective-permute-start.7 = (f32[1024,128]{1,0:T(8,128)S(1)}, f32[1024,128]{1,0:T(8,128)S(1)}, u32[]{:S(2)}, u32[]{:S(2)}) collective-permute-start(f32[1024,128]{1,0:T(8,128)S(1)} %roots.3.halo_ref), channel_id=1, source_target_pairs={{0,1},{1,0},{2,3},{3,2},{4,5},{5,4},{6,7},{7,6},{8,9},{9,8},{10,11... | collective-permute-start | bytes 1572872 | tf_op jit(solution)/shard_map/ppermute | solution.py:532

commit v6 on v5

--- a/solution.py
+++ b/solution.py
@@ -111,12 +111,20 @@
         total = total + group
     mean = jnp.sum(total, axis=0, keepdims=True) / ens
     for kb in range(ens // SUB):
-        out_ref[kb * SUB : (kb + 1) * SUB, :] = groups[kb] - mean
+        pert = groups[kb] - mean
+        for half in range(slots // LANES):
+            at = half * ens + kb * SUB
+            out_ref[at : at + SUB, :] = pert[:, half * LANES : (half + 1) * LANES]
     live = lax.broadcasted_iota(jnp.int32, (1, slots), 1) < count_ref[0]
     innovation = value_ref[...] - mean
     rinv = jnp.where(live, rinv_ref[...], 0.0)
-    row = lax.broadcasted_iota(jnp.int32, (SUB, slots), 0)
-    out_ref[ens : ens + SUB, :] = jnp.where(row == 0, innovation, jnp.where(row == 1, rinv, 0.0))
+    row = lax.broadcasted_iota(jnp.int32, (SUB, LANES), 0)
+    last = jnp.zeros((SUB, LANES), F32)
+    for n, vector in enumerate((innovation, rinv)):
+        for half in range(slots // LANES):
+            lanes = vector[:, half * LANES : (half + 1) * LANES]
+            last = jnp.where(row == n * (slots // LANES) + half, lanes, last)
+    out_ref[slots // LANES * ens :, :] = last
 
 
 def observe(gz, count, members, cell, weight, value, rinv, ids, tapers):
@@ -128,7 +136,7 @@
     return pl.pallas_call(
         observe_kernel,
         out_shape=(
-            jax.ShapeDtypeStruct((ens + SUB, slots), F32),
+            jax.ShapeDtypeStruct((slots // LANES * ens + SUB, LANES), F32),
             jax.ShapeDtypeStruct((patches, 2 * mloc), F32),
             jax.ShapeDtypeStruct((patches, 2 * mloc), F32),
         ),
@@ -236,10 +244,13 @@
     rows = tri + ens
     nt = (((1,), (1,)), ((), ()))
     for t, n in enumerate(bufs):
-        ob = stack[t, :ens, :]
-        rinv = stack[t, ens + 1 : ens + 2, :]
+        parts = zr_s.shape[1] // LANES
+        ob = jnp.concatenate([stack[t, q * ens : (q + 1) * ens, :] for q in range(parts)], axis=1)
+        wi, rinv = [
+            jnp.concatenate([stack[t, ens * parts + n + q : ens * parts + n + q + 1, :] for q in range(parts)], axis=1)
+            for n in (0, parts)
+        ]
         zr_s[...] = ob * rinv
-        wi = stack[t, ens : ens + 1, :]
         for i in range(0, ens, 2):
             ib = i // SUB
             part = jnp.concatenate(
@@ -476,7 +487,7 @@
     columns(gz, pert_ref, mean_ref, part_ref, pair_ref, own_ref, PX, *sizes)
 
 
-def outer_kernel(gz_ref, pert_ref, mean_ref, pair_ref, far_ref, part_ref, out_ref, rest_s):
+def outer_kernel(gz_ref, pert_ref, mean_ref, pair_ref, far_ref, part_ref, out_hbm, rest_s, out_ref, sems):
     ens, levels, width_x, width_y = out_ref.shape
     gz = gz_ref[0]
     first = 3 * PX // 2
@@ -484,10 +495,17 @@
     columns(gz, pert_ref, mean_ref, rest_s, pair_ref, far_ref, first, ens, levels, width_x)
     x = lax.broadcasted_iota(jnp.int32, (width_x, width_y), 0)
     inside = jnp.where(gz == 0, x, width_x - 1 - x) < first
-    for k in range(ens):
-        for level in range(levels):
-            at = slice(k * step_k + level * width_x, k * step_k + (level + 1) * width_x)
-            out_ref[k, level] = jnp.where(inside, part_ref[at, :], rest_s[at, :]).astype(BF16)
+    copies = []
+    for kb in range(ens // SUB):
+        members = pl.ds(kb * SUB, SUB)
+        for k in range(kb * SUB, (kb + 1) * SUB):
+            for level in range(levels):
+                at = slice(k * step_k + level * width_x, k * step_k + (level + 1) * width_x)
+                out_ref[k, level] = jnp.where(inside, part_ref[at, :], rest_s[at, :]).astype(BF16)
+        copies.append(pltpu.make_async_copy(out_ref.at[members], out_hbm.at[members], sems.at[kb]))
+        copies[-1].start()
+    for copy in copies:
+        copy.wait()
 
 
 def update(gz, shape, centred, own, pair, halo, far):
@@ -508,8 +526,12 @@
         outer_kernel,
         out_shape=jax.ShapeDtypeStruct(shape, BF16),
         in_specs=[smem] + [vmem] * 5,
-        out_specs=vmem,
-        scratch_shapes=[pltpu.VMEM((ens * (levels * width_x + SUB), width_y), F32)],
+        out_specs=pl.BlockSpec(memory_space=pltpu.HBM),
+        scratch_shapes=[
+            pltpu.VMEM((ens * (levels * width_x + SUB), width_y), F32),
+            pltpu.VMEM(shape, BF16),
+            pltpu.SemaphoreType.DMA((ens // SUB,)),
+        ],
         compiler_params=params(),
         cost_estimate=micros(1),
         name="outer",
@@ -560,18 +582,17 @@
         jnp.swapaxes(patch_list, 1, 2),
         jnp.swapaxes(patch_taper, 1, 2),
     )
-    rows = ens + SUB
     along = [packet] + [turned(packet, signed(x, n_x)) for x in range(1, n_x)]
     halo_list = turned(sent, -1)
     own_tapers = dense_tapers(gz, own_list, 0, patches, mloc, n_x, n_y, slots)
     along = jnp.stack(along, axis=0)
-    centred = center(members)
-    along = after(along, *own_tapers, *centred)
+    along = after(along, *own_tapers)
     beside = [shifted(along, "gy", signed(y, n_y)) for y in range(1, n_y)]
+    centred = center(after(members, along))
     halo_tapers = dense_tapers(gz, halo_list, -1, patches, mloc, n_x, n_y, slots)
     tapers = own_tapers + halo_tapers
     gram = grams(along, tapers, ens, range(n_x))
-    here = jnp.concatenate([along] + after(beside, gram), axis=0)
+    here = jnp.concatenate([along] + after(beside, gram, *centred), axis=0)
     there = swapped(here)
     if n_y > 1:
         gram = grams(here[n_x:], tapers, ens, range(n_x, n_x * n_y), gram)

time: 40.2 us -> 39.1 us (0.973)
  waiting for transfers between devices: 2.5 us -> 1.76 us
    ppermute x1, waiting for transfers between devices: 1.11 us -> 0.04 us  [shifted(): return lax.ppermute(x, axis, [((i + shift) % size, i) for i in range(size)])]
  transfers between devices with their start and end apart: 8 -> 8, of which waited for: 4 -> 3; matrix products, arithmetic and copies ran while one was open for 0% -> 0% of each run, Pallas kernels for 33% -> 34%
where the time goes in v6:
time: 39.1 us; the launch traced here: 38.9 us
  Pallas kernels  25.4 us (65%)
  starting transfers between devices  9.97 us (25%)
  waiting for transfers between devices  1.76 us (5%)
  between operations  0.93 us (2%)
  local copies, waits for them, and re-layouts  0.85 us (2%)
    pallas_call x2, Pallas kernels, roots(): pl.pallas_call(functools.partial(root_kernel, ens=ens, row=row), out_shap...  10.4 us
    ppermute x4, starting transfers between devices, turned(): return lax.ppermute(x, ('gx', 'gz'), pairs)  7.69 us
    pallas_call x3, Pallas kernels, grams(): pl.pallas_call(functools.partial(gram_kernel, ens=ens, bufs=tuple(bufs),...  5.17 us
    pallas_call x2, Pallas kernels, dense_tapers(): pl.pallas_call(functools.partial(taper_kernel, shift=shift, n_x=n_x, n_y=...  2.84 us
    pallas_call x1, Pallas kernels, observe(): pl.pallas_call(observe_kernel, out_shape=(jax.ShapeDtypeStruct((slots //...  2.6 us
    pallas_call x1, Pallas kernels, update(): pl.pallas_call(functools.partial(inner_kernel, ens=ens, levels=levels, wi...  2.46 us
    pallas_call x1, Pallas kernels, update(): pl.pallas_call(outer_kernel, out_shape=jax.ShapeDtypeStruct(shape, BF16),...  1.67 us
    ppermute x1, starting transfers between devices, shifted(): return lax.ppermute(x, axis, [((i + shift) % size, i) for i in range(size)])  1.56 us
  transfers between devices with their start and end apart: 8, of which 3 were waited for; matrix products, arithmetic and copies ran while one was open for 0% of the time, Pallas kernels for 34%

profile of v6, /device:TPU:0, one launch (start us, length us, event | category | flops | bytes accessed | tf_op | source)
XLA Modules:
  0.0 38.9 jit_solution(15530192118182704678)
XLA Ops:
  0.7 2.6 %observe.1 = (f32[72,128]{1,0:T(8,128)}, f32[128,128]{1,0:T(8,128)}, f32[128,128]{1,0:T(8,128)}) custom-call(s32[1]{0:T(128)} %bitcast.gz_ref, s32[1]{0:T(128)} %bitcast.12.count_ref, bf16[32,8,8,128]{3,2,1,0:T(8,128)(2,1)} %members_ref, s32[8,256]{1,0:T(8,128)} %bitcast.19, f32[8,256]{1,0:T(8,128)} %bitcast.20, f32[1,256]{1,0:T(1,128)} %bitcast.21, ...), custom_call_target="tpu_custom_call" | custom-call | flops 3000000000 | bytes 9000000 | tf_op jit(solution)/shard_map/observe/pallas_call | solution.py:136
  3.3 3.1 %collective-permute-start.2 = (f32[72,128]{1,0:T(8,128)}, f32[72,128]{1,0:T(8,128)S(1)}, u32[]{:S(2)}, u32[]{:S(2)}) collective-permute-start(f32[72,128]{1,0:T(8,128)} %get-tuple-element.18), channel_id=1, source_target_pairs={{12,0},{0,4},{4,8},{8,12},{5,1},{9,5},{13,9},{1,13},{14,2},{2,6},{... | collective-permute-start | bytes 110600 | tf_op jit(solution)/shard_map/ppermute | solution.py:550
  6.3 2.6 %collective-permute-start.1 = (f32[72,128]{1,0:T(8,128)}, f32[72,128]{1,0:T(8,128)S(1)}, u32[]{:S(2)}, u32[]{:S(2)}) collective-permute-start(f32[72,128]{1,0:T(8,128)} %get-tuple-element.18), channel_id=1, source_target_pairs={{8,0},{12,4},{0,8},{4,12},{9,1},{13,5},{1,9},{5,13},{10,2},{14,6},... | collective-permute-start | bytes 110600 | tf_op jit(solution)/shard_map/ppermute | solution.py:550
  8.9 1.3 %collective-permute-start = (f32[72,128]{1,0:T(8,128)}, f32[72,128]{1,0:T(8,128)S(1)}, u32[]{:S(2)}, u32[]{:S(2)}) collective-permute-start(f32[72,128]{1,0:T(8,128)} %get-tuple-element.18), channel_id=1, source_target_pairs={{4,0},{8,4},{12,8},{0,12},{13,1},{1,5},{5,9},{9,13},{6,2},{10,6},{... | collective-permute-start | bytes 110600 | tf_op jit(solution)/shard_map/ppermute | solution.py:550
  10.3 0.7 %collective-permute-start.3 = (f32[128,128]{1,0:T(8,128)}, f32[128,128]{1,0:T(8,128)S(1)}, u32[]{:S(2)}, u32[]{:S(2)}) collective-permute-start(f32[128,128]{1,0:T(8,128)} %get-tuple-element.26), channel_id=1, source_target_pairs={{12,0},{0,4},{4,8},{8,12},{5,1},{9,5},{13,9},{1,13},{14,2},{2,6},{... | collective-permute-start | bytes 196616 | tf_op jit(solution)/shard_map/ppermute | solution.py:550
  11.0 0.0 copy-start.1
  11.0 0.8 %copy-done.1 = f32[128,128]{1,0:T(8,128)S(1)} copy-done((f32[128,128]{1,0:T(8,128)S(1)}, f32[128,128]{1,0:T(8,128)}, u32[]{:S(2)}) %copy-start.1) | copy-done | bytes 65560
  11.8 0.0 copy-start.2
  11.8 0.0 copy-start
  11.8 1.4 %dense_tapers.2 = (bf16[16,128,256]{2,1,0:T(8,128)(2,1)S(1)}, bf16[16,128,256]{2,1,0:T(8,128)(2,1)S(1)}) custom-call(s32[1]{0:T(128)} %bitcast.gz_ref, f32[128,128]{1,0:T(8,128)S(1)} %copy-done.1), custom_call_target="tpu_custom_call" | custom-call | flops 3000000000 | bytes 9000000 | tf_op jit(solution)/shard_map/dense_tapers/pallas_call | solution.py:222
  13.2 0.0 collective-permute-done.2
  13.2 0.0 collective-permute-done.1
  13.2 0.3 collective-permute-done
  13.5 0.0 copy-done.2
  13.5 1.6 %collective-permute-start.4 = (f32[4,72,128]{2,1,0:T(8,128)S(1)}, f32[4,72,128]{2,1,0:T(8,128)S(1)}, u32[]{:S(2)}, u32[]{:S(2)}) collective-permute-start(f32[4,72,128]{2,1,0:T(8,128)S(1)} %pad_maximum_fusion.1.refs_0_), channel_id=1, source_target_pairs={{2,0},{0,2},{3,1},{1,3},{6,4},{4,6},{7,5},{5,7},{10,8},{8,10},{11,... | collective-permute-start | bytes 442376 | tf_op jit(solution)/shard_map/ppermute | solution.py:543
  15.1 0.0 copy-done
  15.1 0.2 center.1
  15.3 1.2 %collective-permute-done.3.list_ref = f32[128,128]{1,0:T(8,128)S(1)} collective-permute-done((f32[128,128]{1,0:T(8,128)}, f32[128,128]{1,0:T(8,128)S(1)}, u32[]{:S(2)}, u32[]{:S(2)}) %collective-permute-start.3) | collective-permute-done | bytes 65568 | tf_op jit(solution)/shard_map/ppermute | solution.py:550
  16.6 1.4 %dense_tapers.3 = (bf16[16,128,256]{2,1,0:T(8,128)(2,1)S(1)}, bf16[16,128,256]{2,1,0:T(8,128)(2,1)S(1)}) custom-call(s32[1]{0:T(128)} %bitcast.gz_ref, f32[128,128]{1,0:T(8,128)S(1)} %collective-permute-done.3.list_ref), custom_call_target="tpu_custom_call" | custom-call | flops 3000000000 | bytes 9000000 | tf_op jit(solution)/shard_map/dense_tapers/pallas_call | solution.py:222
  18.0 1.3 %grams.3.refs_0_ = f32[672,256]{1,0:T(8,128)S(1)} custom-call(f32[4,72,128]{2,1,0:T(8,128)S(1)} %pad_maximum_fusion.1.refs_0_, bf16[16,128,256]{2,1,0:T(8,128)(2,1)S(1)} %get-tuple-element.20.refs_1_.refs_2_, bf16[16,128,256]{2,1,0:T(8,128)(2,1)S(1)} %get-tuple-element.21.refs_2_.refs_3_, bf16[16,128,256]{2,1,0:T(8,128)(2,1)S(1)} %get-tuple-element.27.refs_3_.refs_4_, ...), custom_call_target="tpu_custom_call" | custom-call | flops 2000000000 | bytes 6000000 | tf_op jit(solution)/shard_map/grams/pallas_call | solution.py:285
  19.3 0.0 collective-permute-done.4.refs_1_
  19.4 0.1 collective-permute-start.5
  19.4 1.3 %grams.4.refs_0_ = f32[672,256]{1,0:T(8,128)S(1)} custom-call(f32[672,256]{1,0:T(8,128)S(1)} %grams.3.refs_0_, f32[4,72,128]{2,1,0:T(8,128)S(1)} %collective-permute-done.4.refs_1_, bf16[16,128,256]{2,1,0:T(8,128)(2,1)S(1)} %get-tuple-element.20.refs_1_.refs_2_, bf16[16,128,256]{2,1,0:T(8,128)(2,1)S(1)} %get-tuple-element.21.refs_2_.refs_3_, ...), custom_call_target="tpu_custom_call" | custom-call | flops 2000000000 | bytes 6000000 | tf_op jit(solution)/shard_map/grams/pallas_call | solution.py:285
  20.8 0.2 collective-permute-done.5.refs_1_
  21.0 2.5 %grams.5.gram_ref = f32[672,256]{1,0:T(8,128)S(1)} custom-call(f32[672,256]{1,0:T(8,128)S(1)} %grams.4.refs_0_, f32[8,72,128]{2,1,0:T(8,128)S(1)} %collective-permute-done.5.refs_1_, bf16[16,128,256]{2,1,0:T(8,128)(2,1)S(1)} %get-tuple-element.20.refs_1_.refs_2_, bf16[16,128,256]{2,1,0:T(8,128)(2,1)S(1)} %get-tuple-element.21.refs_2_.refs_3_, ...), custom_call_target="tpu_custom_call" | custom-call | flops 2000000000 | bytes 6000000 | tf_op jit(solution)/shard_map/grams/pallas_call | solution.py:285
  23.5 5.3 %roots.2.own_ref = f32[1024,128]{1,0:T(8,128)S(1)} custom-call(f32[672,256]{1,0:T(8,128)S(1)} %grams.5.gram_ref), custom_call_target="tpu_custom_call" | custom-call | flops 7000000000 | bytes 21000000 | tf_op jit(solution)/shard_map/roots/pallas_call | solution.py:409
  28.8 0.4 collective-permute-start.6
  29.2 5.1 %roots.3.halo_ref = f32[1024,128]{1,0:T(8,128)S(1)} custom-call(f32[672,256]{1,0:T(8,128)S(1)} %grams.5.gram_ref), custom_call_target="tpu_custom_call" | custom-call | flops 7000000000 | bytes 21000000 | tf_op jit(solution)/shard_map/roots/pallas_call | solution.py:409
  34.3 0.3 collective-permute-start.7
  34.6 0.0 collective-permute-done.6.pair_ref
  34.6 2.5 %inner.1.part_ref = f32[2304,128]{1,0:T(8,128)S(1)} custom-call(s32[1]{0:T(128)} %bitcast.gz_ref, f32[2048,128]{1,0:T(8,128)S(1)} %get-tuple-element.24.pert_ref, f32[64,128]{1,0:T(8,128)S(1)} %get-tuple-element.25.mean_ref, f32[1024,128]{1,0:T(8,128)S(1)} %roots.2.own_ref, f32[1024,128]{1,0:T(8,128)S(1)} %collective-permute-done.6.pair_ref, ...), custom_call_target="tpu_custom_call" | custom-call | flops 3000000000 | bytes 9000000 | tf_op jit(solution)/shard_map/inner/pallas_call | solution.py:516
  37.1 0.0 collective-permute-done.7.far_ref
  37.1 1.7 %outer.1 = bf16[32,8,8,128]{3,2,1,0:T(8,128)(2,1)} custom-call(s32[1]{0:T(128)} %bitcast.gz_ref, f32[2048,128]{1,0:T(8,128)S(1)} %get-tuple-element.24.pert_ref, f32[64,128]{1,0:T(8,128)S(1)} %get-tuple-element.25.mean_ref, f32[1024,128]{1,0:T(8,128)S(1)} %collective-permute-done.6.pair_ref, f32[1024,128]{1,0:T(8,128)S(1)} %collective-permute-done.7.far_ref, ...), custom_call_target="tpu_custom_call" | custom-call | flops 1000000000 | bytes 3000000 | tf_op jit(solution)/shard_map/outer/pallas_call | solution.py:525
  (2 shorter events, 0.0 us)
Async XLA Ops:
  3.3 10.0 %collective-permute-start.2 = (f32[72,128]{1,0:T(8,128)}, f32[72,128]{1,0:T(8,128)S(1)}, u32[]{:S(2)}, u32[]{:S(2)}) collective-permute-start(f32[72,128]{1,0:T(8,128)} %get-tuple-element.18), channel_id=1, source_target_pairs={{12,0},{0,4},{4,8},{8,12},{5,1},{9,5},{13,9},{1,13},{14,2},{2,6},{... | collective-permute-start | bytes 110600 | tf_op jit(solution)/shard_map/ppermute | solution.py:550
  6.3 6.9 %collective-permute-start.1 = (f32[72,128]{1,0:T(8,128)}, f32[72,128]{1,0:T(8,128)S(1)}, u32[]{:S(2)}, u32[]{:S(2)}) collective-permute-start(f32[72,128]{1,0:T(8,128)} %get-tuple-element.18), channel_id=1, source_target_pairs={{8,0},{12,4},{0,8},{4,12},{9,1},{13,5},{1,9},{5,13},{10,2},{14,6},... | collective-permute-start | bytes 110600 | tf_op jit(solution)/shard_map/ppermute | solution.py:550
  8.9 4.6 %collective-permute-start = (f32[72,128]{1,0:T(8,128)}, f32[72,128]{1,0:T(8,128)S(1)}, u32[]{:S(2)}, u32[]{:S(2)}) collective-permute-start(f32[72,128]{1,0:T(8,128)} %get-tuple-element.18), channel_id=1, source_target_pairs={{4,0},{8,4},{12,8},{0,12},{13,1},{1,5},{5,9},{9,13},{6,2},{10,6},{... | collective-permute-start | bytes 110600 | tf_op jit(solution)/shard_map/ppermute | solution.py:550
  10.3 6.3 %collective-permute-start.3 = (f32[128,128]{1,0:T(8,128)}, f32[128,128]{1,0:T(8,128)S(1)}, u32[]{:S(2)}, u32[]{:S(2)}) collective-permute-start(f32[128,128]{1,0:T(8,128)} %get-tuple-element.26), channel_id=1, source_target_pairs={{12,0},{0,4},{4,8},{8,12},{5,1},{9,5},{13,9},{1,13},{14,2},{2,6},{... | collective-permute-start | bytes 196616 | tf_op jit(solution)/shard_map/ppermute | solution.py:550
  11.0 0.8 %copy-start.1 = (f32[128,128]{1,0:T(8,128)S(1)}, f32[128,128]{1,0:T(8,128)}, u32[]{:S(2)}) copy-start(f32[128,128]{1,0:T(8,128)} %get-tuple-element.19.list_ref) | copy-start | bytes 196612
  11.8 1.7 %copy-start.2 = (f32[72,128]{1,0:T(8,128)S(1)}, f32[72,128]{1,0:T(8,128)}, u32[]{:S(2)}) copy-start(f32[72,128]{1,0:T(8,128)} %get-tuple-element.18) | copy-start | bytes 110596
  11.8 3.3 %copy-start = (bf16[32,8,8,128]{3,2,1,0:T(8,128)(2,1)S(1)}, bf16[32,8,8,128]{3,2,1,0:T(8,128)(2,1)}, u32[]{:S(2)}) copy-start(bf16[32,8,8,128]{3,2,1,0:T(8,128)(2,1)} %members_ref) | copy-start | bytes 1572868
  13.5 5.8 %collective-permute-start.4 = (f32[4,72,128]{2,1,0:T(8,128)S(1)}, f32[4,72,128]{2,1,0:T(8,128)S(1)}, u32[]{:S(2)}, u32[]{:S(2)}) collective-permute-start(f32[4,72,128]{2,1,0:T(8,128)S(1)} %pad_maximum_fusion.1.refs_0_), channel_id=1, source_target_pairs={{2,0},{0,2},{3,1},{1,3},{6,4},{4,6},{7,5},{5,7},{10,8},{8,10},{11,... | collective-permute-start | bytes 442376 | tf_op jit(solution)/shard_map/ppermute | solution.py:543
  19.4 1.6 %collective-permute-start.5 = (f32[8,72,128]{2,1,0:T(8,128)S(1)}, f32[8,72,128]{2,1,0:T(8,128)S(1)}, u32[]{:S(2)}, u32[]{:S(2)}) collective-permute-start(f32[8,72,128]{2,1,0:T(8,128)S(1)} %pad_maximum_fusion), channel_id=1, source_target_pairs={{0,1},{1,0},{2,3},{3,2},{4,5},{5,4},{6,7},{7,6},{8,9},{9,8},{10,11... | collective-permute-start | bytes 884744 | tf_op jit(solution)/shard_map/ppermute | solution.py:554
  28.8 5.8 %collective-permute-start.6 = (f32[1024,128]{1,0:T(8,128)S(1)}, f32[1024,128]{1,0:T(8,128)S(1)}, u32[]{:S(2)}, u32[]{:S(2)}) collective-permute-start(f32[1024,128]{1,0:T(8,128)S(1)} %roots.2.own_ref), channel_id=1, source_target_pairs={{0,1},{1,0},{2,3},{3,2},{4,5},{5,4},{6,7},{7,6},{8,9},{9,8},{10,11... | collective-permute-start | bytes 1572872 | tf_op jit(solution)/shard_map/ppermute | solution.py:554
  34.3 2.8 %collective-permute-start.7 = (f32[1024,128]{1,0:T(8,128)S(1)}, f32[1024,128]{1,0:T(8,128)S(1)}, u32[]{:S(2)}, u32[]{:S(2)}) collective-permute-start(f32[1024,128]{1,0:T(8,128)S(1)} %roots.3.halo_ref), channel_id=1, source_target_pairs={{0,1},{1,0},{2,3},{3,2},{4,5},{5,4},{6,7},{7,6},{8,9},{9,8},{10,11... | collective-permute-start | bytes 1572872 | tf_op jit(solution)/shard_map/ppermute | solution.py:554

commit v7 on v6

--- a/solution.py
+++ b/solution.py
@@ -10,7 +10,7 @@
 
 PX = 4
 PIT = 40
-BATCH = 8
+BATCH = 16
 F32 = jnp.float32
 BF16 = jnp.bfloat16
 LANES = 128

time: 39.1 us -> 39.1 us (level)
  no operation moved by 1% of the time
where the time goes in v7:
time: 39.1 us; the launch traced here: 38.9 us
  Pallas kernels  25.4 us (65%)
  starting transfers between devices  9.96 us (25%)
  waiting for transfers between devices  1.75 us (4%)
  between operations  0.94 us (2%)
  local copies, waits for them, and re-layouts  0.85 us (2%)
    pallas_call x2, Pallas kernels, roots(): pl.pallas_call(functools.partial(root_kernel, ens=ens, row=row), out_shap...  10.4 us
    ppermute x4, starting transfers between devices, turned(): return lax.ppermute(x, ('gx', 'gz'), pairs)  7.69 us
    pallas_call x3, Pallas kernels, grams(): pl.pallas_call(functools.partial(gram_kernel, ens=ens, bufs=tuple(bufs),...  5.18 us
    pallas_call x2, Pallas kernels, dense_tapers(): pl.pallas_call(functools.partial(taper_kernel, shift=shift, n_x=n_x, n_y=...  2.84 us
    pallas_call x1, Pallas kernels, observe(): pl.pallas_call(observe_kernel, out_shape=(jax.ShapeDtypeStruct((slots //...  2.6 us
    pallas_call x1, Pallas kernels, update(): pl.pallas_call(functools.partial(inner_kernel, ens=ens, levels=levels, wi...  2.46 us
    pallas_call x1, Pallas kernels, update(): pl.pallas_call(outer_kernel, out_shape=jax.ShapeDtypeStruct(shape, BF16),...  1.67 us
    ppermute x1, starting transfers between devices, shifted(): return lax.ppermute(x, axis, [((i + shift) % size, i) for i in range(size)])  1.56 us
  transfers between devices with their start and end apart: 8, of which 3 were waited for; matrix products, arithmetic and copies ran while one was open for 0% of the time, Pallas kernels for 34%

profile of v7, /device:TPU:0, one launch (start us, length us, event | category | flops | bytes accessed | tf_op | source)
XLA Modules:
  0.0 38.9 jit_solution(6238316162992101528)
XLA Ops:
  0.7 2.6 %observe.1 = (f32[72,128]{1,0:T(8,128)}, f32[128,128]{1,0:T(8,128)}, f32[128,128]{1,0:T(8,128)}) custom-call(s32[1]{0:T(128)} %bitcast.gz_ref, s32[1]{0:T(128)} %bitcast.12.count_ref, bf16[32,8,8,128]{3,2,1,0:T(8,128)(2,1)} %members_ref, s32[8,256]{1,0:T(8,128)} %bitcast.19, f32[8,256]{1,0:T(8,128)} %bitcast.20, f32[1,256]{1,0:T(1,128)} %bitcast.21, ...), custom_call_target="tpu_custom_call" | custom-call | flops 3000000000 | bytes 9000000 | tf_op jit(solution)/shard_map/observe/pallas_call | solution.py:136
  3.3 3.1 %collective-permute-start.2 = (f32[72,128]{1,0:T(8,128)}, f32[72,128]{1,0:T(8,128)S(1)}, u32[]{:S(2)}, u32[]{:S(2)}) collective-permute-start(f32[72,128]{1,0:T(8,128)} %get-tuple-element.18), channel_id=1, source_target_pairs={{12,0},{0,4},{4,8},{8,12},{5,1},{9,5},{13,9},{1,13},{14,2},{2,6},{... | collective-permute-start | bytes 110600 | tf_op jit(solution)/shard_map/ppermute | solution.py:550
  6.3 2.6 %collective-permute-start.1 = (f32[72,128]{1,0:T(8,128)}, f32[72,128]{1,0:T(8,128)S(1)}, u32[]{:S(2)}, u32[]{:S(2)}) collective-permute-start(f32[72,128]{1,0:T(8,128)} %get-tuple-element.18), channel_id=1, source_target_pairs={{8,0},{12,4},{0,8},{4,12},{9,1},{13,5},{1,9},{5,13},{10,2},{14,6},... | collective-permute-start | bytes 110600 | tf_op jit(solution)/shard_map/ppermute | solution.py:550
  8.9 1.3 %collective-permute-start = (f32[72,128]{1,0:T(8,128)}, f32[72,128]{1,0:T(8,128)S(1)}, u32[]{:S(2)}, u32[]{:S(2)}) collective-permute-start(f32[72,128]{1,0:T(8,128)} %get-tuple-element.18), channel_id=1, source_target_pairs={{4,0},{8,4},{12,8},{0,12},{13,1},{1,5},{5,9},{9,13},{6,2},{10,6},{... | collective-permute-start | bytes 110600 | tf_op jit(solution)/shard_map/ppermute | solution.py:550
  10.3 0.7 %collective-permute-start.3 = (f32[128,128]{1,0:T(8,128)}, f32[128,128]{1,0:T(8,128)S(1)}, u32[]{:S(2)}, u32[]{:S(2)}) collective-permute-start(f32[128,128]{1,0:T(8,128)} %get-tuple-element.26), channel_id=1, source_target_pairs={{12,0},{0,4},{4,8},{8,12},{5,1},{9,5},{13,9},{1,13},{14,2},{2,6},{... | collective-permute-start | bytes 196616 | tf_op jit(solution)/shard_map/ppermute | solution.py:550
  11.0 0.0 copy-start.1
  11.0 0.8 %copy-done.1 = f32[128,128]{1,0:T(8,128)S(1)} copy-done((f32[128,128]{1,0:T(8,128)S(1)}, f32[128,128]{1,0:T(8,128)}, u32[]{:S(2)}) %copy-start.1) | copy-done | bytes 65560
  11.8 0.0 copy-start.2
  11.8 0.0 copy-start
  11.8 1.4 %dense_tapers.2 = (bf16[16,128,256]{2,1,0:T(8,128)(2,1)S(1)}, bf16[16,128,256]{2,1,0:T(8,128)(2,1)S(1)}) custom-call(s32[1]{0:T(128)} %bitcast.gz_ref, f32[128,128]{1,0:T(8,128)S(1)} %copy-done.1), custom_call_target="tpu_custom_call" | custom-call | flops 3000000000 | bytes 9000000 | tf_op jit(solution)/shard_map/dense_tapers/pallas_call | solution.py:222
  13.2 0.0 collective-permute-done.2
  13.2 0.0 collective-permute-done.1
  13.2 0.3 collective-permute-done
  13.5 0.0 copy-done.2
  13.5 1.6 %collective-permute-start.4 = (f32[4,72,128]{2,1,0:T(8,128)S(1)}, f32[4,72,128]{2,1,0:T(8,128)S(1)}, u32[]{:S(2)}, u32[]{:S(2)}) collective-permute-start(f32[4,72,128]{2,1,0:T(8,128)S(1)} %pad_maximum_fusion.1.refs_0_), channel_id=1, source_target_pairs={{2,0},{0,2},{3,1},{1,3},{6,4},{4,6},{7,5},{5,7},{10,8},{8,10},{11,... | collective-permute-start | bytes 442376 | tf_op jit(solution)/shard_map/ppermute | solution.py:543
  15.1 0.0 copy-done
  15.1 0.2 center.1
  15.3 1.2 %collective-permute-done.3.list_ref = f32[128,128]{1,0:T(8,128)S(1)} collective-permute-done((f32[128,128]{1,0:T(8,128)}, f32[128,128]{1,0:T(8,128)S(1)}, u32[]{:S(2)}, u32[]{:S(2)}) %collective-permute-start.3) | collective-permute-done | bytes 65568 | tf_op jit(solution)/shard_map/ppermute | solution.py:550
  16.5 1.4 %dense_tapers.3 = (bf16[16,128,256]{2,1,0:T(8,128)(2,1)S(1)}, bf16[16,128,256]{2,1,0:T(8,128)(2,1)S(1)}) custom-call(s32[1]{0:T(128)} %bitcast.gz_ref, f32[128,128]{1,0:T(8,128)S(1)} %collective-permute-done.3.list_ref), custom_call_target="tpu_custom_call" | custom-call | flops 3000000000 | bytes 9000000 | tf_op jit(solution)/shard_map/dense_tapers/pallas_call | solution.py:222
  18.0 1.3 %grams.3.refs_0_ = f32[672,256]{1,0:T(8,128)S(1)} custom-call(f32[4,72,128]{2,1,0:T(8,128)S(1)} %pad_maximum_fusion.1.refs_0_, bf16[16,128,256]{2,1,0:T(8,128)(2,1)S(1)} %get-tuple-element.20.refs_1_.refs_2_, bf16[16,128,256]{2,1,0:T(8,128)(2,1)S(1)} %get-tuple-element.21.refs_2_.refs_3_, bf16[16,128,256]{2,1,0:T(8,128)(2,1)S(1)} %get-tuple-element.27.refs_3_.refs_4_, ...), custom_call_target="tpu_custom_call" | custom-call | flops 2000000000 | bytes 6000000 | tf_op jit(solution)/shard_map/grams/pallas_call | solution.py:285
  19.3 0.0 collective-permute-done.4.refs_1_
  19.4 0.1 collective-permute-start.5
  19.4 1.3 %grams.4.refs_0_ = f32[672,256]{1,0:T(8,128)S(1)} custom-call(f32[672,256]{1,0:T(8,128)S(1)} %grams.3.refs_0_, f32[4,72,128]{2,1,0:T(8,128)S(1)} %collective-permute-done.4.refs_1_, bf16[16,128,256]{2,1,0:T(8,128)(2,1)S(1)} %get-tuple-element.20.refs_1_.refs_2_, bf16[16,128,256]{2,1,0:T(8,128)(2,1)S(1)} %get-tuple-element.21.refs_2_.refs_3_, ...), custom_call_target="tpu_custom_call" | custom-call | flops 2000000000 | bytes 6000000 | tf_op jit(solution)/shard_map/grams/pallas_call | solution.py:285
  20.8 0.2 collective-permute-done.5.refs_1_
  21.0 2.5 %grams.5.gram_ref = f32[672,256]{1,0:T(8,128)S(1)} custom-call(f32[672,256]{1,0:T(8,128)S(1)} %grams.4.refs_0_, f32[8,72,128]{2,1,0:T(8,128)S(1)} %collective-permute-done.5.refs_1_, bf16[16,128,256]{2,1,0:T(8,128)(2,1)S(1)} %get-tuple-element.20.refs_1_.refs_2_, bf16[16,128,256]{2,1,0:T(8,128)(2,1)S(1)} %get-tuple-element.21.refs_2_.refs_3_, ...), custom_call_target="tpu_custom_call" | custom-call | flops 2000000000 | bytes 6000000 | tf_op jit(solution)/shard_map/grams/pallas_call | solution.py:285
  23.5 5.3 %roots.2.own_ref = f32[1024,128]{1,0:T(8,128)S(1)} custom-call(f32[672,256]{1,0:T(8,128)S(1)} %grams.5.gram_ref), custom_call_target="tpu_custom_call" | custom-call | flops 7000000000 | bytes 21000000 | tf_op jit(solution)/shard_map/roots/pallas_call | solution.py:409
  28.8 0.4 collective-permute-start.6
  29.2 5.1 %roots.3.halo_ref = f32[1024,128]{1,0:T(8,128)S(1)} custom-call(f32[672,256]{1,0:T(8,128)S(1)} %grams.5.gram_ref), custom_call_target="tpu_custom_call" | custom-call | flops 7000000000 | bytes 21000000 | tf_op jit(solution)/shard_map/roots/pallas_call | solution.py:409
  34.3 0.3 collective-permute-start.7
  34.6 0.0 collective-permute-done.6.pair_ref
  34.6 2.5 %inner.1.part_ref = f32[2304,128]{1,0:T(8,128)S(1)} custom-call(s32[1]{0:T(128)} %bitcast.gz_ref, f32[2048,128]{1,0:T(8,128)S(1)} %get-tuple-element.24.pert_ref, f32[64,128]{1,0:T(8,128)S(1)} %get-tuple-element.25.mean_ref, f32[1024,128]{1,0:T(8,128)S(1)} %roots.2.own_ref, f32[1024,128]{1,0:T(8,128)S(1)} %collective-permute-done.6.pair_ref, ...), custom_call_target="tpu_custom_call" | custom-call | flops 3000000000 | bytes 9000000 | tf_op jit(solution)/shard_map/inner/pallas_call | solution.py:516
  37.1 0.0 collective-permute-done.7.far_ref
  37.1 1.7 %outer.1 = bf16[32,8,8,128]{3,2,1,0:T(8,128)(2,1)} custom-call(s32[1]{0:T(128)} %bitcast.gz_ref, f32[2048,128]{1,0:T(8,128)S(1)} %get-tuple-element.24.pert_ref, f32[64,128]{1,0:T(8,128)S(1)} %get-tuple-element.25.mean_ref, f32[1024,128]{1,0:T(8,128)S(1)} %collective-permute-done.6.pair_ref, f32[1024,128]{1,0:T(8,128)S(1)} %collective-permute-done.7.far_ref, ...), custom_call_target="tpu_custom_call" | custom-call | flops 1000000000 | bytes 3000000 | tf_op jit(solution)/shard_map/outer/pallas_call | solution.py:525
  (2 shorter events, 0.0 us)
Async XLA Ops:
  3.3 10.0 %collective-permute-start.2 = (f32[72,128]{1,0:T(8,128)}, f32[72,128]{1,0:T(8,128)S(1)}, u32[]{:S(2)}, u32[]{:S(2)}) collective-permute-start(f32[72,128]{1,0:T(8,128)} %get-tuple-element.18), channel_id=1, source_target_pairs={{12,0},{0,4},{4,8},{8,12},{5,1},{9,5},{13,9},{1,13},{14,2},{2,6},{... | collective-permute-start | bytes 110600 | tf_op jit(solution)/shard_map/ppermute | solution.py:550
  6.3 6.9 %collective-permute-start.1 = (f32[72,128]{1,0:T(8,128)}, f32[72,128]{1,0:T(8,128)S(1)}, u32[]{:S(2)}, u32[]{:S(2)}) collective-permute-start(f32[72,128]{1,0:T(8,128)} %get-tuple-element.18), channel_id=1, source_target_pairs={{8,0},{12,4},{0,8},{4,12},{9,1},{13,5},{1,9},{5,13},{10,2},{14,6},... | collective-permute-start | bytes 110600 | tf_op jit(solution)/shard_map/ppermute | solution.py:550
  8.9 4.6 %collective-permute-start = (f32[72,128]{1,0:T(8,128)}, f32[72,128]{1,0:T(8,128)S(1)}, u32[]{:S(2)}, u32[]{:S(2)}) collective-permute-start(f32[72,128]{1,0:T(8,128)} %get-tuple-element.18), channel_id=1, source_target_pairs={{4,0},{8,4},{12,8},{0,12},{13,1},{1,5},{5,9},{9,13},{6,2},{10,6},{... | collective-permute-start | bytes 110600 | tf_op jit(solution)/shard_map/ppermute | solution.py:550
  10.3 6.3 %collective-permute-start.3 = (f32[128,128]{1,0:T(8,128)}, f32[128,128]{1,0:T(8,128)S(1)}, u32[]{:S(2)}, u32[]{:S(2)}) collective-permute-start(f32[128,128]{1,0:T(8,128)} %get-tuple-element.26), channel_id=1, source_target_pairs={{12,0},{0,4},{4,8},{8,12},{5,1},{9,5},{13,9},{1,13},{14,2},{2,6},{... | collective-permute-start | bytes 196616 | tf_op jit(solution)/shard_map/ppermute | solution.py:550
  11.0 0.8 %copy-start.1 = (f32[128,128]{1,0:T(8,128)S(1)}, f32[128,128]{1,0:T(8,128)}, u32[]{:S(2)}) copy-start(f32[128,128]{1,0:T(8,128)} %get-tuple-element.19.list_ref) | copy-start | bytes 196612
  11.8 1.7 %copy-start.2 = (f32[72,128]{1,0:T(8,128)S(1)}, f32[72,128]{1,0:T(8,128)}, u32[]{:S(2)}) copy-start(f32[72,128]{1,0:T(8,128)} %get-tuple-element.18) | copy-start | bytes 110596
  11.8 3.3 %copy-start = (bf16[32,8,8,128]{3,2,1,0:T(8,128)(2,1)S(1)}, bf16[32,8,8,128]{3,2,1,0:T(8,128)(2,1)}, u32[]{:S(2)}) copy-start(bf16[32,8,8,128]{3,2,1,0:T(8,128)(2,1)} %members_ref) | copy-start | bytes 1572868
  13.5 5.8 %collective-permute-start.4 = (f32[4,72,128]{2,1,0:T(8,128)S(1)}, f32[4,72,128]{2,1,0:T(8,128)S(1)}, u32[]{:S(2)}, u32[]{:S(2)}) collective-permute-start(f32[4,72,128]{2,1,0:T(8,128)S(1)} %pad_maximum_fusion.1.refs_0_), channel_id=1, source_target_pairs={{2,0},{0,2},{3,1},{1,3},{6,4},{4,6},{7,5},{5,7},{10,8},{8,10},{11,... | collective-permute-start | bytes 442376 | tf_op jit(solution)/shard_map/ppermute | solution.py:543
  19.4 1.6 %collective-permute-start.5 = (f32[8,72,128]{2,1,0:T(8,128)S(1)}, f32[8,72,128]{2,1,0:T(8,128)S(1)}, u32[]{:S(2)}, u32[]{:S(2)}) collective-permute-start(f32[8,72,128]{2,1,0:T(8,128)S(1)} %pad_maximum_fusion), channel_id=1, source_target_pairs={{0,1},{1,0},{2,3},{3,2},{4,5},{5,4},{6,7},{7,6},{8,9},{9,8},{10,11... | collective-permute-start | bytes 884744 | tf_op jit(solution)/shard_map/ppermute | solution.py:554
  28.8 5.8 %collective-permute-start.6 = (f32[1024,128]{1,0:T(8,128)S(1)}, f32[1024,128]{1,0:T(8,128)S(1)}, u32[]{:S(2)}, u32[]{:S(2)}) collective-permute-start(f32[1024,128]{1,0:T(8,128)S(1)} %roots.2.own_ref), channel_id=1, source_target_pairs={{0,1},{1,0},{2,3},{3,2},{4,5},{5,4},{6,7},{7,6},{8,9},{9,8},{10,11... | collective-permute-start | bytes 1572872 | tf_op jit(solution)/shard_map/ppermute | solution.py:554
  34.3 2.8 %collective-permute-start.7 = (f32[1024,128]{1,0:T(8,128)S(1)}, f32[1024,128]{1,0:T(8,128)S(1)}, u32[]{:S(2)}, u32[]{:S(2)}) collective-permute-start(f32[1024,128]{1,0:T(8,128)S(1)} %roots.3.halo_ref), channel_id=1, source_target_pairs={{0,1},{1,0},{2,3},{3,2},{4,5},{5,4},{6,7},{7,6},{8,9},{9,8},{10,11... | collective-permute-start | bytes 1572872 | tf_op jit(solution)/shard_map/ppermute | solution.py:554
